TPU v7x, 32 devices: a whole 2x2x4 slice. The times are simulated.
32 devices in a mesh: groups: 2 (over y), ctx: 4 (over z), mp: 2 (over x), sec: 2 (over core).
Axes of the slice: x: 2, y: 2, z: 4, core: 2. Of those that a mesh axis runs over, the one named last changes fastest.
Arguments:
- queries: bfloat16 [1024, 2048], P(('groups', 'ctx'), ('mp', 'sec')), parts along dimension 0, may hold values from -6 to 6
- keys: bfloat16 [1024, 2048], P(('groups', 'ctx'), ('mp', 'sec')), parts along dimension 0, may hold values from -6 to 6
- values: bfloat16 [1024, 2048], P(('groups', 'ctx'), ('mp', 'sec')), parts along dimension 0, may hold values from -6 to 6
- text_keys: bfloat16 [2048, 2048], P('groups', ('mp', 'sec')), parts along dimension 0, may hold values from -6 to 6
- text_values: bfloat16 [2048, 2048], P('groups', ('mp', 'sec')), parts along dimension 0, may hold values from -6 to 6
- segment: int32 [1024], P(('groups', 'ctx')), parts along dimension 0, may hold values from 0 to 3, never falling along the last dimension, each value on 1 to 384 neighbouring positions
- text_len: int32 [8], P('groups'), parts along dimension 0, may hold values from 1 to 256, as said below
- grad_out: bfloat16 [1024, 2048], P(('groups', 'ctx'), ('mp', 'sec')), parts along dimension 0, may hold values from -6 to 6
Outputs:
- output: bfloat16 [1024, 2048], P(('groups', 'ctx'), ('mp', 'sec')), parts along dimension 0
- grad_q: bfloat16 [1024, 2048], P(('groups', 'ctx'), ('mp', 'sec')), parts along dimension 0
- grad_k: bfloat16 [1024, 2048], P(('groups', 'ctx'), ('mp', 'sec')), parts along dimension 0
- grad_v: bfloat16 [1024, 2048], P(('groups', 'ctx'), ('mp', 'sec')), parts along dimension 0
- grad_text_k: float32 [2048, 2048], P('groups', ('mp', 'sec')), parts along dimension 0
- grad_text_v: float32 [2048, 2048], P('groups', ('mp', 'sec')), parts along dimension 0
There are 2 independent parts, one for each index of `groups`. A program takes and returns all parts, laid end to end along the dimension named above; each array names one. Nothing has to cross between parts.
Inputs may be any that keep to these rules, and one draw needn't show every extreme that they name: `segment`: clip numbers never fall along the sequence; each clip holds 1 to 384 latent tokens and one holds exactly 384. `text_len`: one clip in every draw has all 256 text tokens live, the others fewer.
All inputs are finite; a program needn't handle non-finite values.
Results may differ from a plain program's by a relative error of at most 0.0071.
Values may be sent and summed in bfloat16 or wider, within the bound.
No kernel may reach another device: no remote copies, remote signals or barrier semaphores. Data moves between devices by JAX's collectives and lax.ppermute only.
A program may use at most 128 MiB of HBM per device.

v0:
```python
import math

import jax
import jax.numpy as jnp
from jax import lax
from jax.sharding import PartitionSpec as P

HD = 128


epsilon = 1e-06


def normalize(matrix, head_dim):
    length = matrix.shape[0]
    per_head = matrix.reshape(length, -1, head_dim).astype(jnp.float32)
    inverse = lax.rsqrt(jnp.mean(per_head * per_head, axis=-1, keepdims=True) + epsilon)
    return (per_head * inverse).astype(jnp.bfloat16)


def norm_back(matrix, upstream, head_dim):
    length = matrix.shape[0]
    per_head = matrix.reshape(length, -1, head_dim).astype(jnp.float32)
    inverse = lax.rsqrt(jnp.mean(per_head * per_head, axis=-1, keepdims=True) + epsilon)
    inner = jnp.sum(upstream * per_head, axis=-1, keepdims=True) / head_dim
    return (upstream * inverse - per_head * inner * inverse * inverse * inverse).reshape(length, -1)


def masked_exp(query_n, key_n, allowed, score_scale):
    logits = (
        jnp.einsum("qhd,khd->hqk", query_n, key_n, preferred_element_type=jnp.float32) * score_scale
    )
    return jnp.where(allowed[None], jnp.exp(logits), 0.0)


def backward_terms(query_n, grad_rows, norm_sum, inner, key_n, key_vals, allowed, score_scale):
    expon = masked_exp(query_n, key_n, allowed, score_scale)
    probs = expon / norm_sum[:, :, None]
    weights = probs.astype(jnp.bfloat16)
    dprob = jnp.einsum("qhd,khd->hqk", grad_rows, key_vals, preferred_element_type=jnp.float32)
    dscore = (probs * (dprob - inner[:, :, None])).astype(jnp.bfloat16)
    return (weights, dscore)


def shards(queries, keys, values, text_keys, text_values, segment, text_len, grad_out):
    head_dim = HD
    score_scale = 1.0 / math.sqrt(head_dim)
    length = queries.shape[0]
    query_n = normalize(queries, head_dim)
    key_n = normalize(keys, head_dim)
    text_n = normalize(text_keys, head_dim)
    value_h = values.reshape(length, -1, head_dim)
    text_vh = text_values.reshape(text_values.shape[0], -1, head_dim)
    grad_h = grad_out.reshape(length, -1, head_dim)
    clip_count = text_len.shape[0]
    text_rows = text_keys.shape[0]
    per_clip = text_rows // clip_count
    position = jnp.arange(text_rows, dtype=jnp.int32)
    text_clip = position // per_clip
    text_limit = jnp.sum(
        jnp.where(
            text_clip[:, None] == jnp.arange(clip_count, dtype=jnp.int32)[None, :],
            text_len[None, :],
            0,
        ),
        axis=1,
    )
    text_live = position % per_clip < text_limit
    text_mask = (segment[:, None] == text_clip[None, :]) & text_live[None, :]
    all_seg = lax.all_gather(segment, "ctx", axis=0, tiled=True)

    def guarded(update, totals, pieces, offset):
        return update(totals, pieces, all_seg, offset)

    text_exp = masked_exp(query_n, text_n, text_mask, score_scale)
    text_weight = text_exp.astype(jnp.bfloat16)
    start_state = (
        jnp.sum(text_weight.astype(jnp.float32), axis=-1),
        jnp.einsum("hqk,khd->hqd", text_weight, text_vh, preferred_element_type=jnp.float32),
    )

    def forward_add(totals, pieces, piece_seg, offset):
        key_piece, value_piece = pieces
        piece_len = key_piece.shape[0]
        expon = masked_exp(
            query_n,
            key_piece.reshape(piece_len, -1, head_dim),
            segment[:, None] == piece_seg[None, :],
            score_scale,
        )
        weight_bf = expon.astype(jnp.bfloat16)
        return (
            totals[0] + jnp.sum(weight_bf.astype(jnp.float32), axis=-1),
            totals[1]
            + jnp.einsum(
                "hqk,khd->hqd",
                weight_bf,
                value_piece.reshape(piece_len, -1, head_dim),
                preferred_element_type=jnp.float32,
            ),
        )

    key_flat = key_n.reshape(length, -1)
    norm_sum, accum = guarded(
        forward_add,
        start_state,
        (
            lax.all_gather(key_flat, "ctx", axis=0, tiled=True),
            lax.all_gather(values, "ctx", axis=0, tiled=True),
        ),
        jnp.int32(0),
    )
    attended = jnp.transpose((accum / norm_sum[:, :, None]).astype(jnp.bfloat16), (1, 0, 2))
    output = attended.reshape(length, -1)
    inner = jnp.transpose(
        jnp.sum(grad_h.astype(jnp.float32) * attended.astype(jnp.float32), axis=-1)
    )
    text_wt, text_ds = backward_terms(
        query_n, grad_h, norm_sum, inner, text_n, text_vh, text_mask, score_scale
    )
    query_start = (
        jnp.einsum("hqk,khd->hqd", text_ds, text_n, preferred_element_type=jnp.float32)
        * score_scale
    )

    def query_grad(totals, pieces, piece_seg, offset):
        key_piece, value_piece = pieces
        piece_len = key_piece.shape[0]
        key_part = key_piece.reshape(piece_len, -1, head_dim)
        terms = backward_terms(
            query_n,
            grad_h,
            norm_sum,
            inner,
            key_part,
            value_piece.reshape(piece_len, -1, head_dim),
            segment[:, None] == piece_seg[None, :],
            score_scale,
        )
        return (
            totals
            + jnp.einsum("hqk,khd->hqd", terms[1], key_part, preferred_element_type=jnp.float32)
            * score_scale
        )

    query_total = guarded(
        query_grad,
        query_start,
        (
            lax.all_gather(key_flat, "ctx", axis=0, tiled=True),
            lax.all_gather(values, "ctx", axis=0, tiled=True),
        ),
        jnp.int32(0),
    )
    all_sums, all_inner = (
        lax.all_gather(jnp.transpose(norm_sum), "ctx", axis=0, tiled=True),
        lax.all_gather(jnp.transpose(inner), "ctx", axis=0, tiled=True),
    )

    def key_grad(totals, pieces, piece_seg, offset):
        query_piece, grad_piece = pieces
        piece_len = query_piece.shape[0]
        query_part = query_piece.reshape(piece_len, -1, head_dim)
        grad_part = grad_piece.reshape(piece_len, -1, head_dim)
        piece_sum = jnp.transpose(all_sums)
        piece_inner = jnp.transpose(all_inner)
        weights, dscore = backward_terms(
            query_part,
            grad_part,
            piece_sum,
            piece_inner,
            key_n,
            value_h,
            piece_seg[:, None] == segment[None, :],
            score_scale,
        )
        return (
            jnp.einsum("hqk,qhd->khd", dscore, query_part, preferred_element_type=jnp.float32)
            * score_scale,
            jnp.einsum("hqk,qhd->khd", weights, grad_part, preferred_element_type=jnp.float32),
        )

    query_flat = query_n.reshape(length, -1)
    zeros_key = jnp.zeros(key_n.shape, jnp.float32)
    zeros_text = jnp.zeros(text_n.shape, jnp.float32)
    start_keys = (zeros_key, zeros_key, zeros_text, zeros_text)
    pieces = (
        lax.all_gather(query_flat, "ctx", axis=0, tiled=True),
        lax.all_gather(grad_out, "ctx", axis=0, tiled=True),
    )
    video_part = guarded(key_grad, (start_keys[0], start_keys[1]), pieces, jnp.int32(0))
    query_piece, grad_piece = pieces
    piece_len = query_piece.shape[0]
    piece_seg = all_seg
    query_part = query_piece.reshape(piece_len, -1, head_dim)
    grad_part = grad_piece.reshape(piece_len, -1, head_dim)
    piece_sum = jnp.transpose(all_sums)
    piece_inner = jnp.transpose(all_inner)
    piece_mask = (piece_seg[:, None] == text_clip[None, :]) & text_live[None, :]
    weights, dscore = backward_terms(
        query_part, grad_part, piece_sum, piece_inner, text_n, text_vh, piece_mask, score_scale
    )
    key_total = video_part[0]
    value_total = video_part[1]
    text_dk_sum = (
        jnp.einsum("hqk,qhd->khd", dscore, query_part, preferred_element_type=jnp.float32)
        * score_scale
    ).reshape(text_rows, -1)
    text_dv_sum = jnp.einsum(
        "hqk,qhd->khd", weights, grad_part, preferred_element_type=jnp.float32
    ).reshape(text_rows, -1)
    grad_text_k = norm_back(text_keys, text_dk_sum.reshape(text_rows, -1, head_dim), head_dim)
    grad_q = norm_back(queries, jnp.transpose(query_total, (1, 0, 2)), head_dim).astype(
        jnp.bfloat16
    )
    grad_k = norm_back(keys, key_total, head_dim).astype(jnp.bfloat16)
    grad_v = value_total.reshape(length, -1).astype(jnp.bfloat16)
    return (output, grad_q, grad_k, grad_v, grad_text_k, text_dv_sum)


def solution(mesh):
    in_specs = (
        P(("groups", "ctx"), ("mp", "sec")),
        P(("groups", "ctx"), ("mp", "sec")),
        P(("groups", "ctx"), ("mp", "sec")),
        P("groups", ("mp", "sec")),
        P("groups", ("mp", "sec")),
        P(("groups", "ctx")),
        P("groups"),
        P(("groups", "ctx"), ("mp", "sec")),
    )
    out_specs = (
        P(("groups", "ctx"), ("mp", "sec")),
        P(("groups", "ctx"), ("mp", "sec")),
        P(("groups", "ctx"), ("mp", "sec")),
        P(("groups", "ctx"), ("mp", "sec")),
        P("groups", ("mp", "sec")),
        P("groups", ("mp", "sec")),
    )
    return jax.shard_map(shards, mesh=mesh, in_specs=in_specs, out_specs=out_specs, check_vma=False)
```

profile of v0, /device:TPU:0, one launch (start us, length us, event | category | flops | bytes accessed | tf_op | source)
XLA Modules:
  0.0 175.4 jit_solution(14083042837732607315)
XLA Ops:
  8.1 3.8 %convert_reduce_fusion = (f32[4,128]{1,0:T(4,128)}, f32[4,128,1024]{2,1,0:T(8,128)}) fusion(pred[128,1024]{1,0:T(8,128)(4,1)S(1)} %compare_and_fusion.1, bf16[1024,4,128]{0,2,1:T(8,128)(2,1)} %multiply_convert_fusion.3, f32[128,4]{0,1:T(4,128)S(1)} %add_rsqrt_fusion.2, bf16[128,4,128]{0,2,1:T(8,128)(2,1)S(1)} %bitcast.126), kind=kOutput, calls=%fused_computation.13 | convolution fusion | flops 137035264 | bytes 3411968 | tf_op jit(solution)/shard_map/qhd,khd->hqk/dot_general | solution.py:31
  13.7 16.7 %all_gather.24 = bf16[512,512]{0,1:T(8,128)(2,1)S(1)} all-gather(bf16[128,512]{0,1:T(8,128)(2,1)S(1)} %fusion.51), channel_id=1, replica_groups=mesh['groups'=2,'ctx'=4,'mp'=2,'sec'=2] {'ctx'}, dimensions={0}, use_global_device_ids=true | all-gather | bytes 655360 | tf_op jit(solution)/shard_map/all_gather | solution.py:108
  30.4 10.1 %all-gather = s32[4,1,128]{2,1,0:T(1,128)S(1)} all-gather(s32[1,1,128]{2,1,0:T(1,128)} %bitcast.145), channel_id=1, replica_groups=mesh['groups'=2,'ctx'=4,'mp'=2,'sec'=2] {'ctx'}, dimensions={0}, use_global_device_ids=true | all-gather | bytes 2560 | tf_op jit(solution)/shard_map/all_gather | solution.py:70
  41.3 2.1 %convert_reduce_fusion.1 = (f32[4,128]{1,0:T(4,128)S(1)}, f32[4,128,512]{2,1,0:T(8,128)}) fusion(bf16[512,4,128]{0,2,1:T(8,128)(2,1)S(1)} %bitcast.132, f32[128,4]{0,1:T(4,128)} %copy-done.14, pred[128,512]{1,0:T(8,128)(4,1)S(1)} %broadcast_compare_fusion.1, bf16[128,4,128]{0,2,1:T(8,128)(2,1)S(1)} %bitcast.127), kind=kOutput, calls=%fused_computation.51 | convolution fusion | flops 68615680 | bytes 1773568 | tf_op jit(solution)/shard_map/qhd,khd->hqk/dot_general | solution.py:31
  45.3 16.4 %all_gather.25 = bf16[512,512]{1,0:T(8,128)(2,1)} all-gather(bf16[128,512]{1,0:T(8,128)(2,1)S(1)} %copy-done.4), channel_id=1, replica_groups=mesh['groups'=2,'ctx'=4,'mp'=2,'sec'=2] {'ctx'}, dimensions={0}, use_global_device_ids=true | all-gather | bytes 655360 | tf_op jit(solution)/shard_map/all_gather | solution.py:109
  61.7 2.1 %copy.123 = bf16[512,512]{0,1:T(8,128)(2,1)} copy(bf16[512,512]{1,0:T(8,128)(2,1)} %all_gather.25) | data formatting | bytes 1048576 | tf_op jit(solution)/shard_map/all_gather | solution.py:109
  63.8 3.0 %multiply_reduce_fusion.3 = (f32[128,4]{0,1:T(4,128)}, bf16[128,4,128]{0,2,1:T(8,128)(2,1)}) fusion(bf16[128,512]{0,1:T(8,128)(2,1)S(1)} %copy.124, f32[128,4]{0,1:T(4,128)} %bitcast.143, f32[4,128,128]{1,2,0:T(8,128)} %fusion.29, bf16[512,4,128]{0,2,1:T(8,128)(2,1)} %bitcast.128, f32[4,128,512]{2,1,0:T(8,128)} %get-tuple-element.43), kind=kOutput, calls=%fused_computation.72 | convolution fusion | flops 67829248 | bytes 2101248 | tf_op jit(solution)/shard_map/hqk,khd->hqd/dot_general | solution.py:95
  68.4 3.8 %fusion.21 = f32[4,128,128]{1,2,0:T(8,128)} fusion(bf16[1024,4,128]{0,2,1:T(8,128)(2,1)} %multiply_convert_fusion.3, f32[4,128,1024]{2,1,0:T(8,128)} %get-tuple-element.41, bf16[128,4,128]{0,2,1:T(8,128)(2,1)S(1)} %bitcast.130, f32[4,128]{1,0:T(4,128)} %bitcast.148, f32[4,128]{1,0:T(4,128)} %add.78, pred[128,1024]{1,0:T(8,128)(4,1)} %copy-done.6, ...), kind=kOutput, calls=%fused_computation.34 | convolution fusion | flops 271581184 | bytes 4722688 | tf_op jit(solution)/shard_map/hqk,khd->hqd/dot_general | solution.py:122
  72.3 3.4 %multiply_reduce_fusion.2 = (f32[128,4]{0,1:T(4,128)}, f32[128,4,128]{0,2,1:T(8,128)}) fusion(bf16[128,512]{0,1:T(8,128)(2,1)S(1)} %copy.115, f32[4,128,128]{1,2,0:T(8,128)} %fusion.21, bf16[512,4,128]{0,2,1:T(8,128)(2,1)} %bitcast.133, bf16[128,4,128]{0,2,1:T(8,128)(2,1)S(1)} %bitcast.131, bf16[512,4,128]{0,2,1:T(8,128)(2,1)} %bitcast.129, ...), kind=kOutput, calls=%fused_computation.71 | convolution fusion | flops 135593472 | bytes 2889728 | tf_op jit(solution)/shard_map/hqk,khd->hqd/dot_general | solution.py:142
  76.3 1.7 subtract_convert_fusion.1
  80.4 13.9 %all_gather.26 = bf16[512,512]{0,1:T(8,128)(2,1)S(1)} all-gather(bf16[128,512]{0,1:T(8,128)(2,1)S(1)} %fusion.50), channel_id=1, replica_groups=mesh['groups'=2,'ctx'=4,'mp'=2,'sec'=2] {'ctx'}, dimensions={0}, use_global_device_ids=true | all-gather | bytes 655360 | tf_op jit(solution)/shard_map/all_gather | solution.py:188
  94.2 12.1 %all_gather.27 = f32[512,4]{0,1:T(4,128)S(1)} all-gather(f32[128,4]{0,1:T(4,128)} %bitcast.144), channel_id=1, replica_groups=mesh['groups'=2,'ctx'=4,'mp'=2,'sec'=2] {'ctx'}, dimensions={0}, use_global_device_ids=true | all-gather | bytes 10240 | tf_op jit(solution)/shard_map/all_gather | solution.py:156
  107.1 2.1 %fusion.13 = f32[4,512,128]{2,1,0:T(8,128)} fusion(bf16[512,4,128]{0,2,1:T(8,128)(2,1)S(1)} %bitcast.121, f32[4,512]{1,0:T(4,128)S(1)} %bitcast.146, pred[512,128]{1,0:T(8,128)(4,1)S(1)} %broadcast_compare_fusion, f32[128,4]{0,1:T(4,128)} %copy-done.15, bf16[128,4,128]{0,2,1:T(8,128)(2,1)S(1)} %bitcast.125), kind=kOutput, calls=%fused_computation.24 | convolution fusion | flops 68091904 | bytes 1779712 | tf_op jit(solution)/shard_map/qhd,khd->hqk/dot_general | solution.py:31
  109.3 14.5 %all_gather.28 = bf16[512,512]{0,1:T(8,128)(2,1)} all-gather(bf16[128,512]{0,1:T(8,128)(2,1)S(1)} %copy.124), channel_id=1, replica_groups=mesh['groups'=2,'ctx'=4,'mp'=2,'sec'=2] {'ctx'}, dimensions={0}, use_global_device_ids=true | all-gather | bytes 655360 | tf_op jit(solution)/shard_map/all_gather | solution.py:189
  123.7 12.7 %all_gather.29 = f32[512,4]{0,1:T(4,128)} all-gather(f32[128,4]{0,1:T(4,128)S(1)} %copy-done.20), channel_id=1, replica_groups=mesh['groups'=2,'ctx'=4,'mp'=2,'sec'=2] {'ctx'}, dimensions={0}, use_global_device_ids=true | all-gather | bytes 10240 | tf_op jit(solution)/shard_map/all_gather | solution.py:157
  136.4 2.8 %multiply_reduce_fusion.1 = (f32[128,4]{0,1:T(4,128)}, f32[128,4,128]{0,2,1:T(8,128)S(1)}) fusion(bf16[128,512]{0,1:T(8,128)(2,1)S(1)} %copy.120, bf16[512,4,128]{0,2,1:T(8,128)(2,1)} %bitcast.122, f32[4,512,128]{2,1,0:T(8,128)} %fusion.13, bf16[512,4,128]{0,2,1:T(8,128)(2,1)} %bitcast.115, f32[4,512]{1,0:T(4,128)} %bitcast.138, bf16[128,512]{1,0:T(8,128)(2,1)} %param.10), kind=kOutput, calls=%fused_computation.68 | convolution fusion | flops 135265792 | bytes 2631680 | tf_op jit(solution)/shard_map/hqk,qhd->khd/dot_general | solution.py:178
  141.3 1.7 copy.140
  143.0 1.7 convolution_convert_fusion
  145.9 7.1 %select_divide_fusion = f32[4,512,1024]{2,1,0:T(8,128)} fusion(f32[4,512]{1,0:T(4,128)S(1)} %bitcast.147, pred[512,1024]{1,0:T(8,128)(4,1)S(1)} %compare_and_fusion, bf16[512,4,128]{0,2,1:T(8,128)(2,1)} %bitcast.123, bf16[1024,4,128]{0,2,1:T(8,128)(2,1)} %multiply_convert_fusion.3), kind=kOutput, calls=%fused_computation.1 | convolution fusion | flops 543162368 | bytes 10493952 | tf_op jit(solution)/shard_map/qhd,khd->hqk/dot_general | solution.py:31
  153.0 7.4 %fusion.8 = (f32[1024,4]{0,1:T(4,128)S(1)}, f32[4,128,1024]{2,1,0:T(8,128)}) fusion(f32[1024,512]{0,1:T(8,128)S(1)} %copy.116, bf16[512,4,128]{0,2,1:T(8,128)(2,1)} %bitcast.124, f32[4,512,1024]{2,1,0:T(8,128)} %select_divide_fusion, f32[4,512]{1,0:T(4,128)S(1)} %bitcast.139, bf16[512,4,128]{0,2,1:T(8,128)(2,1)} %bitcast.117, bf16[1024,512]{1,0:T(8,128)(2,1)S(1)} %copy-done), kind=kOutput, calls=%fused_computation.11 | convolution fusion | flops 1081602048 | bytes 14704640 | tf_op jit(solution)/shard_map/hqk,qhd->khd/dot_general | solution.py:206
  160.5 3.6 %fusion.6 = f32[1024,4,128]{0,2,1:T(8,128)} fusion(f32[4,128,1024]{2,1,0:T(8,128)} %get-tuple-element.51, f32[1024,4]{0,1:T(4,128)S(1)} %broadcast_multiply_fusion.1, f32[1024,4]{0,1:T(4,128)S(1)} %copy-done.9, f32[1024,4]{0,1:T(4,128)S(1)} %get-tuple-element.37, f32[1024,512]{0,1:T(8,128)S(1)} %copy.116), kind=kLoop, calls=%fused_computation.9 | loop fusion | flops 3145728 | bytes 6340608 | tf_op jit(solution)/shard_map/sub | solution.py:26
  164.1 2.9 %copy.142 = f32[1024,512]{1,0:T(8,128)} copy(f32[1024,512]{0,1:T(8,128)} %bitcast.119) | data formatting | bytes 4194304
  167.0 5.5 %fusion.1 = f32[4,1024,128]{1,2,0:T(8,128)} fusion(bf16[512,4,128]{0,2,1:T(8,128)(2,1)S(1)} %bitcast.118, f32[4,512,1024]{2,1,0:T(8,128)} %select_divide_fusion), kind=kOutput, calls=%fused_computation.3 | convolution fusion | flops 538968064 | bytes 11010048 | tf_op jit(solution)/shard_map/hqk,qhd->khd/dot_general | solution.py:209
  172.5 2.9 %copy.143 = f32[1024,512]{1,0:T(8,128)} copy(f32[1024,512]{0,1:T(8,128)} %bitcast.120) | data formatting | bytes 4194304
  (73 shorter events, 20.7 us)
Async XLA Ops:
  0.6 43.3 %copy-start = (bf16[1024,512]{1,0:T(8,128)(2,1)S(1)}, bf16[1024,512]{1,0:T(8,128)(2,1)}, u32[]{:S(2)}) copy-start(bf16[1024,512]{1,0:T(8,128)(2,1)} %param.12) | copy-start | bytes 3145732
  1.8 1.6 copy-start.10
  2.5 0.8 copy-start.16
  3.4 4.7 %copy-start.6 = (pred[128,1024]{1,0:T(8,128)(4,1)}, pred[128,1024]{1,0:T(8,128)(4,1)S(1)}, u32[]{:S(2)}) copy-start(pred[128,1024]{1,0:T(8,128)(4,1)S(1)} %compare_and_fusion.1) | copy-start | bytes 393220
  8.1 3.8 %copy-start.14 = (f32[128,4]{0,1:T(4,128)}, f32[128,4]{0,1:T(4,128)S(1)}, u32[]{:S(2)}) copy-start(f32[128,4]{0,1:T(4,128)S(1)} %add_rsqrt_fusion.2) | copy-start | bytes 6148
  13.0 30.4 %copy-start.21 = (f32[4,128]{1,0:T(4,128)S(1)}, f32[4,128]{1,0:T(4,128)}, u32[]{:S(2)}) copy-start(f32[4,128]{1,0:T(4,128)} %get-tuple-element.40) | copy-start | bytes 6148
  13.0 30.9 %copy-start.3 = (f32[4,128,1024]{2,1,0:T(8,128)S(1)}, f32[4,128,1024]{2,1,0:T(8,128)}, u32[]{:S(2)}) copy-start(f32[4,128,1024]{2,1,0:T(8,128)} %get-tuple-element.41) | copy-start | bytes 6291460
  13.0 30.9 %copy-start.7 = (pred[128,1024]{1,0:T(8,128)(4,1)S(1)}, pred[128,1024]{1,0:T(8,128)(4,1)}, u32[]{:S(2)}) copy-start(pred[128,1024]{1,0:T(8,128)(4,1)} %copy-done.6) | copy-start | bytes 393220
  13.7 26.8 %copy-start.15 = (f32[128,4]{0,1:T(4,128)}, f32[128,4]{0,1:T(4,128)S(1)}, u32[]{:S(2)}) copy-start(f32[128,4]{0,1:T(4,128)S(1)} %get-tuple-element.39) | copy-start | bytes 6148
  30.4 10.9 %copy-start.5 = (bf16[512,512]{0,1:T(8,128)(2,1)}, bf16[512,512]{0,1:T(8,128)(2,1)S(1)}, u32[]{:S(2)}) copy-start(bf16[512,512]{0,1:T(8,128)(2,1)S(1)} %all_gather.24) | copy-start | bytes 1572868
  40.5 0.8 copy-start.12
  43.3 2.0 %copy-start.4 = (bf16[128,512]{1,0:T(8,128)(2,1)S(1)}, bf16[128,512]{1,0:T(8,128)(2,1)}, u32[]{:S(2)}) copy-start(bf16[128,512]{1,0:T(8,128)(2,1)} %param.10) | copy-start | bytes 393220
  94.2 15.0 %copy-start.2 = (bf16[512,512]{0,1:T(8,128)(2,1)}, bf16[512,512]{0,1:T(8,128)(2,1)S(1)}, u32[]{:S(2)}) copy-start(bf16[512,512]{0,1:T(8,128)(2,1)S(1)} %all_gather.26) | copy-start | bytes 1572868
  106.3 3.0 %copy-start.18 = (f32[512,4]{0,1:T(4,128)}, f32[512,4]{0,1:T(4,128)S(1)}, u32[]{:S(2)}) copy-start(f32[512,4]{0,1:T(4,128)S(1)} %all_gather.27) | copy-start | bytes 24580
  107.1 16.6 %copy-start.20 = (f32[128,4]{0,1:T(4,128)S(1)}, f32[128,4]{0,1:T(4,128)}, u32[]{:S(2)}) copy-start(f32[128,4]{0,1:T(4,128)} %get-tuple-element.44) | copy-start | bytes 6148
  141.3 4.1 %copy-start.11 = (s32[1024]{0:T(1024)S(1)}, s32[1024]{0:T(1024)}, u32[]{:S(2)}) copy-start(s32[1024]{0:T(1024)} %copy-done.10) | copy-start | bytes 12292
  141.3 4.1 %copy-start.13 = (s32[4,1,128]{2,1,0:T(1,128)S(1)}, s32[4,1,128]{2,1,0:T(1,128)}, u32[]{:S(2)}) copy-start(s32[4,1,128]{2,1,0:T(1,128)} %copy-done.12) | copy-start | bytes 6148
  141.3 4.1 %copy-start.17 = (pred[1024]{0:T(1024)(128)(4,1)S(1)}, pred[1024]{0:T(1024)(128)(4,1)}, u32[]{:S(2)}) copy-start(pred[1024]{0:T(1024)(128)(4,1)} %copy-done.16) | copy-start | bytes 3076
  141.3 4.6 %copy-start.19 = (f32[512,4]{0,1:T(4,128)S(1)}, f32[512,4]{0,1:T(4,128)}, u32[]{:S(2)}) copy-start(f32[512,4]{0,1:T(4,128)} %copy-done.18) | copy-start | bytes 24580
  145.9 7.1 %copy-start.8 = (f32[512,4]{0,1:T(4,128)S(1)}, f32[512,4]{0,1:T(4,128)}, u32[]{:S(2)}) copy-start(f32[512,4]{0,1:T(4,128)} %all_gather.29) | copy-start | bytes 24580
  153.0 7.5 %copy-start.9 = (f32[1024,4]{0,1:T(4,128)S(1)}, f32[1024,4]{0,1:T(4,128)}, u32[]{:S(2)}) copy-start(f32[1024,4]{0,1:T(4,128)} %get-tuple-element.36) | copy-start | bytes 49156
  164.1 2.9 %copy-start.1 = (bf16[512,512]{0,1:T(8,128)(2,1)S(1)}, bf16[512,512]{0,1:T(8,128)(2,1)}, u32[]{:S(2)}) copy-start(bf16[512,512]{0,1:T(8,128)(2,1)} %all_gather.28) | copy-start | bytes 1572868
where the time goes:
time: 176 us; the launch traced here: 175 us
  blocking collectives  96.2 us (55%)
  matrix products  44.2 us (25%)
  local copies, waits for them, and re-layouts  18.4 us (10%)
  other arithmetic  15.7 us (9%)
    all_gather x1, blocking collectives, shards(): lax.all_gather(key_flat, 'ctx', axis=0, tiled=True)  16.7 us
    all_gather x1, blocking collectives, shards(): lax.all_gather(values, 'ctx', axis=0, tiled=True)  16.4 us
    dot_general x4, matrix products, masked_exp(): jnp.einsum('qhd,khd->hqk', query_n, key_n, preferred_element_type=jnp.flo...  15.1 us
    unnamed x53, local copies, waits for them, and re-layouts  14.8 us
    all_gather x1, blocking collectives, shards(): lax.all_gather(grad_out, 'ctx', axis=0, tiled=True)  14.5 us
    all_gather x1, blocking collectives, shards(): lax.all_gather(query_flat, 'ctx', axis=0, tiled=True)  13.9 us
    all_gather x1, blocking collectives, shards(): lax.all_gather(jnp.transpose(inner), 'ctx', axis=0, tiled=True)  12.7 us
    all_gather x1, blocking collectives, shards(): lax.all_gather(jnp.transpose(norm_sum), 'ctx', axis=0, tiled=True)  12.1 us

commit v1 on v0

v1 whole, which is shorter than its diff:
```python
import functools
import math

import jax
import jax.numpy as jnp
from jax import lax
from jax.experimental import pallas as pl
from jax.experimental.pallas import tpu as pltpu
from jax.sharding import PartitionSpec as P

HD = 128
SEG_ROWS = 16
FAR = 16384.0
KEY_BLOCK = 256
ROW_BLOCK = 512

epsilon = 1e-06

F32 = jnp.float32
BF16 = jnp.bfloat16


def inverse_rms(x):
    return lax.rsqrt(jnp.mean(x * x, axis=-1, keepdims=True) + epsilon)


def norm_back(x, upstream):
    inverse = inverse_rms(x)
    inner = jnp.sum(upstream * x, axis=-1, keepdims=True) * (1.0 / HD)
    return upstream * inverse - x * (inner * inverse * inverse * inverse)


def dot(a, b, contract):
    return lax.dot_general(a, b, ((contract[:1], contract[1:]), ((), ())), preferred_element_type=F32)


def pack_kernel(chunks, q_ref, k_ref, v_ref, g_ref, seg_ref, *outs):
    length = q_ref.shape[0]
    for (first, count), out in zip(chunks, outs):
        for b in range(count):
            cols = pl.ds((first + b) * HD, HD)
            for a, ref in enumerate((q_ref, k_ref)):
                x = ref[:, cols].astype(F32)
                out[pl.ds((4 * b + a) * length, length), :] = (x * inverse_rms(x)).astype(BF16)
            for a, ref in enumerate((v_ref, g_ref)):
                out[pl.ds((4 * b + 2 + a) * length, length), :] = ref[:, cols]
        seg = seg_ref[...].astype(F32).astype(BF16)
        out[pl.ds(4 * count * length, SEG_ROWS), :] = jnp.broadcast_to(seg, (SEG_ROWS, length))


def pack(queries, keys, values, grad_out, segment, chunks):
    length = queries.shape[0]
    return pl.pallas_call(
        functools.partial(pack_kernel, chunks),
        out_shape=[
            jax.ShapeDtypeStruct((4 * count * length + SEG_ROWS, HD), BF16) for _, count in chunks
        ],
        name="pack",
    )(queries, keys, values, grad_out, segment.reshape(1, length))


def attend_kernel(n, length, count, routed, *refs):
    refs = list(refs)
    len_ref = refs.pop(0)
    pieces = [refs.pop(0) for _ in range(6 if routed else 2)]
    q_raw, k_raw, tk_ref, tv_ref = refs[:4]
    out_ref, gq_ref, gk_ref, gv_ref, gtk_ref, gtv_ref = refs[-18:-12]
    held, qx, kx, vx, gx, e_ref, dp_ref, dk_ref, dv_ref, dq_ref, att_ref, sems = refs[-12:]
    text_rows = tk_ref.shape[0]
    clips = len_ref.shape[0]
    per_clip = text_rows // clips
    video = n * length
    total = video + text_rows
    head = pl.program_id(0)
    rows_of = min(video, ROW_BLOCK)
    row_blocks = video // rows_of
    scale = 1.0 / math.sqrt(HD)
    exponent = scale * math.log2(math.e)
    seg_at = 4 * count * length

    @pl.when(head == 0)
    def _():
        me = lax.axis_index("ctx")
        if routed:
            own, near, far, hop_far, hop_near, last = pieces
            end = (me == 0) | (me == 3)

            def copy(source, slot):
                return pltpu.make_async_copy(source, held.at[slot], sems.at[slot])

            copy(own, 0).start()
            copy(near, 1).start()

            @pl.when(end)
            def _():
                copy(hop_far, 2).start()
                copy(last, 3).start()

            @pl.when(jnp.logical_not(end))
            def _():
                copy(hop_near, 2).start()
                copy(far, 3).start()

            for slot in range(4):
                copy(own, slot).wait()
        else:
            own, gathered = pieces

            def fetch(s, _):
                source = lax.rem(me + s, n)
                pltpu.make_async_copy(gathered.at[source], held.at[s], sems.at[0]).start()
                pltpu.make_async_copy(gathered.at[source], held.at[s], sems.at[0]).wait()
                return 0

            lax.fori_loop(0, n, fetch, 0)

        lane = lax.broadcasted_iota(jnp.int32, (length, HD), 1)
        sub = lax.broadcasted_iota(jnp.int32, (HD, length), 0).astype(F32)

        def mask_rows(s, _):
            seg = held[s, pl.ds(seg_at, SEG_ROWS), :].astype(F32)[0:1, :]
            onehot = jnp.where(jnp.broadcast_to(seg, (HD, length)) == sub, 1.0, 0.0).T
            rows = pl.ds(pl.multiple_of(s * length, length), length)
            qx[rows, HD:] = jnp.where(lane == clips, 1.0, onehot).astype(BF16)
            kx[rows, HD:] = jnp.where(lane < clips, (onehot - 1.0) * FAR, 0.0).astype(BF16)
            return 0

        lax.fori_loop(0, n, mask_rows, 0, unroll=n <= 4)
        lane = lax.broadcasted_iota(jnp.int32, (per_clip, HD), 1)
        place = lax.broadcasted_iota(jnp.int32, (per_clip, HD), 0)
        for c in range(clips):
            other = jnp.where((lane < clips) & (lane != c), -FAR, 0.0)
            dead = jnp.where((lane == clips) & (place >= len_ref[c]), -FAR, 0.0)
            kx[pl.ds(video + c * per_clip, per_clip), HD:] = (other + dead).astype(BF16)

    def place_rows(s, _):
        rows = pl.ds(pl.multiple_of(s * length, length), length)
        for a, (ref, cols) in enumerate(((qx, pl.ds(0, HD)), (kx, pl.ds(0, HD)), (vx, pl.ds(0, HD)), (gx, pl.ds(0, HD)))):
            at = pl.multiple_of((4 * head + a) * length, length)
            ref[rows, cols] = held[s, pl.ds(at, length), :]
        return 0

    lax.fori_loop(0, n, place_rows, 0, unroll=n <= 4)
    text = tk_ref[...].astype(F32)
    kx[pl.ds(video, text_rows), :HD] = (text * inverse_rms(text)).astype(BF16)
    vx[pl.ds(video, text_rows), :] = tv_ref[...]

    def rows_step(rb, first):
        rows = pl.ds(pl.multiple_of(rb * rows_of, rows_of), rows_of)
        q_all = qx[rows, :]
        q_here = qx[rows, :HD]
        g_here = gx[rows, :]

        def score(kb, sums):
            at = pl.ds(pl.multiple_of(kb * KEY_BLOCK, KEY_BLOCK), KEY_BLOCK)
            e = jnp.exp2(dot(kx[at, :], q_all, (1, 1)) * exponent)
            dp = dot(vx[at, :], g_here, (1, 1))
            e_ref[at, :] = e
            dp_ref[at, :] = dp
            shape = (KEY_BLOCK // 8, 8, rows_of)
            return (
                sums[0] + jnp.sum(e.reshape(shape), axis=0),
                sums[1] + jnp.sum((e * dp).reshape(shape), axis=0),
            )

        blocks = total // KEY_BLOCK
        zero = jnp.zeros((8, rows_of), F32)
        sums = lax.fori_loop(0, blocks, score, (zero, zero), unroll=blocks <= 8)
        inv = 1.0 / jnp.sum(sums[0], axis=0, keepdims=True)
        inner = jnp.sum(sums[1], axis=0, keepdims=True) * inv

        def add(ref, at, value):
            if row_blocks == 1:
                ref[at, :] = value
            else:
                ref[at, :] = jnp.where(rb == 0, value, ref[at, :] + value)

        def terms(at, cols):
            p = e_ref[at, cols] * inv[:, cols]
            ds = p * (dp_ref[at, cols] - inner[:, cols])
            return p.astype(BF16), ds.astype(BF16)

        everything = slice(0, rows_of)
        mine = slice(0, length)

        def query_side(at, p, ds, start):
            att = dot(p, vx[at, :], (0, 0))
            dq = dot(ds, kx[at, :HD], (0, 0))
            if start:
                att_ref[...] = att
                dq_ref[...] = dq
            else:
                att_ref[...] += att
                dq_ref[...] += dq

        def own_rows(at, p, ds, start=False):
            if row_blocks == 1:
                query_side(at, p[:, mine], ds[:, mine], start)
            else:

                @pl.when(rb == 0)
                def _():
                    query_side(at, p[:, mine], ds[:, mine], start)

        own = pl.ds(0, length)
        p, ds = terms(own, everything)
        add(dk_ref, own, dot(ds, q_here, (1, 0)))
        add(dv_ref, own, dot(p, g_here, (1, 0)))
        own_rows(own, p, ds, True)

        def others():
            def other(s, _):
                at = pl.ds(pl.multiple_of(s * length, length), length)
                p, ds = terms(at, mine)
                query_side(at, p, ds, False)
                return 0

            lax.fori_loop(1, n, other, 0, unroll=n <= 4)

        if row_blocks == 1:
            others()
        else:
            pl.when(rb == 0)(others)
        for c in range(text_rows // KEY_BLOCK):
            at = pl.ds(video + c * KEY_BLOCK, KEY_BLOCK)
            to = pl.ds(c * KEY_BLOCK, KEY_BLOCK)
            p, ds = terms(at, everything)
            add(gtk_ref, to, dot(ds, q_here, (1, 0)))
            add(gtv_ref, to, dot(p, g_here, (1, 0)))
            own_rows(at, p, ds)

    if row_blocks == 1:
        rows_step(0, True)
    else:

        def step(rb, _):
            rows_step(rb, False)
            return 0

        lax.fori_loop(0, row_blocks, step, 0)

    out_ref[...] = att_ref[...].astype(BF16)
    gq_ref[...] = norm_back(q_raw[...].astype(F32), dq_ref[...] * scale).astype(BF16)
    gk_ref[...] = norm_back(k_raw[...].astype(F32), dk_ref[...] * scale).astype(BF16)
    gv_ref[...] = dv_ref[...].astype(BF16)
    gtk_ref[...] = norm_back(tk_ref[...].astype(F32), gtk_ref[...] * scale)


def attend(n, chunk, text_len, pieces, queries, keys, text_keys, text_values, before):
    first, count = chunk
    routed = len(pieces) > 2
    length, width = queries.shape
    text_rows = text_keys.shape[0]
    video = n * length
    total = video + text_rows
    rows_of = min(video, ROW_BLOCK)
    anywhere = pl.BlockSpec(memory_space=pl.ANY)

    def column(rows):
        return pl.BlockSpec((rows, HD), lambda h: (0, first + h))

    in_specs = (
        [pl.BlockSpec(memory_space=pltpu.SMEM)]
        + [anywhere] * len(pieces)
        + [column(length)] * 2
        + [column(text_rows)] * 2
        + [anywhere] * len(before)
    )
    out_rows = [length] * 4 + [text_rows] * 2
    out_types = [BF16] * 4 + [F32] * 2
    operands = [text_len, *pieces, queries, keys, text_keys, text_values, *before]
    base = len(operands) - len(before)
    pairs = count * total * rows_of * (video // rows_of)
    return pl.pallas_call(
        functools.partial(attend_kernel, n, length, count, routed),
        grid=(count,),
        in_specs=in_specs,
        out_specs=[column(rows) for rows in out_rows],
        out_shape=[
            jax.ShapeDtypeStruct((rows, width), dtype) for rows, dtype in zip(out_rows, out_types)
        ],
        scratch_shapes=[
            pltpu.VMEM((n, 4 * count * length + SEG_ROWS, HD), BF16),
            pltpu.VMEM((video, 2 * HD), BF16),
            pltpu.VMEM((total, 2 * HD), BF16),
            pltpu.VMEM((total, HD), BF16),
            pltpu.VMEM((video, HD), BF16),
            pltpu.VMEM((total, rows_of), F32),
            pltpu.VMEM((total, rows_of), F32),
            pltpu.VMEM((length, HD), F32),
            pltpu.VMEM((length, HD), F32),
            pltpu.VMEM((length, HD), F32),
            pltpu.VMEM((length, HD), F32),
            pltpu.SemaphoreType.DMA((4,)),
        ],
        input_output_aliases={base + i: i for i in range(len(before))},
        compiler_params=pltpu.CompilerParams(vmem_limit_bytes=56 * 1024 * 1024),
        cost_estimate=pl.CostEstimate(
            flops=12 * pairs * HD, bytes_accessed=count * 3 * 1024 * 1024, transcendentals=pairs
        ),
        name="attend",
    )(*operands)


def shards(n, queries, keys, values, text_keys, text_values, segment, text_len, grad_out):
    heads = queries.shape[1] // HD
    half = max(heads // 2, 1)
    chunks = [(first, half) for first in range(0, heads, half)]
    payloads = pack(queries, keys, values, grad_out, segment, chunks)

    def send(x, pairs):
        return lax.ppermute(x, "ctx", pairs)

    if n == 4:
        outer = [(0, 1), (1, 0), (2, 3), (3, 2)]
        middle = [(1, 2), (2, 1)]
        outward = [(1, 0), (2, 3)]
        first = [(send(x, outer), send(x, middle)) for x in payloads]
        pieces = []
        for x, (near, far) in zip(payloads, first):
            hop_far = send(far, outward)
            hop_near = send(near, middle)
            last = send(hop_near, outward)
            pieces.append((x, near, far, hop_far, hop_near, last))
    else:
        pieces = [(x, lax.all_gather(x, "ctx", axis=0)) for x in payloads]
    outs = ()
    for chunk, piece in zip(chunks, pieces):
        outs = attend(n, chunk, text_len, piece, queries, keys, text_keys, text_values, outs)
    return tuple(outs)


def solution(mesh):
    rows = P(("groups", "ctx"), ("mp", "sec"))
    text = P("groups", ("mp", "sec"))
    in_specs = (rows, rows, rows, text, text, P(("groups", "ctx")), P("groups"), rows)
    out_specs = (rows, rows, rows, rows, text, text)
    return jax.shard_map(
        functools.partial(shards, mesh.shape["ctx"]),
        mesh=mesh,
        in_specs=in_specs,
        out_specs=out_specs,
        check_vma=False,
    )
```

time: 176 us -> 57.7 us (0.33)
  blocking collectives: 96.2 us -> 0 us
  matrix products: 44.2 us -> 0 us
  waiting for transfers between devices: 0 us -> 25.1 us
  Pallas kernels: 0 us -> 18.9 us
  local copies, waits for them, and re-layouts: 18.4 us -> 1.5 us
  other arithmetic: 15.7 us -> 0 us
  starting transfers between devices: 0 us -> 10.9 us
    all_gather x7 -> x0, blocking collectives: 96.2 us -> none  [the longest x1 16.7 us: shards(): lax.all_gather(key_flat, 'ctx', axis=0, tiled=True)]
    dot_general x12 -> x0, matrix products: 44.2 us -> none  [the longest x4 15.1 us: masked_exp(): jnp.einsum('qhd,khd->hqk', query_n, key_n, preferred_element_type=jnp.flo...]
    ppermute x0 -> x10, waiting for transfers between devices: none -> 25.1 us  [send(): return lax.ppermute(x, 'ctx', pairs)]
    pallas_call x0 -> x3, Pallas kernels: none -> 18.9 us  [the longest x2 16.9 us: attend(): pl.pallas_call(functools.partial(attend_kernel, n, length, count, routed)...]
    unnamed x53 -> x20, local copies, waits for them, and re-layouts: 14.8 us -> 1.5 us
    ppermute x0 -> x10, starting transfers between devices: none -> 10.9 us  [send(): return lax.ppermute(x, 'ctx', pairs)]
    convert_element_type x5 -> x0, other arithmetic: 5.03 us -> none  [the longest x3 1.94 us: normalize(): return (per_head * inverse).astype(jnp.bfloat16)]
    sub x1 -> x0, other arithmetic: 3.64 us -> none  [norm_back(): upstream * inverse - per_head * inner * inverse * inverse * inverse]
  transfers between devices with their start and end apart: 0 -> 10, of which waited for: 0 -> 4; matrix products, arithmetic and copies ran while one was open for 0% -> 0% of each run, Pallas kernels for 0% -> 15%
where the time goes in v1:
time: 57.7 us; the launch traced here: 57.4 us
  waiting for transfers between devices  25.1 us (44%)
  Pallas kernels  18.9 us (33%)
  starting transfers between devices  10.9 us (19%)
  local copies, waits for them, and re-layouts  1.5 us (3%)
  between operations  0.85 us (1%)
    ppermute x10, waiting for transfers between devices, send(): return lax.ppermute(x, 'ctx', pairs)  25.1 us
    pallas_call x2, Pallas kernels, attend(): pl.pallas_call(functools.partial(attend_kernel, n, length, count, routed)...  16.9 us
    ppermute x10, starting transfers between devices, send(): return lax.ppermute(x, 'ctx', pairs)  10.9 us
    pallas_call x1, Pallas kernels, pack(): pl.pallas_call(functools.partial(pack_kernel, chunks), out_shape=[jax.Sha...  2.06 us
    unnamed x20, local copies, waits for them, and re-layouts  1.5 us
  transfers between devices with their start and end apart: 10, of which 4 were waited for; matrix products, arithmetic and copies ran while one was open for 0% of the time, Pallas kernels for 15%

profile of v1, /device:TPU:0, one launch (start us, length us, event | category | flops | bytes accessed | tf_op | source)
XLA Modules:
  0.0 57.4 jit_solution(5143750276991528098)
XLA Ops:
  0.6 2.1 %pack.1 = (bf16[1040,128]{1,0:T(8,128)(2,1)}, bf16[1040,128]{1,0:T(8,128)(2,1)}) custom-call(bf16[128,512]{1,0:T(8,128)(2,1)} %refs_7_.3, bf16[128,512]{1,0:T(8,128)(2,1)} %refs_8_.3, bf16[128,512]{1,0:T(8,128)(2,1)} %v_ref.1, bf16[128,512]{1,0:T(8,128)(2,1)} %g_ref.1, s32[1,128]{1,0:T(1,128)} %bitcast.1), custom_call_target="tpu_custom_call" | custom-call | tf_op jit(solution)/shard_map/pack/pallas_call | solution.py:53
  2.7 3.0 %collective-permute-start.5 = (bf16[1040,128]{1,0:T(8,128)(2,1)}, bf16[1040,128]{1,0:T(8,128)(2,1)S(1)}, u32[]{:S(2)}, u32[]{:S(2)}) collective-permute-start(bf16[1040,128]{1,0:T(8,128)(2,1)} %get-tuple-element.15.refs_1_), channel_id=1, source_target_pairs={{0,4},{4,0},{8,12},{12,8},{1,5},{5,1},{9,13},{13,9},{2,6},{6,2},{1... | collective-permute-start | bytes 798728 | tf_op jit(solution)/shard_map/ppermute | solution.py:312
  5.7 0.0 collective-permute-start
  5.8 0.7 %collective-permute-start.6 = (bf16[1040,128]{1,0:T(8,128)(2,1)}, bf16[1040,128]{1,0:T(8,128)(2,1)S(1)}, u32[]{:S(2)}, u32[]{:S(2)}) collective-permute-start(bf16[1040,128]{1,0:T(8,128)(2,1)} %get-tuple-element.15.refs_1_), channel_id=1, source_target_pairs={{4,8},{8,4},{5,9},{9,5},{6,10},{10,6},{7,11},{11,7},{20,24},{24,20... | collective-permute-start | bytes 798728 | tf_op jit(solution)/shard_map/ppermute | solution.py:312
  6.4 6.7 %collective-permute-done.5.refs_2_ = bf16[1040,128]{1,0:T(8,128)(2,1)S(1)} collective-permute-done((bf16[1040,128]{1,0:T(8,128)(2,1)}, bf16[1040,128]{1,0:T(8,128)(2,1)S(1)}, u32[]{:S(2)}, u32[]{:S(2)}) %collective-permute-start.5) | collective-permute-done | bytes 266272 | tf_op jit(solution)/shard_map/ppermute | solution.py:312
  13.2 0.7 %collective-permute-start.8 = (bf16[1040,128]{1,0:T(8,128)(2,1)S(1)}, bf16[1040,128]{1,0:T(8,128)(2,1)S(1)}, u32[]{:S(2)}, u32[]{:S(2)}) collective-permute-start(bf16[1040,128]{1,0:T(8,128)(2,1)S(1)} %collective-permute-done.5.refs_2_), channel_id=1, source_target_pairs={{4,8},{8,4},{5,9},{9,5},{6,10},{10,6},{7,11},{11,7},{20,24},{24,20... | collective-permute-start | bytes 798728 | tf_op jit(solution)/shard_map/ppermute | solution.py:312
  13.8 0.7 %collective-permute-start.1 = (bf16[1040,128]{1,0:T(8,128)(2,1)}, bf16[1040,128]{1,0:T(8,128)(2,1)S(1)}, u32[]{:S(2)}, u32[]{:S(2)}) collective-permute-start(bf16[1040,128]{1,0:T(8,128)(2,1)} %get-tuple-element.14.refs_1_), channel_id=1, source_target_pairs={{4,8},{8,4},{5,9},{9,5},{6,10},{10,6},{7,11},{11,7},{20,24},{24,20... | collective-permute-start | bytes 798728 | tf_op jit(solution)/shard_map/ppermute | solution.py:312
  14.5 3.5 %collective-permute-done.refs_2_ = bf16[1040,128]{1,0:T(8,128)(2,1)S(1)} collective-permute-done((bf16[1040,128]{1,0:T(8,128)(2,1)}, bf16[1040,128]{1,0:T(8,128)(2,1)S(1)}, u32[]{:S(2)}, u32[]{:S(2)}) %collective-permute-start) | collective-permute-done | bytes 266272 | tf_op jit(solution)/shard_map/ppermute | solution.py:312
  18.0 0.7 %collective-permute-start.3 = (bf16[1040,128]{1,0:T(8,128)(2,1)S(1)}, bf16[1040,128]{1,0:T(8,128)(2,1)S(1)}, u32[]{:S(2)}, u32[]{:S(2)}) collective-permute-start(bf16[1040,128]{1,0:T(8,128)(2,1)S(1)} %collective-permute-done.refs_2_), channel_id=1, source_target_pairs={{4,8},{8,4},{5,9},{9,5},{6,10},{10,6},{7,11},{11,7},{20,24},{24,20... | collective-permute-start | bytes 798728 | tf_op jit(solution)/shard_map/ppermute | solution.py:312
  18.7 0.0 collective-permute-done.6.refs_3_
  18.7 1.3 %collective-permute-start.7 = (bf16[1040,128]{1,0:T(8,128)(2,1)S(1)}, bf16[1040,128]{1,0:T(8,128)(2,1)S(1)}, u32[]{:S(2)}, u32[]{:S(2)}) collective-permute-start(bf16[1040,128]{1,0:T(8,128)(2,1)S(1)} %collective-permute-done.6.refs_3_), channel_id=1, source_target_pairs={{4,0},{8,12},{5,1},{9,13},{6,2},{10,14},{7,3},{11,15},{20,16},{24,... | collective-permute-start | bytes 798728 | tf_op jit(solution)/shard_map/ppermute | solution.py:312
  20.0 0.0 collective-permute-done.8.refs_5_
  20.0 1.3 %collective-permute-start.9 = (bf16[1040,128]{1,0:T(8,128)(2,1)S(1)}, bf16[1040,128]{1,0:T(8,128)(2,1)S(1)}, u32[]{:S(2)}, u32[]{:S(2)}) collective-permute-start(bf16[1040,128]{1,0:T(8,128)(2,1)S(1)} %collective-permute-done.8.refs_5_), channel_id=1, source_target_pairs={{4,0},{8,12},{5,1},{9,13},{6,2},{10,14},{7,3},{11,15},{20,16},{24,... | collective-permute-start | bytes 798728 | tf_op jit(solution)/shard_map/ppermute | solution.py:312
  21.3 0.0 collective-permute-done.1.refs_3_
  21.4 1.3 %collective-permute-start.2 = (bf16[1040,128]{1,0:T(8,128)(2,1)S(1)}, bf16[1040,128]{1,0:T(8,128)(2,1)S(1)}, u32[]{:S(2)}, u32[]{:S(2)}) collective-permute-start(bf16[1040,128]{1,0:T(8,128)(2,1)S(1)} %collective-permute-done.1.refs_3_), channel_id=1, source_target_pairs={{4,0},{8,12},{5,1},{9,13},{6,2},{10,14},{7,3},{11,15},{20,16},{24,... | collective-permute-start | bytes 798728 | tf_op jit(solution)/shard_map/ppermute | solution.py:312
  22.7 1.3 %collective-permute-start.4 = (bf16[1040,128]{1,0:T(8,128)(2,1)S(1)}, bf16[1040,128]{1,0:T(8,128)(2,1)S(1)}, u32[]{:S(2)}, u32[]{:S(2)}) collective-permute-start(bf16[1040,128]{1,0:T(8,128)(2,1)S(1)} %collective-permute-done.3.refs_5_), channel_id=1, source_target_pairs={{4,0},{8,12},{5,1},{9,13},{6,2},{10,14},{7,3},{11,15},{20,16},{24,... | collective-permute-start | bytes 798728 | tf_op jit(solution)/shard_map/ppermute | solution.py:312
  24.0 9.2 %collective-permute-done.7.refs_4_ = bf16[1040,128]{1,0:T(8,128)(2,1)S(1)} collective-permute-done((bf16[1040,128]{1,0:T(8,128)(2,1)S(1)}, bf16[1040,128]{1,0:T(8,128)(2,1)S(1)}, u32[]{:S(2)}, u32[]{:S(2)}) %collective-permute-start.7) | collective-permute-done | bytes 266272 | tf_op jit(solution)/shard_map/ppermute | solution.py:312
  33.2 5.7 %collective-permute-done.9.refs_6_ = bf16[1040,128]{1,0:T(8,128)(2,1)S(1)} collective-permute-done((bf16[1040,128]{1,0:T(8,128)(2,1)S(1)}, bf16[1040,128]{1,0:T(8,128)(2,1)S(1)}, u32[]{:S(2)}, u32[]{:S(2)}) %collective-permute-start.9) | collective-permute-done | bytes 266272 | tf_op jit(solution)/shard_map/ppermute | solution.py:312
  38.9 0.7 %copy-done.9 = bf16[1040,128]{1,0:T(8,128)(2,1)} copy-done((bf16[1040,128]{1,0:T(8,128)(2,1)}, bf16[1040,128]{1,0:T(8,128)(2,1)S(1)}, u32[]{:S(2)}) %copy-start.9) | copy-done | bytes 266264
  39.6 8.4 %attend.2 = (bf16[128,512]{1,0:T(8,128)(2,1)}, bf16[128,512]{1,0:T(8,128)(2,1)}, bf16[128,512]{1,0:T(8,128)(2,1)}, bf16[128,512]{1,0:T(8,128)(2,1)}, f32[1024,512]{1,0:T(8,128)}, /*index=5*/f32[1024,512]{1,0:T(8,128)}) custom-call(s32[4]{0:T(128)} %refs_0_.3, bf16[1040,128]{1,0:T(8,128)(2,1)} %get-tuple-element.15.refs_1_, bf16[1040,128]{1,0:T(8,128)(2,1)} %copy-done.2, ...), custom_call_target="tpu_custom_call" | custom-call | flops 2415919104 | bytes 6291456 | tf_op jit(solution)/shard_map/attend/pallas_call | solution.py:274
  48.1 0.0 collective-permute-done.2.refs_4_
  48.1 0.7 %copy-done.6 = bf16[1040,128]{1,0:T(8,128)(2,1)} copy-done((bf16[1040,128]{1,0:T(8,128)(2,1)}, bf16[1040,128]{1,0:T(8,128)(2,1)S(1)}, u32[]{:S(2)}) %copy-start.6) | copy-done | bytes 266264
  48.8 0.1 copy-done.8
  48.9 8.5 %attend.3 = (bf16[128,512]{1,0:T(8,128)(2,1)}, bf16[128,512]{1,0:T(8,128)(2,1)}, bf16[128,512]{1,0:T(8,128)(2,1)}, bf16[128,512]{1,0:T(8,128)(2,1)}, f32[1024,512]{1,0:T(8,128)}, /*index=5*/f32[1024,512]{1,0:T(8,128)}) custom-call(s32[4]{0:T(128)} %refs_0_.3, ...), custom_call_target="tpu_custom_call", output_to_operand_aliasing={{0}: (11, {}), {1}: (12, {}), {2}: (13, {}), {3}: (14, {}),... | custom-call | flops 2415919104 | bytes 6291456 | tf_op jit(solution)/shard_map/attend/pallas_call | solution.py:274
  (19 shorter events, 0.0 us)
Async XLA Ops:
  2.7 10.5 %collective-permute-start.5 = (bf16[1040,128]{1,0:T(8,128)(2,1)}, bf16[1040,128]{1,0:T(8,128)(2,1)S(1)}, u32[]{:S(2)}, u32[]{:S(2)}) collective-permute-start(bf16[1040,128]{1,0:T(8,128)(2,1)} %get-tuple-element.15.refs_1_), channel_id=1, source_target_pairs={{0,4},{4,0},{8,12},{12,8},{1,5},{5,1},{9,13},{13,9},{2,6},{6,2},{1... | collective-permute-start | bytes 798728 | tf_op jit(solution)/shard_map/ppermute | solution.py:312
  5.7 12.3 %collective-permute-start = (bf16[1040,128]{1,0:T(8,128)(2,1)}, bf16[1040,128]{1,0:T(8,128)(2,1)S(1)}, u32[]{:S(2)}, u32[]{:S(2)}) collective-permute-start(bf16[1040,128]{1,0:T(8,128)(2,1)} %get-tuple-element.14.refs_1_), channel_id=1, source_target_pairs={{0,4},{4,0},{8,12},{12,8},{1,5},{5,1},{9,13},{13,9},{2,6},{6,2},{1... | collective-permute-start | bytes 798728 | tf_op jit(solution)/shard_map/ppermute | solution.py:312
  5.8 13.0 %collective-permute-start.6 = (bf16[1040,128]{1,0:T(8,128)(2,1)}, bf16[1040,128]{1,0:T(8,128)(2,1)S(1)}, u32[]{:S(2)}, u32[]{:S(2)}) collective-permute-start(bf16[1040,128]{1,0:T(8,128)(2,1)} %get-tuple-element.15.refs_1_), channel_id=1, source_target_pairs={{4,8},{8,4},{5,9},{9,5},{6,10},{10,6},{7,11},{11,7},{20,24},{24,20... | collective-permute-start | bytes 798728 | tf_op jit(solution)/shard_map/ppermute | solution.py:312
  13.1 25.7 %copy-start.2 = (bf16[1040,128]{1,0:T(8,128)(2,1)}, bf16[1040,128]{1,0:T(8,128)(2,1)S(1)}, u32[]{:S(2)}) copy-start(bf16[1040,128]{1,0:T(8,128)(2,1)S(1)} %collective-permute-done.5.refs_2_) | copy-start | bytes 798724
  13.2 6.9 %collective-permute-start.8 = (bf16[1040,128]{1,0:T(8,128)(2,1)S(1)}, bf16[1040,128]{1,0:T(8,128)(2,1)S(1)}, u32[]{:S(2)}, u32[]{:S(2)}) collective-permute-start(bf16[1040,128]{1,0:T(8,128)(2,1)S(1)} %collective-permute-done.5.refs_2_), channel_id=1, source_target_pairs={{4,8},{8,4},{5,9},{9,5},{6,10},{10,6},{7,11},{11,7},{20,24},{24,20... | collective-permute-start | bytes 798728 | tf_op jit(solution)/shard_map/ppermute | solution.py:312
  13.8 7.5 %collective-permute-start.1 = (bf16[1040,128]{1,0:T(8,128)(2,1)}, bf16[1040,128]{1,0:T(8,128)(2,1)S(1)}, u32[]{:S(2)}, u32[]{:S(2)}) collective-permute-start(bf16[1040,128]{1,0:T(8,128)(2,1)} %get-tuple-element.14.refs_1_), channel_id=1, source_target_pairs={{4,8},{8,4},{5,9},{9,5},{6,10},{10,6},{7,11},{11,7},{20,24},{24,20... | collective-permute-start | bytes 798728 | tf_op jit(solution)/shard_map/ppermute | solution.py:312
  18.0 30.0 %copy-start = (bf16[1040,128]{1,0:T(8,128)(2,1)}, bf16[1040,128]{1,0:T(8,128)(2,1)S(1)}, u32[]{:S(2)}) copy-start(bf16[1040,128]{1,0:T(8,128)(2,1)S(1)} %collective-permute-done.refs_2_) | copy-start | bytes 798724
  18.0 4.6 %collective-permute-start.3 = (bf16[1040,128]{1,0:T(8,128)(2,1)S(1)}, bf16[1040,128]{1,0:T(8,128)(2,1)S(1)}, u32[]{:S(2)}, u32[]{:S(2)}) collective-permute-start(bf16[1040,128]{1,0:T(8,128)(2,1)S(1)} %collective-permute-done.refs_2_), channel_id=1, source_target_pairs={{4,8},{8,4},{5,9},{9,5},{6,10},{10,6},{7,11},{11,7},{20,24},{24,20... | collective-permute-start | bytes 798728 | tf_op jit(solution)/shard_map/ppermute | solution.py:312
  18.7 20.2 %copy-start.4 = (bf16[1040,128]{1,0:T(8,128)(2,1)}, bf16[1040,128]{1,0:T(8,128)(2,1)S(1)}, u32[]{:S(2)}) copy-start(bf16[1040,128]{1,0:T(8,128)(2,1)S(1)} %collective-permute-done.6.refs_3_) | copy-start | bytes 798724
  18.7 14.5 %collective-permute-start.7 = (bf16[1040,128]{1,0:T(8,128)(2,1)S(1)}, bf16[1040,128]{1,0:T(8,128)(2,1)S(1)}, u32[]{:S(2)}, u32[]{:S(2)}) collective-permute-start(bf16[1040,128]{1,0:T(8,128)(2,1)S(1)} %collective-permute-done.6.refs_3_), channel_id=1, source_target_pairs={{4,0},{8,12},{5,1},{9,13},{6,2},{10,14},{7,3},{11,15},{20,16},{24,... | collective-permute-start | bytes 798728 | tf_op jit(solution)/shard_map/ppermute | solution.py:312
  20.0 18.9 %copy-start.5 = (bf16[1040,128]{1,0:T(8,128)(2,1)}, bf16[1040,128]{1,0:T(8,128)(2,1)S(1)}, u32[]{:S(2)}) copy-start(bf16[1040,128]{1,0:T(8,128)(2,1)S(1)} %collective-permute-done.8.refs_5_) | copy-start | bytes 798724
  20.0 18.8 %collective-permute-start.9 = (bf16[1040,128]{1,0:T(8,128)(2,1)S(1)}, bf16[1040,128]{1,0:T(8,128)(2,1)S(1)}, u32[]{:S(2)}, u32[]{:S(2)}) collective-permute-start(bf16[1040,128]{1,0:T(8,128)(2,1)S(1)} %collective-permute-done.8.refs_5_), channel_id=1, source_target_pairs={{4,0},{8,12},{5,1},{9,13},{6,2},{10,14},{7,3},{11,15},{20,16},{24,... | collective-permute-start | bytes 798728 | tf_op jit(solution)/shard_map/ppermute | solution.py:312
  21.4 26.7 %copy-start.1 = (bf16[1040,128]{1,0:T(8,128)(2,1)}, bf16[1040,128]{1,0:T(8,128)(2,1)S(1)}, u32[]{:S(2)}) copy-start(bf16[1040,128]{1,0:T(8,128)(2,1)S(1)} %collective-permute-done.1.refs_3_) | copy-start | bytes 798724
  21.4 26.7 %collective-permute-start.2 = (bf16[1040,128]{1,0:T(8,128)(2,1)S(1)}, bf16[1040,128]{1,0:T(8,128)(2,1)S(1)}, u32[]{:S(2)}, u32[]{:S(2)}) collective-permute-start(bf16[1040,128]{1,0:T(8,128)(2,1)S(1)} %collective-permute-done.1.refs_3_), channel_id=1, source_target_pairs={{4,0},{8,12},{5,1},{9,13},{6,2},{10,14},{7,3},{11,15},{20,16},{24,... | collective-permute-start | bytes 798728 | tf_op jit(solution)/shard_map/ppermute | solution.py:312
  22.7 25.4 %copy-start.3 = (bf16[1040,128]{1,0:T(8,128)(2,1)}, bf16[1040,128]{1,0:T(8,128)(2,1)S(1)}, u32[]{:S(2)}) copy-start(bf16[1040,128]{1,0:T(8,128)(2,1)S(1)} %collective-permute-done.3.refs_5_) | copy-start | bytes 798724
  22.7 25.4 %collective-permute-start.4 = (bf16[1040,128]{1,0:T(8,128)(2,1)S(1)}, bf16[1040,128]{1,0:T(8,128)(2,1)S(1)}, u32[]{:S(2)}, u32[]{:S(2)}) collective-permute-start(bf16[1040,128]{1,0:T(8,128)(2,1)S(1)} %collective-permute-done.3.refs_5_), channel_id=1, source_target_pairs={{4,0},{8,12},{5,1},{9,13},{6,2},{10,14},{7,3},{11,15},{20,16},{24,... | collective-permute-start | bytes 798728 | tf_op jit(solution)/shard_map/ppermute | solution.py:312
  33.2 5.7 %copy-start.7 = (bf16[1040,128]{1,0:T(8,128)(2,1)}, bf16[1040,128]{1,0:T(8,128)(2,1)S(1)}, u32[]{:S(2)}) copy-start(bf16[1040,128]{1,0:T(8,128)(2,1)S(1)} %collective-permute-done.7.refs_4_) | copy-start | bytes 798724
  38.9 0.7 %copy-start.9 = (bf16[1040,128]{1,0:T(8,128)(2,1)}, bf16[1040,128]{1,0:T(8,128)(2,1)S(1)}, u32[]{:S(2)}) copy-start(bf16[1040,128]{1,0:T(8,128)(2,1)S(1)} %collective-permute-done.9.refs_6_) | copy-start | bytes 798724
  48.1 0.7 %copy-start.6 = (bf16[1040,128]{1,0:T(8,128)(2,1)}, bf16[1040,128]{1,0:T(8,128)(2,1)S(1)}, u32[]{:S(2)}) copy-start(bf16[1040,128]{1,0:T(8,128)(2,1)S(1)} %collective-permute-done.2.refs_4_) | copy-start | bytes 798724
  48.1 0.8 %copy-start.8 = (bf16[1040,128]{1,0:T(8,128)(2,1)}, bf16[1040,128]{1,0:T(8,128)(2,1)S(1)}, u32[]{:S(2)}) copy-start(bf16[1040,128]{1,0:T(8,128)(2,1)S(1)} %collective-permute-done.4.refs_6_) | copy-start | bytes 798724

commit v2 on v1

--- a/solution.py
+++ b/solution.py
@@ -62,7 +62,7 @@
 def attend_kernel(n, length, count, routed, *refs):
     refs = list(refs)
     len_ref = refs.pop(0)
-    pieces = [refs.pop(0) for _ in range(6 if routed else 2)]
+    pieces = [refs.pop(0) for _ in range(5 if routed else 2)]
     q_raw, k_raw, tk_ref, tv_ref = refs[:4]
     out_ref, gq_ref, gk_ref, gv_ref, gtk_ref, gtv_ref = refs[-18:-12]
     held, qx, kx, vx, gx, e_ref, dp_ref, dk_ref, dv_ref, dq_ref, att_ref, sems = refs[-12:]
@@ -82,7 +82,7 @@
     def _():
         me = lax.axis_index("ctx")
         if routed:
-            own, near, far, hop_far, hop_near, last = pieces
+            own, near, skip, far, last = pieces
             end = (me == 0) | (me == 3)
 
             def copy(source, slot):
@@ -90,15 +90,14 @@
 
             copy(own, 0).start()
             copy(near, 1).start()
+            copy(skip, 2).start()
 
             @pl.when(end)
             def _():
-                copy(hop_far, 2).start()
                 copy(last, 3).start()
 
             @pl.when(jnp.logical_not(end))
             def _():
-                copy(hop_near, 2).start()
                 copy(far, 3).start()
 
             for slot in range(4):
@@ -294,7 +293,7 @@
             pltpu.SemaphoreType.DMA((4,)),
         ],
         input_output_aliases={base + i: i for i in range(len(before))},
-        compiler_params=pltpu.CompilerParams(vmem_limit_bytes=56 * 1024 * 1024),
+        compiler_params=pltpu.CompilerParams(vmem_limit_bytes=(16 if routed else 56) * 1024 * 1024),
         cost_estimate=pl.CostEstimate(
             flops=12 * pairs * HD, bytes_accessed=count * 3 * 1024 * 1024, transcendentals=pairs
         ),
@@ -313,15 +312,16 @@
 
     if n == 4:
         outer = [(0, 1), (1, 0), (2, 3), (3, 2)]
+        across = [(0, 2), (2, 0), (1, 3), (3, 1)]
         middle = [(1, 2), (2, 1)]
         outward = [(1, 0), (2, 3)]
-        first = [(send(x, outer), send(x, middle)) for x in payloads]
         pieces = []
-        for x, (near, far) in zip(payloads, first):
-            hop_far = send(far, outward)
-            hop_near = send(near, middle)
-            last = send(hop_near, outward)
-            pieces.append((x, near, far, hop_far, hop_near, last))
+        for x in payloads:
+            skip = send(x, across)
+            near = send(x, outer)
+            far = send(x, middle)
+            last = send(skip, outward)
+            pieces.append((x, near, skip, far, last))
     else:
         pieces = [(x, lax.all_gather(x, "ctx", axis=0)) for x in payloads]
     outs = ()

time: 57.7 us -> 57.1 us (0.990)
  waiting for transfers between devices: 25.1 us -> 19.3 us
  local copies, waits for them, and re-layouts: 1.5 us -> 5.87 us
  starting transfers between devices: 10.9 us -> 14.9 us
  Pallas kernels: 18.9 us -> 15.9 us
    ppermute x10 -> x8, waiting for transfers between devices: 25.1 us -> 19.3 us  [send(): return lax.ppermute(x, 'ctx', pairs)]
    unnamed x20 -> x18, local copies, waits for them, and re-layouts: 1.5 us -> 5.87 us
    ppermute x10 -> x8, starting transfers between devices: 10.9 us -> 14.9 us  [send(): return lax.ppermute(x, 'ctx', pairs)]
    pallas_call x2, Pallas kernels: 16.9 us -> 13.9 us  [attend(): pl.pallas_call(functools.partial(attend_kernel, n, length, count, routed)...]
  transfers between devices with their start and end apart: 10 -> 8, of which waited for: 4 -> 3; matrix products, arithmetic and copies ran while one was open for 0% -> 0% of each run, Pallas kernels for 15% -> 12%
where the time goes in v2:
time: 57.1 us; the launch traced here: 56.7 us
  waiting for transfers between devices  19.3 us (34%)
  Pallas kernels  15.9 us (28%)
  starting transfers between devices  14.9 us (26%)
  local copies, waits for them, and re-layouts  5.87 us (10%)
  between operations  0.74 us (1%)
    ppermute x8, waiting for transfers between devices, send(): return lax.ppermute(x, 'ctx', pairs)  19.3 us
    ppermute x8, starting transfers between devices, send(): return lax.ppermute(x, 'ctx', pairs)  14.9 us
    pallas_call x2, Pallas kernels, attend(): pl.pallas_call(functools.partial(attend_kernel, n, length, count, routed)...  13.9 us
    unnamed x18, local copies, waits for them, and re-layouts  5.87 us
    pallas_call x1, Pallas kernels, pack(): pl.pallas_call(functools.partial(pack_kernel, chunks), out_shape=[jax.Sha...  2.07 us
  transfers between devices with their start and end apart: 8, of which 3 were waited for; matrix products, arithmetic and copies ran while one was open for 0% of the time, Pallas kernels for 12%

profile of v2, /device:TPU:0, one launch (start us, length us, event | category | flops | bytes accessed | tf_op | source)
XLA Modules:
  0.0 56.7 jit_solution(17140131092801972483)
XLA Ops:
  0.6 2.1 %pack.1 = (bf16[1040,128]{1,0:T(8,128)(2,1)}, bf16[1040,128]{1,0:T(8,128)(2,1)}) custom-call(bf16[128,512]{1,0:T(8,128)(2,1)} %refs_6_.3, bf16[128,512]{1,0:T(8,128)(2,1)} %refs_7_.3, bf16[128,512]{1,0:T(8,128)(2,1)} %v_ref.1, bf16[128,512]{1,0:T(8,128)(2,1)} %g_ref.1, s32[1,128]{1,0:T(1,128)} %bitcast.1), custom_call_target="tpu_custom_call" | custom-call | tf_op jit(solution)/shard_map/pack/pallas_call | solution.py:53
  2.7 4.0 %collective-permute-start.5 = (bf16[1040,128]{1,0:T(8,128)(2,1)}, bf16[1040,128]{1,0:T(8,128)(2,1)S(1)}, u32[]{:S(2)}, u32[]{:S(2)}) collective-permute-start(bf16[1040,128]{1,0:T(8,128)(2,1)} %get-tuple-element.15.refs_1_), channel_id=1, source_target_pairs={{0,8},{8,0},{4,12},{12,4},{1,9},{9,1},{5,13},{13,5},{2,10},{10,2},... | collective-permute-start | bytes 798728 | tf_op jit(solution)/shard_map/ppermute | solution.py:311
  6.7 0.0 collective-permute-start.1
  6.8 0.7 %collective-permute-start.6 = (bf16[1040,128]{1,0:T(8,128)(2,1)}, bf16[1040,128]{1,0:T(8,128)(2,1)S(1)}, u32[]{:S(2)}, u32[]{:S(2)}) collective-permute-start(bf16[1040,128]{1,0:T(8,128)(2,1)} %get-tuple-element.15.refs_1_), channel_id=1, source_target_pairs={{4,8},{8,4},{5,9},{9,5},{6,10},{10,6},{7,11},{11,7},{20,24},{24,20... | collective-permute-start | bytes 798728 | tf_op jit(solution)/shard_map/ppermute | solution.py:311
  7.4 4.8 %collective-permute-start.4 = (bf16[1040,128]{1,0:T(8,128)(2,1)}, bf16[1040,128]{1,0:T(8,128)(2,1)S(1)}, u32[]{:S(2)}, u32[]{:S(2)}) collective-permute-start(bf16[1040,128]{1,0:T(8,128)(2,1)} %get-tuple-element.15.refs_1_), channel_id=1, source_target_pairs={{0,4},{4,0},{8,12},{12,8},{1,5},{5,1},{9,13},{13,9},{2,6},{6,2},{1... | collective-permute-start | bytes 798728 | tf_op jit(solution)/shard_map/ppermute | solution.py:311
  12.2 13.4 %collective-permute-done.5.refs_3_ = bf16[1040,128]{1,0:T(8,128)(2,1)S(1)} collective-permute-done((bf16[1040,128]{1,0:T(8,128)(2,1)}, bf16[1040,128]{1,0:T(8,128)(2,1)S(1)}, u32[]{:S(2)}, u32[]{:S(2)}) %collective-permute-start.5) | collective-permute-done | bytes 266272 | tf_op jit(solution)/shard_map/ppermute | solution.py:311
  25.6 1.3 %collective-permute-start.7 = (bf16[1040,128]{1,0:T(8,128)(2,1)S(1)}, bf16[1040,128]{1,0:T(8,128)(2,1)S(1)}, u32[]{:S(2)}, u32[]{:S(2)}) collective-permute-start(bf16[1040,128]{1,0:T(8,128)(2,1)S(1)} %collective-permute-done.5.refs_3_), channel_id=1, source_target_pairs={{4,0},{8,12},{5,1},{9,13},{6,2},{10,14},{7,3},{11,15},{20,16},{24,... | collective-permute-start | bytes 798728 | tf_op jit(solution)/shard_map/ppermute | solution.py:311
  26.9 0.7 %collective-permute-start.2 = (bf16[1040,128]{1,0:T(8,128)(2,1)}, bf16[1040,128]{1,0:T(8,128)(2,1)S(1)}, u32[]{:S(2)}, u32[]{:S(2)}) collective-permute-start(bf16[1040,128]{1,0:T(8,128)(2,1)} %get-tuple-element.14.refs_1_), channel_id=1, source_target_pairs={{4,8},{8,4},{5,9},{9,5},{6,10},{10,6},{7,11},{11,7},{20,24},{24,20... | collective-permute-start | bytes 798728 | tf_op jit(solution)/shard_map/ppermute | solution.py:311
  27.6 3.7 %collective-permute-done.1.refs_3_ = bf16[1040,128]{1,0:T(8,128)(2,1)S(1)} collective-permute-done((bf16[1040,128]{1,0:T(8,128)(2,1)}, bf16[1040,128]{1,0:T(8,128)(2,1)S(1)}, u32[]{:S(2)}, u32[]{:S(2)}) %collective-permute-start.1) | collective-permute-done | bytes 266272 | tf_op jit(solution)/shard_map/ppermute | solution.py:311
  31.3 2.1 %collective-permute-start = (bf16[1040,128]{1,0:T(8,128)(2,1)}, bf16[1040,128]{1,0:T(8,128)(2,1)S(1)}, u32[]{:S(2)}, u32[]{:S(2)}) collective-permute-start(bf16[1040,128]{1,0:T(8,128)(2,1)} %get-tuple-element.14.refs_1_), channel_id=1, source_target_pairs={{0,4},{4,0},{8,12},{12,8},{1,5},{5,1},{9,13},{13,9},{2,6},{6,2},{1... | collective-permute-start | bytes 798728 | tf_op jit(solution)/shard_map/ppermute | solution.py:311
  33.4 0.0 collective-permute-done.6.refs_4_
  33.4 1.3 %collective-permute-start.3 = (bf16[1040,128]{1,0:T(8,128)(2,1)S(1)}, bf16[1040,128]{1,0:T(8,128)(2,1)S(1)}, u32[]{:S(2)}, u32[]{:S(2)}) collective-permute-start(bf16[1040,128]{1,0:T(8,128)(2,1)S(1)} %collective-permute-done.1.refs_3_), channel_id=1, source_target_pairs={{4,0},{8,12},{5,1},{9,13},{6,2},{10,14},{7,3},{11,15},{20,16},{24,... | collective-permute-start | bytes 798728 | tf_op jit(solution)/shard_map/ppermute | solution.py:311
  34.7 0.0 collective-permute-done.4.refs_2_
  34.7 2.2 %collective-permute-done.7.refs_5_ = bf16[1040,128]{1,0:T(8,128)(2,1)S(1)} collective-permute-done((bf16[1040,128]{1,0:T(8,128)(2,1)S(1)}, bf16[1040,128]{1,0:T(8,128)(2,1)S(1)}, u32[]{:S(2)}, u32[]{:S(2)}) %collective-permute-start.7) | collective-permute-done | bytes 266272 | tf_op jit(solution)/shard_map/ppermute | solution.py:311
  36.9 0.9 %copy-done = bf16[128,512]{1,0:T(8,128)(2,1)S(1)} copy-done((bf16[128,512]{1,0:T(8,128)(2,1)S(1)}, bf16[128,512]{1,0:T(8,128)(2,1)}, u32[]{:S(2)}) %copy-start) | copy-done | bytes 131096
  37.8 0.9 %copy-done.1 = bf16[128,512]{1,0:T(8,128)(2,1)S(1)} copy-done((bf16[128,512]{1,0:T(8,128)(2,1)S(1)}, bf16[128,512]{1,0:T(8,128)(2,1)}, u32[]{:S(2)}) %copy-start.1) | copy-done | bytes 131096
  38.7 1.2 %copy-done.2 = bf16[1024,512]{1,0:T(8,128)(2,1)S(1)} copy-done((bf16[1024,512]{1,0:T(8,128)(2,1)S(1)}, bf16[1024,512]{1,0:T(8,128)(2,1)}, u32[]{:S(2)}) %copy-start.2) | copy-done | bytes 1048600
  40.0 1.2 %copy-done.4 = bf16[1024,512]{1,0:T(8,128)(2,1)S(1)} copy-done((bf16[1024,512]{1,0:T(8,128)(2,1)S(1)}, bf16[1024,512]{1,0:T(8,128)(2,1)}, u32[]{:S(2)}) %copy-start.4) | copy-done | bytes 1048600
  41.2 0.9 %copy-done.7 = bf16[1040,128]{1,0:T(8,128)(2,1)S(1)} copy-done((bf16[1040,128]{1,0:T(8,128)(2,1)S(1)}, bf16[1040,128]{1,0:T(8,128)(2,1)}, u32[]{:S(2)}) %copy-start.7) | copy-done | bytes 266264
  42.1 0.7 %copy-done.8 = s32[4]{0:T(128)S(1)} copy-done((s32[4]{0:T(128)S(1)}, s32[4]{0:T(128)}, u32[]{:S(2)}) %copy-start.8) | copy-done | bytes 40
  42.8 6.9 %attend.2 = (bf16[128,512]{1,0:T(8,128)(2,1)}, bf16[128,512]{1,0:T(8,128)(2,1)}, bf16[128,512]{1,0:T(8,128)(2,1)}, bf16[128,512]{1,0:T(8,128)(2,1)}, f32[1024,512]{1,0:T(8,128)}, /*index=5*/f32[1024,512]{1,0:T(8,128)}) custom-call(s32[4]{0:T(128)S(1)} %copy-done.8, bf16[1040,128]{1,0:T(8,128)(2,1)S(1)} %copy-done.7, ...), custom_call_target="tpu_custom_call" | custom-call | flops 2415919104 | bytes 6291456 | tf_op jit(solution)/shard_map/attend/pallas_call | solution.py:273
  49.7 0.0 collective-permute-done.refs_2_
  49.7 0.0 collective-permute-done.3.refs_5_
  49.8 7.0 %attend.3 = (bf16[128,512]{1,0:T(8,128)(2,1)}, bf16[128,512]{1,0:T(8,128)(2,1)}, bf16[128,512]{1,0:T(8,128)(2,1)}, bf16[128,512]{1,0:T(8,128)(2,1)}, f32[1024,512]{1,0:T(8,128)}, /*index=5*/f32[1024,512]{1,0:T(8,128)}) custom-call(s32[4]{0:T(128)S(1)} %copy-done.8, ...), custom_call_target="tpu_custom_call", output_to_operand_aliasing={{0}: (10, {}), {1}: (11, {}), {2}: (12, {}), {3}: (13, {}),... | custom-call | flops 2415919104 | bytes 6291456 | tf_op jit(solution)/shard_map/attend/pallas_call | solution.py:273
  (13 shorter events, 0.0 us)
Async XLA Ops:
  2.7 22.9 %collective-permute-start.5 = (bf16[1040,128]{1,0:T(8,128)(2,1)}, bf16[1040,128]{1,0:T(8,128)(2,1)S(1)}, u32[]{:S(2)}, u32[]{:S(2)}) collective-permute-start(bf16[1040,128]{1,0:T(8,128)(2,1)} %get-tuple-element.15.refs_1_), channel_id=1, source_target_pairs={{0,8},{8,0},{4,12},{12,4},{1,9},{9,1},{5,13},{13,5},{2,10},{10,2},... | collective-permute-start | bytes 798728 | tf_op jit(solution)/shard_map/ppermute | solution.py:311
  6.7 24.5 %collective-permute-start.1 = (bf16[1040,128]{1,0:T(8,128)(2,1)}, bf16[1040,128]{1,0:T(8,128)(2,1)S(1)}, u32[]{:S(2)}, u32[]{:S(2)}) collective-permute-start(bf16[1040,128]{1,0:T(8,128)(2,1)} %get-tuple-element.14.refs_1_), channel_id=1, source_target_pairs={{0,8},{8,0},{4,12},{12,4},{1,9},{9,1},{5,13},{13,5},{2,10},{10,2},... | collective-permute-start | bytes 798728 | tf_op jit(solution)/shard_map/ppermute | solution.py:311
  6.8 26.7 %collective-permute-start.6 = (bf16[1040,128]{1,0:T(8,128)(2,1)}, bf16[1040,128]{1,0:T(8,128)(2,1)S(1)}, u32[]{:S(2)}, u32[]{:S(2)}) collective-permute-start(bf16[1040,128]{1,0:T(8,128)(2,1)} %get-tuple-element.15.refs_1_), channel_id=1, source_target_pairs={{4,8},{8,4},{5,9},{9,5},{6,10},{10,6},{7,11},{11,7},{20,24},{24,20... | collective-permute-start | bytes 798728 | tf_op jit(solution)/shard_map/ppermute | solution.py:311
  7.4 27.3 %collective-permute-start.4 = (bf16[1040,128]{1,0:T(8,128)(2,1)}, bf16[1040,128]{1,0:T(8,128)(2,1)S(1)}, u32[]{:S(2)}, u32[]{:S(2)}) collective-permute-start(bf16[1040,128]{1,0:T(8,128)(2,1)} %get-tuple-element.15.refs_1_), channel_id=1, source_target_pairs={{0,4},{4,0},{8,12},{12,8},{1,5},{5,1},{9,13},{13,9},{2,6},{6,2},{1... | collective-permute-start | bytes 798728 | tf_op jit(solution)/shard_map/ppermute | solution.py:311
  25.6 11.3 %collective-permute-start.7 = (bf16[1040,128]{1,0:T(8,128)(2,1)S(1)}, bf16[1040,128]{1,0:T(8,128)(2,1)S(1)}, u32[]{:S(2)}, u32[]{:S(2)}) collective-permute-start(bf16[1040,128]{1,0:T(8,128)(2,1)S(1)} %collective-permute-done.5.refs_3_), channel_id=1, source_target_pairs={{4,0},{8,12},{5,1},{9,13},{6,2},{10,14},{7,3},{11,15},{20,16},{24,... | collective-permute-start | bytes 798728 | tf_op jit(solution)/shard_map/ppermute | solution.py:311
  26.9 22.8 %collective-permute-start.2 = (bf16[1040,128]{1,0:T(8,128)(2,1)}, bf16[1040,128]{1,0:T(8,128)(2,1)S(1)}, u32[]{:S(2)}, u32[]{:S(2)}) collective-permute-start(bf16[1040,128]{1,0:T(8,128)(2,1)} %get-tuple-element.14.refs_1_), channel_id=1, source_target_pairs={{4,8},{8,4},{5,9},{9,5},{6,10},{10,6},{7,11},{11,7},{20,24},{24,20... | collective-permute-start | bytes 798728 | tf_op jit(solution)/shard_map/ppermute | solution.py:311
  31.3 18.4 %collective-permute-start = (bf16[1040,128]{1,0:T(8,128)(2,1)}, bf16[1040,128]{1,0:T(8,128)(2,1)S(1)}, u32[]{:S(2)}, u32[]{:S(2)}) collective-permute-start(bf16[1040,128]{1,0:T(8,128)(2,1)} %get-tuple-element.14.refs_1_), channel_id=1, source_target_pairs={{0,4},{4,0},{8,12},{12,8},{1,5},{5,1},{9,13},{13,9},{2,6},{6,2},{1... | collective-permute-start | bytes 798728 | tf_op jit(solution)/shard_map/ppermute | solution.py:311
  33.4 16.3 %collective-permute-start.3 = (bf16[1040,128]{1,0:T(8,128)(2,1)S(1)}, bf16[1040,128]{1,0:T(8,128)(2,1)S(1)}, u32[]{:S(2)}, u32[]{:S(2)}) collective-permute-start(bf16[1040,128]{1,0:T(8,128)(2,1)S(1)} %collective-permute-done.1.refs_3_), channel_id=1, source_target_pairs={{4,0},{8,12},{5,1},{9,13},{6,2},{10,14},{7,3},{11,15},{20,16},{24,... | collective-permute-start | bytes 798728 | tf_op jit(solution)/shard_map/ppermute | solution.py:311
  36.9 0.9 %copy-start = (bf16[128,512]{1,0:T(8,128)(2,1)S(1)}, bf16[128,512]{1,0:T(8,128)(2,1)}, u32[]{:S(2)}) copy-start(bf16[128,512]{1,0:T(8,128)(2,1)} %refs_6_.3) | copy-start | bytes 393220
  37.8 0.9 %copy-start.1 = (bf16[128,512]{1,0:T(8,128)(2,1)S(1)}, bf16[128,512]{1,0:T(8,128)(2,1)}, u32[]{:S(2)}) copy-start(bf16[128,512]{1,0:T(8,128)(2,1)} %refs_7_.3) | copy-start | bytes 393220
  38.7 1.2 %copy-start.2 = (bf16[1024,512]{1,0:T(8,128)(2,1)S(1)}, bf16[1024,512]{1,0:T(8,128)(2,1)}, u32[]{:S(2)}) copy-start(bf16[1024,512]{1,0:T(8,128)(2,1)} %refs_8_.3) | copy-start | bytes 3145732
  40.0 1.2 %copy-start.4 = (bf16[1024,512]{1,0:T(8,128)(2,1)S(1)}, bf16[1024,512]{1,0:T(8,128)(2,1)}, u32[]{:S(2)}) copy-start(bf16[1024,512]{1,0:T(8,128)(2,1)} %refs_9_.3) | copy-start | bytes 3145732
  41.2 1.0 %copy-start.7 = (bf16[1040,128]{1,0:T(8,128)(2,1)S(1)}, bf16[1040,128]{1,0:T(8,128)(2,1)}, u32[]{:S(2)}) copy-start(bf16[1040,128]{1,0:T(8,128)(2,1)} %get-tuple-element.15.refs_1_) | copy-start | bytes 798724
  42.1 0.7 %copy-start.8 = (s32[4]{0:T(128)S(1)}, s32[4]{0:T(128)}, u32[]{:S(2)}) copy-start(s32[4]{0:T(128)} %refs_0_.3) | copy-start | bytes 52
  42.8 6.9 %copy-start.3 = (bf16[1024,512]{1,0:T(8,128)(2,1)S(1)}, bf16[1024,512]{1,0:T(8,128)(2,1)}, u32[]{:S(2)}) copy-start(bf16[1024,512]{1,0:T(8,128)(2,1)} %refs_8_.3) | copy-start | bytes 3145732
  42.8 7.0 %copy-start.5 = (bf16[1024,512]{1,0:T(8,128)(2,1)S(1)}, bf16[1024,512]{1,0:T(8,128)(2,1)}, u32[]{:S(2)}) copy-start(bf16[1024,512]{1,0:T(8,128)(2,1)} %refs_9_.3) | copy-start | bytes 3145732
  42.8 7.0 %copy-start.6 = (bf16[1040,128]{1,0:T(8,128)(2,1)S(1)}, bf16[1040,128]{1,0:T(8,128)(2,1)}, u32[]{:S(2)}) copy-start(bf16[1040,128]{1,0:T(8,128)(2,1)} %get-tuple-element.14.refs_1_) | copy-start | bytes 798724

commit v3 on v2

--- a/solution.py
+++ b/solution.py
@@ -59,10 +59,10 @@
     )(queries, keys, values, grad_out, segment.reshape(1, length))
 
 
-def attend_kernel(n, length, count, routed, *refs):
+def attend_kernel(n, length, count, *refs):
     refs = list(refs)
     len_ref = refs.pop(0)
-    pieces = [refs.pop(0) for _ in range(5 if routed else 2)]
+    gathered = refs.pop(0)
     q_raw, k_raw, tk_ref, tv_ref = refs[:4]
     out_ref, gq_ref, gk_ref, gv_ref, gtk_ref, gtv_ref = refs[-18:-12]
     held, qx, kx, vx, gx, e_ref, dp_ref, dk_ref, dv_ref, dq_ref, att_ref, sems = refs[-12:]
@@ -81,37 +81,14 @@
     @pl.when(head == 0)
     def _():
         me = lax.axis_index("ctx")
-        if routed:
-            own, near, skip, far, last = pieces
-            end = (me == 0) | (me == 3)
-
-            def copy(source, slot):
-                return pltpu.make_async_copy(source, held.at[slot], sems.at[slot])
-
-            copy(own, 0).start()
-            copy(near, 1).start()
-            copy(skip, 2).start()
-
-            @pl.when(end)
-            def _():
-                copy(last, 3).start()
-
-            @pl.when(jnp.logical_not(end))
-            def _():
-                copy(far, 3).start()
-
-            for slot in range(4):
-                copy(own, slot).wait()
-        else:
-            own, gathered = pieces
-
-            def fetch(s, _):
-                source = lax.rem(me + s, n)
-                pltpu.make_async_copy(gathered.at[source], held.at[s], sems.at[0]).start()
-                pltpu.make_async_copy(gathered.at[source], held.at[s], sems.at[0]).wait()
-                return 0
-
-            lax.fori_loop(0, n, fetch, 0)
+        def fetch(s, _):
+            source = lax.rem(me + s, n)
+            copy = pltpu.make_async_copy(gathered.at[source], held.at[s], sems.at[0])
+            copy.start()
+            copy.wait()
+            return 0
+
+        lax.fori_loop(0, n, fetch, 0)
 
         lane = lax.broadcasted_iota(jnp.int32, (length, HD), 1)
         sub = lax.broadcasted_iota(jnp.int32, (HD, length), 0).astype(F32)
@@ -245,9 +222,8 @@
     gtk_ref[...] = norm_back(tk_ref[...].astype(F32), gtk_ref[...] * scale)
 
 
-def attend(n, chunk, text_len, pieces, queries, keys, text_keys, text_values, before):
+def attend(n, chunk, text_len, gathered, queries, keys, text_keys, text_values, before):
     first, count = chunk
-    routed = len(pieces) > 2
     length, width = queries.shape
     text_rows = text_keys.shape[0]
     video = n * length
@@ -260,18 +236,18 @@
 
     in_specs = (
         [pl.BlockSpec(memory_space=pltpu.SMEM)]
-        + [anywhere] * len(pieces)
+        + [anywhere]
         + [column(length)] * 2
         + [column(text_rows)] * 2
         + [anywhere] * len(before)
     )
     out_rows = [length] * 4 + [text_rows] * 2
     out_types = [BF16] * 4 + [F32] * 2
-    operands = [text_len, *pieces, queries, keys, text_keys, text_values, *before]
+    operands = [text_len, gathered, queries, keys, text_keys, text_values, *before]
     base = len(operands) - len(before)
     pairs = count * total * rows_of * (video // rows_of)
     return pl.pallas_call(
-        functools.partial(attend_kernel, n, length, count, routed),
+        functools.partial(attend_kernel, n, length, count),
         grid=(count,),
         in_specs=in_specs,
         out_specs=[column(rows) for rows in out_rows],
@@ -290,14 +266,262 @@
             pltpu.VMEM((length, HD), F32),
             pltpu.VMEM((length, HD), F32),
             pltpu.VMEM((length, HD), F32),
-            pltpu.SemaphoreType.DMA((4,)),
+            pltpu.SemaphoreType.DMA((1,)),
         ],
         input_output_aliases={base + i: i for i in range(len(before))},
-        compiler_params=pltpu.CompilerParams(vmem_limit_bytes=(16 if routed else 56) * 1024 * 1024),
+        compiler_params=pltpu.CompilerParams(vmem_limit_bytes=56 * 1024 * 1024),
         cost_estimate=pl.CostEstimate(
             flops=12 * pairs * HD, bytes_accessed=count * 3 * 1024 * 1024, transcendentals=pairs
         ),
         name="attend",
+    )(*operands)
+
+
+def text_kernel(len_ref, tk_ref, tv_ref, kt_ref, vt_ref):
+    text_rows, width = tk_ref.shape
+    clips = len_ref.shape[0]
+    per_clip = text_rows // clips
+    lane = lax.broadcasted_iota(jnp.int32, (per_clip, HD), 1)
+    place = lax.broadcasted_iota(jnp.int32, (per_clip, HD), 0)
+    for c in range(clips):
+        other = jnp.where((lane < clips) & (lane != c), -FAR, 0.0)
+        dead = jnp.where((lane == clips) & (place >= len_ref[c]), -FAR, 0.0)
+        mask = (other + dead).astype(BF16)
+        rows = pl.ds(c * per_clip, per_clip)
+        for h in range(width // HD):
+            to = pl.ds(h * text_rows + c * per_clip, per_clip)
+            x = tk_ref[rows, pl.ds(h * HD, HD)].astype(F32)
+            kt_ref[to, :HD] = (x * inverse_rms(x)).astype(BF16)
+            kt_ref[to, HD:] = mask
+    vt_ref[...] = tv_ref[...]
+
+
+def prepare_text(text_len, text_keys, text_values):
+    text_rows, width = text_keys.shape
+    whole = pl.BlockSpec(memory_space=pltpu.VMEM)
+    return pl.pallas_call(
+        text_kernel,
+        in_specs=[pl.BlockSpec(memory_space=pltpu.SMEM), whole, whole],
+        out_specs=[whole, whole],
+        out_shape=[
+            jax.ShapeDtypeStruct((width // HD * text_rows, 2 * HD), BF16),
+            jax.ShapeDtypeStruct((text_rows, width), BF16),
+        ],
+        compiler_params=pltpu.CompilerParams(vmem_limit_bytes=12 * 1024 * 1024),
+        cost_estimate=pl.CostEstimate(
+            flops=8 * text_rows * width, bytes_accessed=6 * text_rows * width, transcendentals=0
+        ),
+        name="prepare_text",
+    )(text_len, text_keys, text_values)
+
+
+def line_kernel(first, count, clips, *refs):
+    own, near, skip, far, last, kt, vt, q_any, k_any, t_any = refs[:10]
+    out, gq, gk, gv, gtk, gtv = refs[-26:-20]
+    (pick, qx, kx, vx, gx, qs, gs, e_row, e_col, e_text, d_row, d_col, d_text) = refs[-20:-7]
+    raw_q, raw_k, raw_t, staged, staged_text, in_sems, out_sems = refs[-7:]
+    length = raw_q.shape[1]
+    text_rows = vt.shape[0]
+    per_clip = text_rows // clips
+    half = 2 * length
+    video = 4 * length
+    scale = 1.0 / math.sqrt(HD)
+    exponent = scale * math.log2(math.e)
+    seg_at = 4 * count * length
+
+    fetches = []
+    for b in range(count):
+        cols = pl.ds((first + b) * HD, HD)
+        for a, (source, target) in enumerate(((q_any, raw_q), (k_any, raw_k), (t_any, raw_t))):
+            copy = pltpu.make_async_copy(source.at[:, cols], target.at[b], in_sems.at[3 * b + a])
+            copy.start()
+            fetches.append(copy)
+
+    me = lax.axis_index("ctx")
+    end = (me == 0) | (me == 3)
+
+    @pl.when(end)
+    def _():
+        pick[...] = last[...]
+
+    @pl.when(jnp.logical_not(end))
+    def _():
+        pick[...] = far[...]
+
+    pieces = (own, near, skip, pick)
+    lane = lax.broadcasted_iota(jnp.int32, (length, HD), 1)
+    sub = lax.broadcasted_iota(jnp.int32, (HD, length), 0).astype(F32)
+    tops = []
+    for s, piece in enumerate(pieces):
+        seg = piece[pl.ds(seg_at, SEG_ROWS), :].astype(F32)[0:1, :]
+        tops.append(jnp.max(seg))
+        onehot = jnp.where(jnp.broadcast_to(seg, (HD, length)) == sub, 1.0, 0.0).T
+        rows = pl.ds(s * length, length)
+        qx[rows, HD:] = jnp.where(lane == clips, 1.0, onehot).astype(BF16)
+        kx[rows, HD:] = jnp.where(lane < clips, (onehot - 1.0) * FAR, 0.0).astype(BF16)
+    flipped = me >= 2
+    middle = jnp.where(
+        flipped, jnp.maximum(tops[2], tops[3]), jnp.maximum(tops[0], tops[1])
+    ).astype(jnp.int32)
+
+    pairs = []
+    for k in range(clips + 1):
+        second = k > middle
+        clip = jnp.where(second, k - 1, k)
+        here = second == flipped
+        at = pl.multiple_of(jnp.where(here, 0, half), half)
+        pairs.append((clip, here, pl.ds(at, half)))
+
+    def split_sum(x):
+        return jnp.sum(x.reshape(x.shape[0] // 8, 8, x.shape[1]), axis=0)
+
+    mine = slice(0, length)
+    stores = []
+
+    def put(source, target, cols, rows=None):
+        to = target.at[:, cols] if rows is None else target.at[rows, cols]
+        copy = pltpu.make_async_copy(source, to, out_sems.at[len(stores)])
+        copy.start()
+        stores.append(copy)
+
+    for b in range(count):
+        cols = pl.ds((first + b) * HD, HD)
+        for s, piece in enumerate(pieces):
+            rows = pl.ds(s * length, length)
+            for a, (ref, to) in enumerate(((qx, pl.ds(0, HD)), (kx, pl.ds(0, HD)), (vx, pl.ds(0, HD)), (gx, pl.ds(0, HD)))):
+                ref[rows, to] = piece[pl.ds((4 * b + a) * length, length), :]
+
+        norm = [jnp.zeros((8, half), F32)] * 2
+        mean = [jnp.zeros((8, half), F32)] * 2
+        for j in range(2):
+            for i in range(2):
+                keys, rows = pl.ds(j * half, half), pl.ds(i * half, half)
+                e = jnp.exp2(dot(kx[keys, :], qx[rows, :], (1, 1)) * exponent)
+                dp = dot(vx[keys, :], gx[rows, :], (1, 1))
+                norm[i] = norm[i] + split_sum(e)
+                mean[i] = mean[i] + split_sum(e * dp)
+                if j == 0:
+                    e_row[:, rows] = e[mine, :].astype(BF16)
+                    d_row[:, rows] = dp[mine, :]
+                if i == 0:
+                    e_col[keys, :] = e[:, mine].astype(BF16)
+                    d_col[keys, :] = dp[:, mine]
+        for k, (clip, here, rows) in enumerate(pairs):
+            keys = pl.ds(pl.multiple_of((first + b) * text_rows + clip * per_clip, per_clip), per_clip)
+            vals = pl.ds(pl.multiple_of(clip * per_clip, per_clip), per_clip)
+            e = jnp.exp2(dot(kt[keys, :], qx[rows, :], (1, 1)) * exponent)
+            dp = dot(vt[vals, cols], gx[rows, :], (1, 1))
+            e_text[k] = e.astype(BF16)
+            d_text[k] = dp
+            for sums, part in ((norm, split_sum(e)), (mean, split_sum(e * dp))):
+                sums[0] = sums[0] + jnp.where(here, part, 0.0)
+                sums[1] = sums[1] + jnp.where(here, 0.0, part)
+
+        inv = [1.0 / jnp.sum(x, axis=0, keepdims=True) for x in norm]
+        inner = [jnp.sum(x, axis=0, keepdims=True) * y for x, y in zip(mean, inv)]
+        turned = []
+        for s in range(4):
+            part = inv[s // 2][:, (s % 2) * length : (s % 2 + 1) * length]
+            turned.append(jnp.broadcast_to(part, (HD, length)).T)
+            rows = pl.ds(s * length, length)
+            qs[rows, :] = (qx[rows, :HD].astype(F32) * (turned[s] * scale)).astype(BF16)
+            gs[rows, :] = (gx[rows, :].astype(F32) * turned[s]).astype(BF16)
+
+        att = jnp.zeros((length, HD), F32)
+        dq = jnp.zeros((length, HD), F32)
+        fetches[3 * b + 2].wait()
+        before = None
+        for k, (clip, here, rows) in enumerate(pairs):
+            keys = pl.ds(pl.multiple_of((first + b) * text_rows + clip * per_clip, per_clip), per_clip)
+            vals = pl.ds(pl.multiple_of(clip * per_clip, per_clip), per_clip)
+            eb = e_text[k]
+            away = jnp.where(here, inner[0], inner[1])
+            ds = (eb.astype(F32) * (d_text[k] - away)).astype(BF16)
+            dk = dot(ds, qs[rows, :], (1, 0))
+            dv = dot(eb, gs[rows, :], (1, 0))
+            att = att + jnp.where(here, dot(eb[:, mine], vt[vals, cols], (0, 0)), 0.0)
+            dq = dq + jnp.where(here, dot(ds[:, mine], kt[keys, :HD], (0, 0)), 0.0)
+            if before is not None:
+                c = k - 1
+                low, high = c <= middle, c >= middle
+                to = pl.ds(c * per_clip, per_clip)
+                total = jnp.where(low, before[0], 0.0) + jnp.where(high, dk, 0.0)
+                staged_text[b, 0, to, :] = norm_back(raw_t[b, to, :].astype(F32), total)
+                staged_text[b, 1, to, :] = jnp.where(low, before[1], 0.0) + jnp.where(high, dv, 0.0)
+                put(staged_text.at[b, 0, to], gtk, cols, to)
+                put(staged_text.at[b, 1, to], gtv, cols, to)
+            before = (dk, dv)
+
+        eb = e_row[...]
+        inner_all = jnp.concatenate(inner, axis=1)
+        ds = (eb.astype(F32) * (d_row[...] - inner_all)).astype(BF16)
+        dk = dot(ds, qs[...], (1, 0))
+        dv = dot(eb, gs[...], (1, 0))
+        eb = e_col[...]
+        ds = (eb.astype(F32) * (d_col[...] - inner[0][:, mine])).astype(BF16)
+        att = att + dot(eb, vx[...], (0, 0))
+        dq = dq + dot(ds, kx[:, :HD], (0, 0))
+        fetches[3 * b].wait()
+        fetches[3 * b + 1].wait()
+        staged[b, 0] = (att * turned[0]).astype(BF16)
+        staged[b, 1] = norm_back(raw_q[b].astype(F32), dq * (turned[0] * scale)).astype(BF16)
+        staged[b, 2] = norm_back(raw_k[b].astype(F32), dk).astype(BF16)
+        staged[b, 3] = dv.astype(BF16)
+        for a, target in enumerate((out, gq, gk, gv)):
+            put(staged.at[b, a], target, cols)
+    for copy in stores:
+        copy.wait()
+
+
+def attend_line(chunk, clips, pieces, text, queries, keys, text_keys, before):
+    first, count = chunk
+    length, width = queries.shape
+    text_rows = text_keys.shape[0]
+    per_clip = text_rows // clips
+    half, video = 2 * length, 4 * length
+    anywhere = pl.BlockSpec(memory_space=pl.ANY)
+    remote = pl.BlockSpec(memory_space=pltpu.HBM)
+    held = pl.BlockSpec(memory_space=pltpu.VMEM)
+    out_rows = [length] * 4 + [text_rows] * 2
+    out_types = [BF16] * 4 + [F32] * 2
+    operands = [*pieces, *text, queries, keys, text_keys, *before]
+    base = len(operands) - len(before)
+    work = count * video * (video + text_rows)
+    return pl.pallas_call(
+        functools.partial(line_kernel, first, count, clips),
+        in_specs=[held] * 7 + [remote] * 3 + [remote] * len(before),
+        out_specs=[remote] * 6,
+        out_shape=[
+            jax.ShapeDtypeStruct((rows, width), dtype) for rows, dtype in zip(out_rows, out_types)
+        ],
+        scratch_shapes=[
+            pltpu.VMEM((4 * count * length + SEG_ROWS, HD), BF16),
+            pltpu.VMEM((video, 2 * HD), BF16),
+            pltpu.VMEM((video, 2 * HD), BF16),
+            pltpu.VMEM((video, HD), BF16),
+            pltpu.VMEM((video, HD), BF16),
+            pltpu.VMEM((video, HD), BF16),
+            pltpu.VMEM((video, HD), BF16),
+            pltpu.VMEM((length, video), BF16),
+            pltpu.VMEM((video, length), BF16),
+            pltpu.VMEM((clips + 1, per_clip, half), BF16),
+            pltpu.VMEM((length, video), F32),
+            pltpu.VMEM((video, length), F32),
+            pltpu.VMEM((clips + 1, per_clip, half), F32),
+            pltpu.VMEM((count, length, HD), BF16),
+            pltpu.VMEM((count, length, HD), BF16),
+            pltpu.VMEM((count, text_rows, HD), BF16),
+            pltpu.VMEM((count, 4, length, HD), BF16),
+            pltpu.VMEM((count, 2, text_rows, HD), F32),
+            pltpu.SemaphoreType.DMA((3 * count,)),
+            pltpu.SemaphoreType.DMA((count * (2 * clips + 4),)),
+        ],
+        input_output_aliases={base + i: i for i in range(len(before))},
+        compiler_params=pltpu.CompilerParams(vmem_limit_bytes=16 * 1024 * 1024),
+        cost_estimate=pl.CostEstimate(
+            flops=12 * work * HD, bytes_accessed=count * 2 * 1024 * 1024, transcendentals=work
+        ),
+        name="attend_line",
     )(*operands)
 
 
@@ -322,11 +546,19 @@
             far = send(x, middle)
             last = send(skip, outward)
             pieces.append((x, near, skip, far, last))
-    else:
-        pieces = [(x, lax.all_gather(x, "ctx", axis=0)) for x in payloads]
+        text = prepare_text(text_len, text_keys, text_values)
+        outs = ()
+        for chunk, piece in zip(chunks, pieces):
+            outs = attend_line(
+                chunk, text_len.shape[0], piece, text, queries, keys, text_keys, outs
+            )
+        return tuple(outs)
     outs = ()
-    for chunk, piece in zip(chunks, pieces):
-        outs = attend(n, chunk, text_len, piece, queries, keys, text_keys, text_values, outs)
+    for chunk, x in zip(chunks, payloads):
+        gathered = lax.all_gather(x, "ctx", axis=0)
+        outs = attend(
+            n, chunk, text_len, gathered, queries, keys, text_keys, text_values, outs
+        )
     return tuple(outs)
 
 

time: 57.1 us -> 53.3 us (0.933)
  local copies, waits for them, and re-layouts: 5.87 us -> 3.12 us
  Pallas kernels: 15.9 us -> 14.2 us
  waiting for transfers between devices: 19.3 us -> 20 us
    unnamed x18 -> x16, local copies, waits for them, and re-layouts: 5.87 us -> 3.12 us
    pallas_call x2 -> x3, Pallas kernels: 13.9 us -> 12.1 us  [the longest x2 10.7 us: attend_line(): pl.pallas_call(functools.partial(line_kernel, first, count, clips), in_sp...]
    ppermute x8, waiting for transfers between devices: 19.3 us -> 20 us  [send(): return lax.ppermute(x, 'ctx', pairs)]
  transfers between devices with their start and end apart: 8 -> 8, of which waited for: 3 -> 3; matrix products, arithmetic and copies ran while one was open for 0% -> 0% of each run, Pallas kernels for 12% -> 13%
where the time goes in v3:
time: 53.3 us; the launch traced here: 53 us
  waiting for transfers between devices  20 us (38%)
  starting transfers between devices  14.9 us (28%)
  Pallas kernels  14.2 us (27%)
  local copies, waits for them, and re-layouts  3.12 us (6%)
  between operations  0.78 us (1%)
    ppermute x8, waiting for transfers between devices, send(): return lax.ppermute(x, 'ctx', pairs)  20 us
    ppermute x8, starting transfers between devices, send(): return lax.ppermute(x, 'ctx', pairs)  14.9 us
    pallas_call x2, Pallas kernels, attend_line(): pl.pallas_call(functools.partial(line_kernel, first, count, clips), in_sp...  10.7 us
    unnamed x16, local copies, waits for them, and re-layouts  3.12 us
    pallas_call x1, Pallas kernels, pack(): pl.pallas_call(functools.partial(pack_kernel, chunks), out_shape=[jax.Sha...  2.11 us
    pallas_call x1, Pallas kernels, prepare_text(): pl.pallas_call(text_kernel, in_specs=[pl.BlockSpec(memory_space=pltpu.SME...  1.38 us
  transfers between devices with their start and end apart: 8, of which 3 were waited for; matrix products, arithmetic and copies ran while one was open for 0% of the time, Pallas kernels for 13%

profile of v3, /device:TPU:0, one launch (start us, length us, event | category | flops | bytes accessed | tf_op | source)
XLA Modules:
  0.0 53.0 jit_solution(15271347682771401445)
XLA Ops:
  0.7 2.1 %pack.1 = (bf16[1040,128]{1,0:T(8,128)(2,1)}, bf16[1040,128]{1,0:T(8,128)(2,1)}) custom-call(bf16[128,512]{1,0:T(8,128)(2,1)} %refs_7_.3, bf16[128,512]{1,0:T(8,128)(2,1)} %refs_8_.3, bf16[128,512]{1,0:T(8,128)(2,1)} %v_ref.1, bf16[128,512]{1,0:T(8,128)(2,1)} %g_ref.1, s32[1,128]{1,0:T(1,128)} %bitcast.1), custom_call_target="tpu_custom_call" | custom-call | tf_op jit(solution)/shard_map/pack/pallas_call | solution.py:53
  2.8 4.0 %collective-permute-start.5 = (bf16[1040,128]{1,0:T(8,128)(2,1)}, bf16[1040,128]{1,0:T(8,128)(2,1)S(1)}, u32[]{:S(2)}, u32[]{:S(2)}) collective-permute-start(bf16[1040,128]{1,0:T(8,128)(2,1)} %get-tuple-element.19.refs_0_), channel_id=1, source_target_pairs={{0,8},{8,0},{4,12},{12,4},{1,9},{9,1},{5,13},{13,5},{2,10},{10,2},... | collective-permute-start | bytes 798728 | tf_op jit(solution)/shard_map/ppermute | solution.py:535
  6.8 0.0 collective-permute-start.1
  6.8 0.7 %collective-permute-start.6 = (bf16[1040,128]{1,0:T(8,128)(2,1)}, bf16[1040,128]{1,0:T(8,128)(2,1)S(1)}, u32[]{:S(2)}, u32[]{:S(2)}) collective-permute-start(bf16[1040,128]{1,0:T(8,128)(2,1)} %get-tuple-element.19.refs_0_), channel_id=1, source_target_pairs={{4,8},{8,4},{5,9},{9,5},{6,10},{10,6},{7,11},{11,7},{20,24},{24,20... | collective-permute-start | bytes 798728 | tf_op jit(solution)/shard_map/ppermute | solution.py:535
  7.5 4.8 %collective-permute-start.4 = (bf16[1040,128]{1,0:T(8,128)(2,1)}, bf16[1040,128]{1,0:T(8,128)(2,1)S(1)}, u32[]{:S(2)}, u32[]{:S(2)}) collective-permute-start(bf16[1040,128]{1,0:T(8,128)(2,1)} %get-tuple-element.19.refs_0_), channel_id=1, source_target_pairs={{0,4},{4,0},{8,12},{12,8},{1,5},{5,1},{9,13},{13,9},{2,6},{6,2},{1... | collective-permute-start | bytes 798728 | tf_op jit(solution)/shard_map/ppermute | solution.py:535
  12.3 13.4 %collective-permute-done.5.refs_2_ = bf16[1040,128]{1,0:T(8,128)(2,1)S(1)} collective-permute-done((bf16[1040,128]{1,0:T(8,128)(2,1)}, bf16[1040,128]{1,0:T(8,128)(2,1)S(1)}, u32[]{:S(2)}, u32[]{:S(2)}) %collective-permute-start.5) | collective-permute-done | bytes 266272 | tf_op jit(solution)/shard_map/ppermute | solution.py:535
  25.6 1.3 %collective-permute-start.7 = (bf16[1040,128]{1,0:T(8,128)(2,1)S(1)}, bf16[1040,128]{1,0:T(8,128)(2,1)S(1)}, u32[]{:S(2)}, u32[]{:S(2)}) collective-permute-start(bf16[1040,128]{1,0:T(8,128)(2,1)S(1)} %collective-permute-done.5.refs_2_), channel_id=1, source_target_pairs={{4,0},{8,12},{5,1},{9,13},{6,2},{10,14},{7,3},{11,15},{20,16},{24,... | collective-permute-start | bytes 798728 | tf_op jit(solution)/shard_map/ppermute | solution.py:535
  26.9 0.7 %collective-permute-start.2 = (bf16[1040,128]{1,0:T(8,128)(2,1)}, bf16[1040,128]{1,0:T(8,128)(2,1)S(1)}, u32[]{:S(2)}, u32[]{:S(2)}) collective-permute-start(bf16[1040,128]{1,0:T(8,128)(2,1)} %get-tuple-element.16.refs_0_), channel_id=1, source_target_pairs={{4,8},{8,4},{5,9},{9,5},{6,10},{10,6},{7,11},{11,7},{20,24},{24,20... | collective-permute-start | bytes 798728 | tf_op jit(solution)/shard_map/ppermute | solution.py:535
  27.6 3.7 %collective-permute-done.1.refs_2_ = bf16[1040,128]{1,0:T(8,128)(2,1)S(1)} collective-permute-done((bf16[1040,128]{1,0:T(8,128)(2,1)}, bf16[1040,128]{1,0:T(8,128)(2,1)S(1)}, u32[]{:S(2)}, u32[]{:S(2)}) %collective-permute-start.1) | collective-permute-done | bytes 266272 | tf_op jit(solution)/shard_map/ppermute | solution.py:535
  31.3 2.1 %collective-permute-start = (bf16[1040,128]{1,0:T(8,128)(2,1)}, bf16[1040,128]{1,0:T(8,128)(2,1)S(1)}, u32[]{:S(2)}, u32[]{:S(2)}) collective-permute-start(bf16[1040,128]{1,0:T(8,128)(2,1)} %get-tuple-element.16.refs_0_), channel_id=1, source_target_pairs={{0,4},{4,0},{8,12},{12,8},{1,5},{5,1},{9,13},{13,9},{2,6},{6,2},{1... | collective-permute-start | bytes 798728 | tf_op jit(solution)/shard_map/ppermute | solution.py:535
  33.5 0.0 collective-permute-done.6.refs_3_
  33.5 1.3 %collective-permute-start.3 = (bf16[1040,128]{1,0:T(8,128)(2,1)S(1)}, bf16[1040,128]{1,0:T(8,128)(2,1)S(1)}, u32[]{:S(2)}, u32[]{:S(2)}) collective-permute-start(bf16[1040,128]{1,0:T(8,128)(2,1)S(1)} %collective-permute-done.1.refs_2_), channel_id=1, source_target_pairs={{4,0},{8,12},{5,1},{9,13},{6,2},{10,14},{7,3},{11,15},{20,16},{24,... | collective-permute-start | bytes 798728 | tf_op jit(solution)/shard_map/ppermute | solution.py:535
  34.8 0.0 copy-start
  34.8 1.2 %copy-done = bf16[1024,512]{1,0:T(8,128)(2,1)S(1)} copy-done((bf16[1024,512]{1,0:T(8,128)(2,1)S(1)}, bf16[1024,512]{1,0:T(8,128)(2,1)}, u32[]{:S(2)}) %copy-start) | copy-done | bytes 1048600
  36.0 1.2 %copy-done.2 = bf16[1024,512]{1,0:T(8,128)(2,1)S(1)} copy-done((bf16[1024,512]{1,0:T(8,128)(2,1)S(1)}, bf16[1024,512]{1,0:T(8,128)(2,1)}, u32[]{:S(2)}) %copy-start.2) | copy-done | bytes 1048600
  37.2 0.7 %copy-done.6 = s32[4]{0:T(128)S(1)} copy-done((s32[4]{0:T(128)S(1)}, s32[4]{0:T(128)}, u32[]{:S(2)}) %copy-start.6) | copy-done | bytes 40
  37.9 1.4 %prepare_text.1 = (bf16[4096,256]{1,0:T(8,128)(2,1)S(1)}, bf16[1024,512]{1,0:T(8,128)(2,1)S(1)}) custom-call(s32[4]{0:T(128)S(1)} %copy-done.6, bf16[1024,512]{1,0:T(8,128)(2,1)S(1)} %copy-done, bf16[1024,512]{1,0:T(8,128)(2,1)S(1)} %copy-done.2), custom_call_target="tpu_custom_call" | custom-call | flops 4194304 | bytes 3145728 | tf_op jit(solution)/shard_map/prepare_text/pallas_call | solution.py:302
  39.3 0.0 collective-permute-done.4.refs_1_
  39.3 0.0 collective-permute-done.7.refs_4_
  39.4 5.4 %attend_line.2 = (bf16[128,512]{1,0:T(8,128)(2,1)}, bf16[128,512]{1,0:T(8,128)(2,1)}, bf16[128,512]{1,0:T(8,128)(2,1)}, bf16[128,512]{1,0:T(8,128)(2,1)}, f32[1024,512]{1,0:T(8,128)}, /*index=5*/f32[1024,512]{1,0:T(8,128)}) custom-call(bf16[1040,128]{1,0:T(8,128)(2,1)S(1)} %copy-done.7, bf16[1040,128]{1,0:T(8,128)(2,1)S(1)} %collective-permute-done.4.refs_1_, ...), custom_call_target="tpu_custom_call" | custom-call | flops 2415919104 | bytes 4194304 | tf_op jit(solution)/shard_map/attend_line/pallas_call | solution.py:490
  44.7 0.0 collective-permute-done.2.refs_3_
  44.7 0.0 collective-permute-done.refs_1_
  44.7 2.9 %collective-permute-done.3.refs_4_ = bf16[1040,128]{1,0:T(8,128)(2,1)S(1)} collective-permute-done((bf16[1040,128]{1,0:T(8,128)(2,1)S(1)}, bf16[1040,128]{1,0:T(8,128)(2,1)S(1)}, u32[]{:S(2)}, u32[]{:S(2)}) %collective-permute-start.3) | collective-permute-done | bytes 266272 | tf_op jit(solution)/shard_map/ppermute | solution.py:535
  47.6 5.3 %attend_line.3 = (bf16[128,512]{1,0:T(8,128)(2,1)}, bf16[128,512]{1,0:T(8,128)(2,1)}, bf16[128,512]{1,0:T(8,128)(2,1)}, bf16[128,512]{1,0:T(8,128)(2,1)}, f32[1024,512]{1,0:T(8,128)}, /*index=5*/f32[1024,512]{1,0:T(8,128)}) custom-call(bf16[1040,128]{1,0:T(8,128)(2,1)S(1)} %copy-done.5, ...), custom_call_target="tpu_custom_call", output_to_operand_aliasing={{0}: (10, {}), {1}: (11, {}), {2}: (12, {}), {3}: (13, {}),... | custom-call | flops 2415919104 | bytes 4194304 | tf_op jit(solution)/shard_map/attend_line/pallas_call | solution.py:490
  (12 shorter events, 0.0 us)
Async XLA Ops:
  0.6 38.7 %copy-start.4 = (bf16[128,512]{1,0:T(8,128)(2,1)S(1)}, bf16[128,512]{1,0:T(8,128)(2,1)}, u32[]{:S(2)}) copy-start(bf16[128,512]{1,0:T(8,128)(2,1)} %refs_8_.3) | copy-start | bytes 393220
  0.6 38.7 %copy-start.3 = (bf16[128,512]{1,0:T(8,128)(2,1)S(1)}, bf16[128,512]{1,0:T(8,128)(2,1)}, u32[]{:S(2)}) copy-start(bf16[128,512]{1,0:T(8,128)(2,1)} %refs_7_.3) | copy-start | bytes 393220
  2.8 22.9 %collective-permute-start.5 = (bf16[1040,128]{1,0:T(8,128)(2,1)}, bf16[1040,128]{1,0:T(8,128)(2,1)S(1)}, u32[]{:S(2)}, u32[]{:S(2)}) collective-permute-start(bf16[1040,128]{1,0:T(8,128)(2,1)} %get-tuple-element.19.refs_0_), channel_id=1, source_target_pairs={{0,8},{8,0},{4,12},{12,4},{1,9},{9,1},{5,13},{13,5},{2,10},{10,2},... | collective-permute-start | bytes 798728 | tf_op jit(solution)/shard_map/ppermute | solution.py:535
  6.8 24.5 %collective-permute-start.1 = (bf16[1040,128]{1,0:T(8,128)(2,1)}, bf16[1040,128]{1,0:T(8,128)(2,1)S(1)}, u32[]{:S(2)}, u32[]{:S(2)}) collective-permute-start(bf16[1040,128]{1,0:T(8,128)(2,1)} %get-tuple-element.16.refs_0_), channel_id=1, source_target_pairs={{0,8},{8,0},{4,12},{12,4},{1,9},{9,1},{5,13},{13,5},{2,10},{10,2},... | collective-permute-start | bytes 798728 | tf_op jit(solution)/shard_map/ppermute | solution.py:535
  6.8 26.7 %collective-permute-start.6 = (bf16[1040,128]{1,0:T(8,128)(2,1)}, bf16[1040,128]{1,0:T(8,128)(2,1)S(1)}, u32[]{:S(2)}, u32[]{:S(2)}) collective-permute-start(bf16[1040,128]{1,0:T(8,128)(2,1)} %get-tuple-element.19.refs_0_), channel_id=1, source_target_pairs={{4,8},{8,4},{5,9},{9,5},{6,10},{10,6},{7,11},{11,7},{20,24},{24,20... | collective-permute-start | bytes 798728 | tf_op jit(solution)/shard_map/ppermute | solution.py:535
  7.5 31.8 %collective-permute-start.4 = (bf16[1040,128]{1,0:T(8,128)(2,1)}, bf16[1040,128]{1,0:T(8,128)(2,1)S(1)}, u32[]{:S(2)}, u32[]{:S(2)}) collective-permute-start(bf16[1040,128]{1,0:T(8,128)(2,1)} %get-tuple-element.19.refs_0_), channel_id=1, source_target_pairs={{0,4},{4,0},{8,12},{12,8},{1,5},{5,1},{9,13},{13,9},{2,6},{6,2},{1... | collective-permute-start | bytes 798728 | tf_op jit(solution)/shard_map/ppermute | solution.py:535
  25.6 13.7 %collective-permute-start.7 = (bf16[1040,128]{1,0:T(8,128)(2,1)S(1)}, bf16[1040,128]{1,0:T(8,128)(2,1)S(1)}, u32[]{:S(2)}, u32[]{:S(2)}) collective-permute-start(bf16[1040,128]{1,0:T(8,128)(2,1)S(1)} %collective-permute-done.5.refs_2_), channel_id=1, source_target_pairs={{4,0},{8,12},{5,1},{9,13},{6,2},{10,14},{7,3},{11,15},{20,16},{24,... | collective-permute-start | bytes 798728 | tf_op jit(solution)/shard_map/ppermute | solution.py:535
  26.9 17.8 %collective-permute-start.2 = (bf16[1040,128]{1,0:T(8,128)(2,1)}, bf16[1040,128]{1,0:T(8,128)(2,1)S(1)}, u32[]{:S(2)}, u32[]{:S(2)}) collective-permute-start(bf16[1040,128]{1,0:T(8,128)(2,1)} %get-tuple-element.16.refs_0_), channel_id=1, source_target_pairs={{4,8},{8,4},{5,9},{9,5},{6,10},{10,6},{7,11},{11,7},{20,24},{24,20... | collective-permute-start | bytes 798728 | tf_op jit(solution)/shard_map/ppermute | solution.py:535
  31.3 13.4 %collective-permute-start = (bf16[1040,128]{1,0:T(8,128)(2,1)}, bf16[1040,128]{1,0:T(8,128)(2,1)S(1)}, u32[]{:S(2)}, u32[]{:S(2)}) collective-permute-start(bf16[1040,128]{1,0:T(8,128)(2,1)} %get-tuple-element.16.refs_0_), channel_id=1, source_target_pairs={{0,4},{4,0},{8,12},{12,8},{1,5},{5,1},{9,13},{13,9},{2,6},{6,2},{1... | collective-permute-start | bytes 798728 | tf_op jit(solution)/shard_map/ppermute | solution.py:535
  33.5 14.1 %collective-permute-start.3 = (bf16[1040,128]{1,0:T(8,128)(2,1)S(1)}, bf16[1040,128]{1,0:T(8,128)(2,1)S(1)}, u32[]{:S(2)}, u32[]{:S(2)}) collective-permute-start(bf16[1040,128]{1,0:T(8,128)(2,1)S(1)} %collective-permute-done.1.refs_2_), channel_id=1, source_target_pairs={{4,0},{8,12},{5,1},{9,13},{6,2},{10,14},{7,3},{11,15},{20,16},{24,... | collective-permute-start | bytes 798728 | tf_op jit(solution)/shard_map/ppermute | solution.py:535
  34.8 1.2 %copy-start = (bf16[1024,512]{1,0:T(8,128)(2,1)S(1)}, bf16[1024,512]{1,0:T(8,128)(2,1)}, u32[]{:S(2)}) copy-start(bf16[1024,512]{1,0:T(8,128)(2,1)} %refs_9_.3) | copy-start | bytes 3145732
  36.0 1.2 %copy-start.2 = (bf16[1024,512]{1,0:T(8,128)(2,1)S(1)}, bf16[1024,512]{1,0:T(8,128)(2,1)}, u32[]{:S(2)}) copy-start(bf16[1024,512]{1,0:T(8,128)(2,1)} %tv_ref.1) | copy-start | bytes 3145732
  37.2 0.7 %copy-start.6 = (s32[4]{0:T(128)S(1)}, s32[4]{0:T(128)}, u32[]{:S(2)}) copy-start(s32[4]{0:T(128)} %len_ref.1) | copy-start | bytes 52
  37.9 1.4 %copy-start.1 = (bf16[1024,512]{1,0:T(8,128)(2,1)S(1)}, bf16[1024,512]{1,0:T(8,128)(2,1)}, u32[]{:S(2)}) copy-start(bf16[1024,512]{1,0:T(8,128)(2,1)} %refs_9_.3) | copy-start | bytes 3145732
  37.9 1.4 %copy-start.7 = (bf16[1040,128]{1,0:T(8,128)(2,1)S(1)}, bf16[1040,128]{1,0:T(8,128)(2,1)}, u32[]{:S(2)}) copy-start(bf16[1040,128]{1,0:T(8,128)(2,1)} %get-tuple-element.19.refs_0_) | copy-start | bytes 798724
  39.3 8.3 %copy-start.5 = (bf16[1040,128]{1,0:T(8,128)(2,1)S(1)}, bf16[1040,128]{1,0:T(8,128)(2,1)}, u32[]{:S(2)}) copy-start(bf16[1040,128]{1,0:T(8,128)(2,1)} %get-tuple-element.16.refs_0_) | copy-start | bytes 798724

commit v4 on v3

--- a/solution.py
+++ b/solution.py
@@ -539,14 +539,18 @@
         across = [(0, 2), (2, 0), (1, 3), (3, 1)]
         middle = [(1, 2), (2, 1)]
         outward = [(1, 0), (2, 3)]
-        pieces = []
-        for x in payloads:
-            skip = send(x, across)
-            near = send(x, outer)
-            far = send(x, middle)
-            last = send(skip, outward)
-            pieces.append((x, near, skip, far, last))
         text = prepare_text(text_len, text_keys, text_values)
+
+        def after(x, *others):
+            return lax.optimization_barrier((x, *others))[0]
+
+        a, b = payloads
+        skip_a, near_a = send(a, across), send(a, outer)
+        skip_b, near_b = send(b, across), send(b, outer)
+        far_a, far_b = send(a, middle), send(b, middle)
+        last_a = send(after(skip_a, near_b, *text), outward)
+        last_b = send(skip_b, outward)
+        pieces = [(a, near_a, skip_a, far_a, last_a), (b, near_b, skip_b, far_b, last_b)]
         outs = ()
         for chunk, piece in zip(chunks, pieces):
             outs = attend_line(

time: 53.3 us -> 48.1 us (0.902)
  waiting for transfers between devices: 20 us -> 15.4 us
  starting transfers between devices: 14.9 us -> 14.3 us
    ppermute x8, waiting for transfers between devices: 20 us -> 15.4 us  [send(): return lax.ppermute(x, 'ctx', pairs)]
    ppermute x8, starting transfers between devices: 14.9 us -> 14.3 us  [send(): return lax.ppermute(x, 'ctx', pairs)]
  transfers between devices with their start and end apart: 8 -> 8, of which waited for: 3 -> 4; matrix products, arithmetic and copies ran while one was open for 0% -> 0% of each run, Pallas kernels for 13% -> 14%
where the time goes in v4:
time: 48.1 us; the launch traced here: 47.9 us
  waiting for transfers between devices  15.4 us (32%)
  starting transfers between devices  14.3 us (30%)
  Pallas kernels  14.2 us (30%)
  local copies, waits for them, and re-layouts  3.12 us (6%)
  between operations  0.76 us (2%)
    ppermute x8, waiting for transfers between devices, send(): return lax.ppermute(x, 'ctx', pairs)  15.4 us
    ppermute x8, starting transfers between devices, send(): return lax.ppermute(x, 'ctx', pairs)  14.3 us
    pallas_call x2, Pallas kernels, attend_line(): pl.pallas_call(functools.partial(line_kernel, first, count, clips), in_sp...  10.7 us
    unnamed x16, local copies, waits for them, and re-layouts  3.12 us
    pallas_call x1, Pallas kernels, pack(): pl.pallas_call(functools.partial(pack_kernel, chunks), out_shape=[jax.Sha...  2.11 us
    pallas_call x1, Pallas kernels, prepare_text(): pl.pallas_call(text_kernel, in_specs=[pl.BlockSpec(memory_space=pltpu.SME...  1.38 us
  transfers between devices with their start and end apart: 8, of which 4 were waited for; matrix products, arithmetic and copies ran while one was open for 0% of the time, Pallas kernels for 14%

profile of v4, /device:TPU:0, one launch (start us, length us, event | category | flops | bytes accessed | tf_op | source)
XLA Modules:
  0.0 47.9 jit_solution(13386630947267527753)
XLA Ops:
  0.6 0.0 copy-start.4
  0.7 2.1 %pack.1 = (bf16[1040,128]{1,0:T(8,128)(2,1)}, bf16[1040,128]{1,0:T(8,128)(2,1)}) custom-call(bf16[128,512]{1,0:T(8,128)(2,1)} %refs_7_.3, bf16[128,512]{1,0:T(8,128)(2,1)} %refs_8_.3, bf16[128,512]{1,0:T(8,128)(2,1)} %v_ref.1, bf16[128,512]{1,0:T(8,128)(2,1)} %g_ref.1, s32[1,128]{1,0:T(1,128)} %bitcast.1), custom_call_target="tpu_custom_call" | custom-call | tf_op jit(solution)/shard_map/pack/pallas_call | solution.py:53
  2.8 3.0 %collective-permute-start = (bf16[1040,128]{1,0:T(8,128)(2,1)}, bf16[1040,128]{1,0:T(8,128)(2,1)S(1)}, u32[]{:S(2)}, u32[]{:S(2)}) collective-permute-start(bf16[1040,128]{1,0:T(8,128)(2,1)} %get-tuple-element.17.refs_0_), channel_id=1, source_target_pairs={{0,4},{4,0},{8,12},{12,8},{1,5},{5,1},{9,13},{13,9},{2,6},{6,2},{1... | collective-permute-start | bytes 798728 | tf_op jit(solution)/shard_map/ppermute | solution.py:535
  5.8 2.6 %collective-permute-start.5 = (bf16[1040,128]{1,0:T(8,128)(2,1)}, bf16[1040,128]{1,0:T(8,128)(2,1)S(1)}, u32[]{:S(2)}, u32[]{:S(2)}) collective-permute-start(bf16[1040,128]{1,0:T(8,128)(2,1)} %get-tuple-element.20.refs_0_), channel_id=1, source_target_pairs={{0,8},{8,0},{4,12},{12,4},{1,9},{9,1},{5,13},{13,5},{2,10},{10,2},... | collective-permute-start | bytes 798728 | tf_op jit(solution)/shard_map/ppermute | solution.py:535
  8.4 0.3 collective-permute-start.1
  8.7 0.7 %collective-permute-start.6 = (bf16[1040,128]{1,0:T(8,128)(2,1)}, bf16[1040,128]{1,0:T(8,128)(2,1)S(1)}, u32[]{:S(2)}, u32[]{:S(2)}) collective-permute-start(bf16[1040,128]{1,0:T(8,128)(2,1)} %get-tuple-element.20.refs_0_), channel_id=1, source_target_pairs={{4,8},{8,4},{5,9},{9,5},{6,10},{10,6},{7,11},{11,7},{20,24},{24,20... | collective-permute-start | bytes 798728 | tf_op jit(solution)/shard_map/ppermute | solution.py:535
  9.4 4.4 %collective-permute-start.4 = (bf16[1040,128]{1,0:T(8,128)(2,1)}, bf16[1040,128]{1,0:T(8,128)(2,1)S(1)}, u32[]{:S(2)}, u32[]{:S(2)}) collective-permute-start(bf16[1040,128]{1,0:T(8,128)(2,1)} %get-tuple-element.20.refs_0_), channel_id=1, source_target_pairs={{0,4},{4,0},{8,12},{12,8},{1,5},{5,1},{9,13},{13,9},{2,6},{6,2},{1... | collective-permute-start | bytes 798728 | tf_op jit(solution)/shard_map/ppermute | solution.py:535
  13.8 1.2 %copy-done = bf16[1024,512]{1,0:T(8,128)(2,1)S(1)} copy-done((bf16[1024,512]{1,0:T(8,128)(2,1)S(1)}, bf16[1024,512]{1,0:T(8,128)(2,1)}, u32[]{:S(2)}) %copy-start) | copy-done | bytes 1048600
  15.1 1.2 %copy-done.2 = bf16[1024,512]{1,0:T(8,128)(2,1)S(1)} copy-done((bf16[1024,512]{1,0:T(8,128)(2,1)S(1)}, bf16[1024,512]{1,0:T(8,128)(2,1)}, u32[]{:S(2)}) %copy-start.2) | copy-done | bytes 1048600
  16.3 0.7 %copy-done.6 = s32[4]{0:T(128)S(1)} copy-done((s32[4]{0:T(128)S(1)}, s32[4]{0:T(128)}, u32[]{:S(2)}) %copy-start.6) | copy-done | bytes 40
  16.9 1.4 %prepare_text.1 = (bf16[4096,256]{1,0:T(8,128)(2,1)S(1)}, bf16[1024,512]{1,0:T(8,128)(2,1)S(1)}) custom-call(s32[4]{0:T(128)S(1)} %copy-done.6, bf16[1024,512]{1,0:T(8,128)(2,1)S(1)} %copy-done, bf16[1024,512]{1,0:T(8,128)(2,1)S(1)} %copy-done.2), custom_call_target="tpu_custom_call" | custom-call | flops 4194304 | bytes 3145728 | tf_op jit(solution)/shard_map/prepare_text/pallas_call | solution.py:302
  18.3 0.5 collective-permute-done.refs_1_
  18.8 8.9 %collective-permute-done.5.refs_2_ = bf16[1040,128]{1,0:T(8,128)(2,1)S(1)} collective-permute-done((bf16[1040,128]{1,0:T(8,128)(2,1)}, bf16[1040,128]{1,0:T(8,128)(2,1)S(1)}, u32[]{:S(2)}, u32[]{:S(2)}) %collective-permute-start.5) | collective-permute-done | bytes 266272 | tf_op jit(solution)/shard_map/ppermute | solution.py:535
  27.7 1.3 %collective-permute-start.7 = (bf16[1040,128]{1,0:T(8,128)(2,1)S(1)}, bf16[1040,128]{1,0:T(8,128)(2,1)S(1)}, u32[]{:S(2)}, u32[]{:S(2)}) collective-permute-start(bf16[1040,128]{1,0:T(8,128)(2,1)S(1)} %collective-permute-done.5.refs_2_), channel_id=1, source_target_pairs={{4,0},{8,12},{5,1},{9,13},{6,2},{10,14},{7,3},{11,15},{20,16},{24,... | collective-permute-start | bytes 798728 | tf_op jit(solution)/shard_map/ppermute | solution.py:535
  29.0 0.7 %collective-permute-start.2 = (bf16[1040,128]{1,0:T(8,128)(2,1)S(1)}, bf16[1040,128]{1,0:T(8,128)(2,1)S(1)}, u32[]{:S(2)}, u32[]{:S(2)}) collective-permute-start(bf16[1040,128]{1,0:T(8,128)(2,1)S(1)} %copy-done.5), channel_id=1, source_target_pairs={{4,8},{8,4},{5,9},{9,5},{6,10},{10,6},{7,11},{11,7},{20,24},{24,20... | collective-permute-start | bytes 798728 | tf_op jit(solution)/shard_map/ppermute | solution.py:535
  29.7 3.7 %collective-permute-done.1.refs_2_ = bf16[1040,128]{1,0:T(8,128)(2,1)S(1)} collective-permute-done((bf16[1040,128]{1,0:T(8,128)(2,1)}, bf16[1040,128]{1,0:T(8,128)(2,1)S(1)}, u32[]{:S(2)}, u32[]{:S(2)}) %collective-permute-start.1) | collective-permute-done | bytes 266272 | tf_op jit(solution)/shard_map/ppermute | solution.py:535
  33.4 1.3 %collective-permute-start.3 = (bf16[1040,128]{1,0:T(8,128)(2,1)S(1)}, bf16[1040,128]{1,0:T(8,128)(2,1)S(1)}, u32[]{:S(2)}, u32[]{:S(2)}) collective-permute-start(bf16[1040,128]{1,0:T(8,128)(2,1)S(1)} %collective-permute-done.1.refs_2_), channel_id=1, source_target_pairs={{4,0},{8,12},{5,1},{9,13},{6,2},{10,14},{7,3},{11,15},{20,16},{24,... | collective-permute-start | bytes 798728 | tf_op jit(solution)/shard_map/ppermute | solution.py:535
  34.7 0.0 collective-permute-done.6.refs_3_
  34.7 0.0 collective-permute-done.4.refs_1_
  34.7 2.4 %collective-permute-done.7.refs_4_ = bf16[1040,128]{1,0:T(8,128)(2,1)S(1)} collective-permute-done((bf16[1040,128]{1,0:T(8,128)(2,1)S(1)}, bf16[1040,128]{1,0:T(8,128)(2,1)S(1)}, u32[]{:S(2)}, u32[]{:S(2)}) %collective-permute-start.7) | collective-permute-done | bytes 266272 | tf_op jit(solution)/shard_map/ppermute | solution.py:535
  37.1 5.4 %attend_line.2 = (bf16[128,512]{1,0:T(8,128)(2,1)}, bf16[128,512]{1,0:T(8,128)(2,1)}, bf16[128,512]{1,0:T(8,128)(2,1)}, bf16[128,512]{1,0:T(8,128)(2,1)}, f32[1024,512]{1,0:T(8,128)}, /*index=5*/f32[1024,512]{1,0:T(8,128)}) custom-call(bf16[1040,128]{1,0:T(8,128)(2,1)S(1)} %copy-done.7, bf16[1040,128]{1,0:T(8,128)(2,1)S(1)} %collective-permute-done.4.refs_1_, ...), custom_call_target="tpu_custom_call" | custom-call | flops 2415919104 | bytes 4194304 | tf_op jit(solution)/shard_map/attend_line/pallas_call | solution.py:490
  42.5 0.0 collective-permute-done.2.refs_3_
  42.5 0.0 collective-permute-done.3.refs_4_
  42.5 5.4 %attend_line.3 = (bf16[128,512]{1,0:T(8,128)(2,1)}, bf16[128,512]{1,0:T(8,128)(2,1)}, bf16[128,512]{1,0:T(8,128)(2,1)}, bf16[128,512]{1,0:T(8,128)(2,1)}, f32[1024,512]{1,0:T(8,128)}, /*index=5*/f32[1024,512]{1,0:T(8,128)}) custom-call(bf16[1040,128]{1,0:T(8,128)(2,1)S(1)} %copy-done.5, ...), custom_call_target="tpu_custom_call", output_to_operand_aliasing={{0}: (10, {}), {1}: (11, {}), {2}: (12, {}), {3}: (13, {}),... | custom-call | flops 2415919104 | bytes 4194304 | tf_op jit(solution)/shard_map/attend_line/pallas_call | solution.py:490
  (12 shorter events, 0.0 us)
Async XLA Ops:
  0.6 36.4 %copy-start.4 = (bf16[128,512]{1,0:T(8,128)(2,1)S(1)}, bf16[128,512]{1,0:T(8,128)(2,1)}, u32[]{:S(2)}) copy-start(bf16[128,512]{1,0:T(8,128)(2,1)} %refs_8_.3) | copy-start | bytes 393220
  0.6 36.4 %copy-start.3 = (bf16[128,512]{1,0:T(8,128)(2,1)S(1)}, bf16[128,512]{1,0:T(8,128)(2,1)}, u32[]{:S(2)}) copy-start(bf16[128,512]{1,0:T(8,128)(2,1)} %refs_7_.3) | copy-start | bytes 393220
  2.8 16.0 %collective-permute-start = (bf16[1040,128]{1,0:T(8,128)(2,1)}, bf16[1040,128]{1,0:T(8,128)(2,1)S(1)}, u32[]{:S(2)}, u32[]{:S(2)}) collective-permute-start(bf16[1040,128]{1,0:T(8,128)(2,1)} %get-tuple-element.17.refs_0_), channel_id=1, source_target_pairs={{0,4},{4,0},{8,12},{12,8},{1,5},{5,1},{9,13},{13,9},{2,6},{6,2},{1... | collective-permute-start | bytes 798728 | tf_op jit(solution)/shard_map/ppermute | solution.py:535
  5.8 21.9 %collective-permute-start.5 = (bf16[1040,128]{1,0:T(8,128)(2,1)}, bf16[1040,128]{1,0:T(8,128)(2,1)S(1)}, u32[]{:S(2)}, u32[]{:S(2)}) collective-permute-start(bf16[1040,128]{1,0:T(8,128)(2,1)} %get-tuple-element.20.refs_0_), channel_id=1, source_target_pairs={{0,8},{8,0},{4,12},{12,4},{1,9},{9,1},{5,13},{13,5},{2,10},{10,2},... | collective-permute-start | bytes 798728 | tf_op jit(solution)/shard_map/ppermute | solution.py:535
  8.4 25.0 %collective-permute-start.1 = (bf16[1040,128]{1,0:T(8,128)(2,1)}, bf16[1040,128]{1,0:T(8,128)(2,1)S(1)}, u32[]{:S(2)}, u32[]{:S(2)}) collective-permute-start(bf16[1040,128]{1,0:T(8,128)(2,1)} %get-tuple-element.17.refs_0_), channel_id=1, source_target_pairs={{0,8},{8,0},{4,12},{12,4},{1,9},{9,1},{5,13},{13,5},{2,10},{10,2},... | collective-permute-start | bytes 798728 | tf_op jit(solution)/shard_map/ppermute | solution.py:535
  8.7 26.0 %collective-permute-start.6 = (bf16[1040,128]{1,0:T(8,128)(2,1)}, bf16[1040,128]{1,0:T(8,128)(2,1)S(1)}, u32[]{:S(2)}, u32[]{:S(2)}) collective-permute-start(bf16[1040,128]{1,0:T(8,128)(2,1)} %get-tuple-element.20.refs_0_), channel_id=1, source_target_pairs={{4,8},{8,4},{5,9},{9,5},{6,10},{10,6},{7,11},{11,7},{20,24},{24,20... | collective-permute-start | bytes 798728 | tf_op jit(solution)/shard_map/ppermute | solution.py:535
  9.4 25.3 %collective-permute-start.4 = (bf16[1040,128]{1,0:T(8,128)(2,1)}, bf16[1040,128]{1,0:T(8,128)(2,1)S(1)}, u32[]{:S(2)}, u32[]{:S(2)}) collective-permute-start(bf16[1040,128]{1,0:T(8,128)(2,1)} %get-tuple-element.20.refs_0_), channel_id=1, source_target_pairs={{0,4},{4,0},{8,12},{12,8},{1,5},{5,1},{9,13},{13,9},{2,6},{6,2},{1... | collective-permute-start | bytes 798728 | tf_op jit(solution)/shard_map/ppermute | solution.py:535
  13.8 1.2 %copy-start = (bf16[1024,512]{1,0:T(8,128)(2,1)S(1)}, bf16[1024,512]{1,0:T(8,128)(2,1)}, u32[]{:S(2)}) copy-start(bf16[1024,512]{1,0:T(8,128)(2,1)} %refs_9_.3) | copy-start | bytes 3145732
  15.1 1.2 %copy-start.2 = (bf16[1024,512]{1,0:T(8,128)(2,1)S(1)}, bf16[1024,512]{1,0:T(8,128)(2,1)}, u32[]{:S(2)}) copy-start(bf16[1024,512]{1,0:T(8,128)(2,1)} %tv_ref.1) | copy-start | bytes 3145732
  16.3 0.7 %copy-start.6 = (s32[4]{0:T(128)S(1)}, s32[4]{0:T(128)}, u32[]{:S(2)}) copy-start(s32[4]{0:T(128)} %len_ref.1) | copy-start | bytes 52
  16.9 12.1 %copy-start.5 = (bf16[1040,128]{1,0:T(8,128)(2,1)S(1)}, bf16[1040,128]{1,0:T(8,128)(2,1)}, u32[]{:S(2)}) copy-start(bf16[1040,128]{1,0:T(8,128)(2,1)} %get-tuple-element.17.refs_0_) | copy-start | bytes 798724
  16.9 20.1 %copy-start.1 = (bf16[1024,512]{1,0:T(8,128)(2,1)S(1)}, bf16[1024,512]{1,0:T(8,128)(2,1)}, u32[]{:S(2)}) copy-start(bf16[1024,512]{1,0:T(8,128)(2,1)} %refs_9_.3) | copy-start | bytes 3145732
  16.9 20.1 %copy-start.7 = (bf16[1040,128]{1,0:T(8,128)(2,1)S(1)}, bf16[1040,128]{1,0:T(8,128)(2,1)}, u32[]{:S(2)}) copy-start(bf16[1040,128]{1,0:T(8,128)(2,1)} %get-tuple-element.20.refs_0_) | copy-start | bytes 798724
  27.7 9.3 %collective-permute-start.7 = (bf16[1040,128]{1,0:T(8,128)(2,1)S(1)}, bf16[1040,128]{1,0:T(8,128)(2,1)S(1)}, u32[]{:S(2)}, u32[]{:S(2)}) collective-permute-start(bf16[1040,128]{1,0:T(8,128)(2,1)S(1)} %collective-permute-done.5.refs_2_), channel_id=1, source_target_pairs={{4,0},{8,12},{5,1},{9,13},{6,2},{10,14},{7,3},{11,15},{20,16},{24,... | collective-permute-start | bytes 798728 | tf_op jit(solution)/shard_map/ppermute | solution.py:535
  29.0 13.4 %collective-permute-start.2 = (bf16[1040,128]{1,0:T(8,128)(2,1)S(1)}, bf16[1040,128]{1,0:T(8,128)(2,1)S(1)}, u32[]{:S(2)}, u32[]{:S(2)}) collective-permute-start(bf16[1040,128]{1,0:T(8,128)(2,1)S(1)} %copy-done.5), channel_id=1, source_target_pairs={{4,8},{8,4},{5,9},{9,5},{6,10},{10,6},{7,11},{11,7},{20,24},{24,20... | collective-permute-start | bytes 798728 | tf_op jit(solution)/shard_map/ppermute | solution.py:535
  33.4 9.1 %collective-permute-start.3 = (bf16[1040,128]{1,0:T(8,128)(2,1)S(1)}, bf16[1040,128]{1,0:T(8,128)(2,1)S(1)}, u32[]{:S(2)}, u32[]{:S(2)}) collective-permute-start(bf16[1040,128]{1,0:T(8,128)(2,1)S(1)} %collective-permute-done.1.refs_2_), channel_id=1, source_target_pairs={{4,0},{8,12},{5,1},{9,13},{6,2},{10,14},{7,3},{11,15},{20,16},{24,... | collective-permute-start | bytes 798728 | tf_op jit(solution)/shard_map/ppermute | solution.py:535

commit v5 on v4

--- a/solution.py
+++ b/solution.py
@@ -277,7 +277,7 @@
     )(*operands)
 
 
-def text_kernel(len_ref, tk_ref, tv_ref, kt_ref, vt_ref):
+def text_kernel(len_ref, tk_ref, tv_ref, kt_ref, vt_ref, inv_ref):
     text_rows, width = tk_ref.shape
     clips = len_ref.shape[0]
     per_clip = text_rows // clips
@@ -291,8 +291,10 @@
         for h in range(width // HD):
             to = pl.ds(h * text_rows + c * per_clip, per_clip)
             x = tk_ref[rows, pl.ds(h * HD, HD)].astype(F32)
-            kt_ref[to, :HD] = (x * inverse_rms(x)).astype(BF16)
+            inverse = inverse_rms(x)
+            kt_ref[to, :HD] = (x * inverse).astype(BF16)
             kt_ref[to, HD:] = mask
+            inv_ref[to, :] = jnp.broadcast_to(inverse, (per_clip, HD))
     vt_ref[...] = tv_ref[...]
 
 
@@ -302,12 +304,13 @@
     return pl.pallas_call(
         text_kernel,
         in_specs=[pl.BlockSpec(memory_space=pltpu.SMEM), whole, whole],
-        out_specs=[whole, whole],
+        out_specs=[whole, whole, whole],
         out_shape=[
             jax.ShapeDtypeStruct((width // HD * text_rows, 2 * HD), BF16),
             jax.ShapeDtypeStruct((text_rows, width), BF16),
+            jax.ShapeDtypeStruct((width // HD * text_rows, HD), F32),
         ],
-        compiler_params=pltpu.CompilerParams(vmem_limit_bytes=12 * 1024 * 1024),
+        compiler_params=pltpu.CompilerParams(vmem_limit_bytes=16 * 1024 * 1024),
         cost_estimate=pl.CostEstimate(
             flops=8 * text_rows * width, bytes_accessed=6 * text_rows * width, transcendentals=0
         ),
@@ -316,7 +319,7 @@
 
 
 def line_kernel(first, count, clips, *refs):
-    own, near, skip, far, last, kt, vt, q_any, k_any, t_any = refs[:10]
+    own, near, skip, far, last, kt, vt, inv_t, q_any, k_any, t_any = refs[:11]
     out, gq, gk, gv, gtk, gtv = refs[-26:-20]
     (pick, qx, kx, vx, gx, qs, gs, e_row, e_col, e_text, d_row, d_col, d_text) = refs[-20:-7]
     raw_q, raw_k, raw_t, staged, staged_text, in_sems, out_sems = refs[-7:]
@@ -357,8 +360,11 @@
         tops.append(jnp.max(seg))
         onehot = jnp.where(jnp.broadcast_to(seg, (HD, length)) == sub, 1.0, 0.0).T
         rows = pl.ds(s * length, length)
-        qx[rows, HD:] = jnp.where(lane == clips, 1.0, onehot).astype(BF16)
-        kx[rows, HD:] = jnp.where(lane < clips, (onehot - 1.0) * FAR, 0.0).astype(BF16)
+        q_mask = jnp.where(lane == clips, 1.0, onehot).astype(BF16)
+        k_mask = jnp.where(lane < clips, (onehot - 1.0) * FAR, 0.0).astype(BF16)
+        for b in range(count):
+            qx[b, rows, HD:] = q_mask
+            kx[b, rows, HD:] = k_mask
     flipped = me >= 2
     middle = jnp.where(
         flipped, jnp.maximum(tops[2], tops[3]), jnp.maximum(tops[0], tops[1])
@@ -377,98 +383,134 @@
 
     mine = slice(0, length)
     stores = []
-
-    def put(source, target, cols, rows=None):
-        to = target.at[:, cols] if rows is None else target.at[rows, cols]
-        copy = pltpu.make_async_copy(source, to, out_sems.at[len(stores)])
+    state = [{} for _ in range(count)]
+
+    def columns(b):
+        return pl.ds((first + b) * HD, HD)
+
+    def put(source, target, b):
+        copy = pltpu.make_async_copy(source, target.at[:, columns(b)], out_sems.at[len(stores)])
         copy.start()
         stores.append(copy)
 
-    for b in range(count):
-        cols = pl.ds((first + b) * HD, HD)
+    def text_at(b, clip):
+        keys = pl.ds(pl.multiple_of((first + b) * text_rows + clip * per_clip, per_clip), per_clip)
+        return keys, pl.ds(pl.multiple_of(clip * per_clip, per_clip), per_clip)
+
+    def place(b):
         for s, piece in enumerate(pieces):
             rows = pl.ds(s * length, length)
-            for a, (ref, to) in enumerate(((qx, pl.ds(0, HD)), (kx, pl.ds(0, HD)), (vx, pl.ds(0, HD)), (gx, pl.ds(0, HD)))):
-                ref[rows, to] = piece[pl.ds((4 * b + a) * length, length), :]
-
+            for a, ref in enumerate((qx, kx, vx, gx)):
+                ref[b, rows, :HD] = piece[pl.ds((4 * b + a) * length, length), :]
+
+    def video_scores(b):
         norm = [jnp.zeros((8, half), F32)] * 2
         mean = [jnp.zeros((8, half), F32)] * 2
         for j in range(2):
             for i in range(2):
                 keys, rows = pl.ds(j * half, half), pl.ds(i * half, half)
-                e = jnp.exp2(dot(kx[keys, :], qx[rows, :], (1, 1)) * exponent)
-                dp = dot(vx[keys, :], gx[rows, :], (1, 1))
+                e = jnp.exp2(dot(kx[b, keys, :], qx[b, rows, :], (1, 1)) * exponent)
+                dp = dot(vx[b, keys, :], gx[b, rows, :], (1, 1))
                 norm[i] = norm[i] + split_sum(e)
                 mean[i] = mean[i] + split_sum(e * dp)
                 if j == 0:
-                    e_row[:, rows] = e[mine, :].astype(BF16)
-                    d_row[:, rows] = dp[mine, :]
+                    e_row[b, :, rows] = e[mine, :].astype(BF16)
+                    d_row[b, :, rows] = dp[mine, :]
                 if i == 0:
-                    e_col[keys, :] = e[:, mine].astype(BF16)
-                    d_col[keys, :] = dp[:, mine]
-        for k, (clip, here, rows) in enumerate(pairs):
-            keys = pl.ds(pl.multiple_of((first + b) * text_rows + clip * per_clip, per_clip), per_clip)
-            vals = pl.ds(pl.multiple_of(clip * per_clip, per_clip), per_clip)
-            e = jnp.exp2(dot(kt[keys, :], qx[rows, :], (1, 1)) * exponent)
-            dp = dot(vt[vals, cols], gx[rows, :], (1, 1))
-            e_text[k] = e.astype(BF16)
-            d_text[k] = dp
-            for sums, part in ((norm, split_sum(e)), (mean, split_sum(e * dp))):
-                sums[0] = sums[0] + jnp.where(here, part, 0.0)
-                sums[1] = sums[1] + jnp.where(here, 0.0, part)
-
-        inv = [1.0 / jnp.sum(x, axis=0, keepdims=True) for x in norm]
-        inner = [jnp.sum(x, axis=0, keepdims=True) * y for x, y in zip(mean, inv)]
-        turned = []
+                    e_col[b, keys, :] = e[:, mine].astype(BF16)
+                    d_col[b, keys, :] = dp[:, mine]
+        state[b].update(norm=norm, mean=mean)
+
+    def text_scores(b, k):
+        clip, here, rows = pairs[k]
+        keys, vals = text_at(b, clip)
+        e = jnp.exp2(dot(kt[keys, :], qx[b, rows, :], (1, 1)) * exponent)
+        dp = dot(vt[vals, columns(b)], gx[b, rows, :], (1, 1))
+        e_text[b, k] = e.astype(BF16)
+        d_text[b, k] = dp
+        for name, part in (("norm", split_sum(e)), ("mean", split_sum(e * dp))):
+            sums = state[b][name]
+            sums[0] = sums[0] + jnp.where(here, part, 0.0)
+            sums[1] = sums[1] + jnp.where(here, 0.0, part)
+
+    def close_sums(b):
+        inv = [1.0 / jnp.sum(x, axis=0, keepdims=True) for x in state[b]["norm"]]
+        inner = [jnp.sum(x, axis=0, keepdims=True) * y for x, y in zip(state[b]["mean"], inv)]
         for s in range(4):
             part = inv[s // 2][:, (s % 2) * length : (s % 2 + 1) * length]
-            turned.append(jnp.broadcast_to(part, (HD, length)).T)
+            turned = jnp.broadcast_to(part, (HD, length)).T
+            if s == 0:
+                state[b]["turned"] = turned
             rows = pl.ds(s * length, length)
-            qs[rows, :] = (qx[rows, :HD].astype(F32) * (turned[s] * scale)).astype(BF16)
-            gs[rows, :] = (gx[rows, :].astype(F32) * turned[s]).astype(BF16)
-
-        att = jnp.zeros((length, HD), F32)
-        dq = jnp.zeros((length, HD), F32)
-        fetches[3 * b + 2].wait()
-        before = None
-        for k, (clip, here, rows) in enumerate(pairs):
-            keys = pl.ds(pl.multiple_of((first + b) * text_rows + clip * per_clip, per_clip), per_clip)
-            vals = pl.ds(pl.multiple_of(clip * per_clip, per_clip), per_clip)
-            eb = e_text[k]
-            away = jnp.where(here, inner[0], inner[1])
-            ds = (eb.astype(F32) * (d_text[k] - away)).astype(BF16)
-            dk = dot(ds, qs[rows, :], (1, 0))
-            dv = dot(eb, gs[rows, :], (1, 0))
-            att = att + jnp.where(here, dot(eb[:, mine], vt[vals, cols], (0, 0)), 0.0)
-            dq = dq + jnp.where(here, dot(ds[:, mine], kt[keys, :HD], (0, 0)), 0.0)
-            if before is not None:
-                c = k - 1
-                low, high = c <= middle, c >= middle
-                to = pl.ds(c * per_clip, per_clip)
-                total = jnp.where(low, before[0], 0.0) + jnp.where(high, dk, 0.0)
-                staged_text[b, 0, to, :] = norm_back(raw_t[b, to, :].astype(F32), total)
-                staged_text[b, 1, to, :] = jnp.where(low, before[1], 0.0) + jnp.where(high, dv, 0.0)
-                put(staged_text.at[b, 0, to], gtk, cols, to)
-                put(staged_text.at[b, 1, to], gtv, cols, to)
-            before = (dk, dv)
-
-        eb = e_row[...]
-        inner_all = jnp.concatenate(inner, axis=1)
-        ds = (eb.astype(F32) * (d_row[...] - inner_all)).astype(BF16)
-        dk = dot(ds, qs[...], (1, 0))
-        dv = dot(eb, gs[...], (1, 0))
-        eb = e_col[...]
-        ds = (eb.astype(F32) * (d_col[...] - inner[0][:, mine])).astype(BF16)
-        att = att + dot(eb, vx[...], (0, 0))
-        dq = dq + dot(ds, kx[:, :HD], (0, 0))
-        fetches[3 * b].wait()
-        fetches[3 * b + 1].wait()
-        staged[b, 0] = (att * turned[0]).astype(BF16)
-        staged[b, 1] = norm_back(raw_q[b].astype(F32), dq * (turned[0] * scale)).astype(BF16)
+            qs[b, rows, :] = (qx[b, rows, :HD].astype(F32) * (turned * scale)).astype(BF16)
+            gs[b, rows, :] = (gx[b, rows, :].astype(F32) * turned).astype(BF16)
+        state[b].update(
+            inner=inner, att=jnp.zeros((length, HD), F32), dq=jnp.zeros((length, HD), F32), before=None
+        )
+
+    def text_grads(b, k):
+        me_b = state[b]
+        clip, here, rows = pairs[k]
+        keys, vals = text_at(b, clip)
+        eb = e_text[b, k]
+        away = jnp.where(here, me_b["inner"][0], me_b["inner"][1])
+        ds = (eb.astype(F32) * (d_text[b, k] - away)).astype(BF16)
+        dk = dot(ds, qs[b, rows, :], (1, 0))
+        dv = dot(eb, gs[b, rows, :], (1, 0))
+        me_b["att"] += jnp.where(here, dot(eb[:, mine], vt[vals, columns(b)], (0, 0)), 0.0)
+        me_b["dq"] += jnp.where(here, dot(ds[:, mine], kt[keys, :HD], (0, 0)), 0.0)
+        if k:
+            c = k - 1
+            low, high = c <= middle, c >= middle
+            to = pl.ds(c * per_clip, per_clip)
+            total = jnp.where(low, me_b["before"][0], 0.0) + jnp.where(high, dk, 0.0)
+            x = raw_t[b, to, :].astype(F32)
+            inverse = inv_t[pl.ds((first + b) * text_rows + c * per_clip, per_clip), :]
+            along = jnp.sum(total * x, axis=-1, keepdims=True)
+            staged_text[b, 0, to, :] = inverse * (
+                total - x * (along * (inverse * inverse * (1.0 / HD)))
+            )
+            staged_text[b, 1, to, :] = jnp.where(low, me_b["before"][1], 0.0) + jnp.where(high, dv, 0.0)
+        me_b["before"] = (dk, dv)
+
+    def put_text(b):
+        put(staged_text.at[b, 0], gtk, b)
+        put(staged_text.at[b, 1], gtv, b)
+
+    def video_grads(b):
+        me_b = state[b]
+        eb = e_row[b]
+        inner_all = jnp.concatenate(me_b["inner"], axis=1)
+        ds = (eb.astype(F32) * (d_row[b] - inner_all)).astype(BF16)
+        dk = dot(ds, qs[b], (1, 0))
+        dv = dot(eb, gs[b], (1, 0))
+        eb = e_col[b]
+        ds = (eb.astype(F32) * (d_col[b] - me_b["inner"][0][:, mine])).astype(BF16)
+        att = me_b["att"] + dot(eb, vx[b], (0, 0))
+        dq = me_b["dq"] + dot(ds, kx[b, :, :HD], (0, 0))
+        turned = me_b["turned"]
+        staged[b, 0] = (att * turned).astype(BF16)
+        staged[b, 1] = norm_back(raw_q[b].astype(F32), dq * (turned * scale)).astype(BF16)
         staged[b, 2] = norm_back(raw_k[b].astype(F32), dk).astype(BF16)
         staged[b, 3] = dv.astype(BF16)
+
+    def put_rows(b):
         for a, target in enumerate((out, gq, gk, gv)):
-            put(staged.at[b, a], target, cols)
+            put(staged.at[b, a], target, b)
+
+    for b in range(count):
+        place(b)
+        video_scores(b)
+        for k in range(clips + 1):
+            text_scores(b, k)
+        close_sums(b)
+        for a in range(3):
+            fetches[3 * b + a].wait()
+        for k in range(clips + 1):
+            text_grads(b, k)
+        video_grads(b)
+        put_text(b)
+        put_rows(b)
     for copy in stores:
         copy.wait()
 
@@ -489,32 +531,32 @@
     work = count * video * (video + text_rows)
     return pl.pallas_call(
         functools.partial(line_kernel, first, count, clips),
-        in_specs=[held] * 7 + [remote] * 3 + [remote] * len(before),
+        in_specs=[held] * 8 + [remote] * 3 + [remote] * len(before),
         out_specs=[remote] * 6,
         out_shape=[
             jax.ShapeDtypeStruct((rows, width), dtype) for rows, dtype in zip(out_rows, out_types)
         ],
         scratch_shapes=[
             pltpu.VMEM((4 * count * length + SEG_ROWS, HD), BF16),
-            pltpu.VMEM((video, 2 * HD), BF16),
-            pltpu.VMEM((video, 2 * HD), BF16),
-            pltpu.VMEM((video, HD), BF16),
-            pltpu.VMEM((video, HD), BF16),
-            pltpu.VMEM((video, HD), BF16),
-            pltpu.VMEM((video, HD), BF16),
-            pltpu.VMEM((length, video), BF16),
-            pltpu.VMEM((video, length), BF16),
-            pltpu.VMEM((clips + 1, per_clip, half), BF16),
-            pltpu.VMEM((length, video), F32),
-            pltpu.VMEM((video, length), F32),
-            pltpu.VMEM((clips + 1, per_clip, half), F32),
+            pltpu.VMEM((count, video, 2 * HD), BF16),
+            pltpu.VMEM((count, video, 2 * HD), BF16),
+            pltpu.VMEM((count, video, HD), BF16),
+            pltpu.VMEM((count, video, HD), BF16),
+            pltpu.VMEM((count, video, HD), BF16),
+            pltpu.VMEM((count, video, HD), BF16),
+            pltpu.VMEM((count, length, video), BF16),
+            pltpu.VMEM((count, video, length), BF16),
+            pltpu.VMEM((count, clips + 1, per_clip, half), BF16),
+            pltpu.VMEM((count, length, video), F32),
+            pltpu.VMEM((count, video, length), F32),
+            pltpu.VMEM((count, clips + 1, per_clip, half), F32),
             pltpu.VMEM((count, length, HD), BF16),
             pltpu.VMEM((count, length, HD), BF16),
             pltpu.VMEM((count, text_rows, HD), BF16),
             pltpu.VMEM((count, 4, length, HD), BF16),
             pltpu.VMEM((count, 2, text_rows, HD), F32),
             pltpu.SemaphoreType.DMA((3 * count,)),
-            pltpu.SemaphoreType.DMA((count * (2 * clips + 4),)),
+            pltpu.SemaphoreType.DMA((6 * count,)),
         ],
         input_output_aliases={base + i: i for i in range(len(before))},
         compiler_params=pltpu.CompilerParams(vmem_limit_bytes=16 * 1024 * 1024),

time: 48.1 us -> 47.7 us (level)
  no operation moved by 1% of the time
where the time goes in v5:
time: 47.7 us; the launch traced here: 47.4 us
  waiting for transfers between devices  15.4 us (32%)
  starting transfers between devices  14.3 us (30%)
  Pallas kernels  13.8 us (29%)
  local copies, waits for them, and re-layouts  3.12 us (7%)
  between operations  0.76 us (2%)
    ppermute x8, waiting for transfers between devices, send(): return lax.ppermute(x, 'ctx', pairs)  15.4 us
    ppermute x8, starting transfers between devices, send(): return lax.ppermute(x, 'ctx', pairs)  14.3 us
    pallas_call x2, Pallas kernels, attend_line(): pl.pallas_call(functools.partial(line_kernel, first, count, clips), in_sp...  10.3 us
    unnamed x16, local copies, waits for them, and re-layouts  3.12 us
    pallas_call x1, Pallas kernels, pack(): pl.pallas_call(functools.partial(pack_kernel, chunks), out_shape=[jax.Sha...  2.11 us
    pallas_call x1, Pallas kernels, prepare_text(): pl.pallas_call(text_kernel, in_specs=[pl.BlockSpec(memory_space=pltpu.SME...  1.39 us
  transfers between devices with their start and end apart: 8, of which 4 were waited for; matrix products, arithmetic and copies ran while one was open for 0% of the time, Pallas kernels for 14%

profile of v5, /device:TPU:0, one launch (start us, length us, event | category | flops | bytes accessed | tf_op | source)
XLA Modules:
  0.0 47.4 jit_solution(9910761264947935107)
XLA Ops:
  0.6 0.0 copy-start.4
  0.7 2.1 %pack.1 = (bf16[1040,128]{1,0:T(8,128)(2,1)}, bf16[1040,128]{1,0:T(8,128)(2,1)}) custom-call(bf16[128,512]{1,0:T(8,128)(2,1)} %refs_8_.3, bf16[128,512]{1,0:T(8,128)(2,1)} %refs_9_.3, bf16[128,512]{1,0:T(8,128)(2,1)} %v_ref.1, bf16[128,512]{1,0:T(8,128)(2,1)} %g_ref.1, s32[1,128]{1,0:T(1,128)} %bitcast.1), custom_call_target="tpu_custom_call" | custom-call | tf_op jit(solution)/shard_map/pack/pallas_call | solution.py:53
  2.8 3.0 %collective-permute-start = (bf16[1040,128]{1,0:T(8,128)(2,1)}, bf16[1040,128]{1,0:T(8,128)(2,1)S(1)}, u32[]{:S(2)}, u32[]{:S(2)}) collective-permute-start(bf16[1040,128]{1,0:T(8,128)(2,1)} %get-tuple-element.18.refs_0_), channel_id=1, source_target_pairs={{0,4},{4,0},{8,12},{12,8},{1,5},{5,1},{9,13},{13,9},{2,6},{6,2},{1... | collective-permute-start | bytes 798728 | tf_op jit(solution)/shard_map/ppermute | solution.py:577
  5.8 2.6 %collective-permute-start.5 = (bf16[1040,128]{1,0:T(8,128)(2,1)}, bf16[1040,128]{1,0:T(8,128)(2,1)S(1)}, u32[]{:S(2)}, u32[]{:S(2)}) collective-permute-start(bf16[1040,128]{1,0:T(8,128)(2,1)} %get-tuple-element.22.refs_0_), channel_id=1, source_target_pairs={{0,8},{8,0},{4,12},{12,4},{1,9},{9,1},{5,13},{13,5},{2,10},{10,2},... | collective-permute-start | bytes 798728 | tf_op jit(solution)/shard_map/ppermute | solution.py:577
  8.4 0.3 collective-permute-start.1
  8.7 0.7 %collective-permute-start.6 = (bf16[1040,128]{1,0:T(8,128)(2,1)}, bf16[1040,128]{1,0:T(8,128)(2,1)S(1)}, u32[]{:S(2)}, u32[]{:S(2)}) collective-permute-start(bf16[1040,128]{1,0:T(8,128)(2,1)} %get-tuple-element.22.refs_0_), channel_id=1, source_target_pairs={{4,8},{8,4},{5,9},{9,5},{6,10},{10,6},{7,11},{11,7},{20,24},{24,20... | collective-permute-start | bytes 798728 | tf_op jit(solution)/shard_map/ppermute | solution.py:577
  9.4 4.4 %collective-permute-start.4 = (bf16[1040,128]{1,0:T(8,128)(2,1)}, bf16[1040,128]{1,0:T(8,128)(2,1)S(1)}, u32[]{:S(2)}, u32[]{:S(2)}) collective-permute-start(bf16[1040,128]{1,0:T(8,128)(2,1)} %get-tuple-element.22.refs_0_), channel_id=1, source_target_pairs={{0,4},{4,0},{8,12},{12,8},{1,5},{5,1},{9,13},{13,9},{2,6},{6,2},{1... | collective-permute-start | bytes 798728 | tf_op jit(solution)/shard_map/ppermute | solution.py:577
  13.8 1.2 %copy-done = bf16[1024,512]{1,0:T(8,128)(2,1)S(1)} copy-done((bf16[1024,512]{1,0:T(8,128)(2,1)S(1)}, bf16[1024,512]{1,0:T(8,128)(2,1)}, u32[]{:S(2)}) %copy-start) | copy-done | bytes 1048600
  15.1 1.2 %copy-done.2 = bf16[1024,512]{1,0:T(8,128)(2,1)S(1)} copy-done((bf16[1024,512]{1,0:T(8,128)(2,1)S(1)}, bf16[1024,512]{1,0:T(8,128)(2,1)}, u32[]{:S(2)}) %copy-start.2) | copy-done | bytes 1048600
  16.3 0.7 %copy-done.6 = s32[4]{0:T(128)S(1)} copy-done((s32[4]{0:T(128)S(1)}, s32[4]{0:T(128)}, u32[]{:S(2)}) %copy-start.6) | copy-done | bytes 40
  16.9 1.4 %prepare_text.1 = (bf16[4096,256]{1,0:T(8,128)(2,1)S(1)}, bf16[1024,512]{1,0:T(8,128)(2,1)S(1)}, f32[4096,128]{1,0:T(8,128)S(1)}) custom-call(s32[4]{0:T(128)S(1)} %copy-done.6, bf16[1024,512]{1,0:T(8,128)(2,1)S(1)} %copy-done, bf16[1024,512]{1,0:T(8,128)(2,1)S(1)} %copy-done.2), custom_call_target="tpu_custom_call" | custom-call | flops 4194304 | bytes 3145728 | tf_op jit(solution)/shard_map/prepare_text/pallas_call | solution.py:304
  18.3 0.5 collective-permute-done.refs_1_
  18.8 8.9 %collective-permute-done.5.refs_2_ = bf16[1040,128]{1,0:T(8,128)(2,1)S(1)} collective-permute-done((bf16[1040,128]{1,0:T(8,128)(2,1)}, bf16[1040,128]{1,0:T(8,128)(2,1)S(1)}, u32[]{:S(2)}, u32[]{:S(2)}) %collective-permute-start.5) | collective-permute-done | bytes 266272 | tf_op jit(solution)/shard_map/ppermute | solution.py:577
  27.7 1.3 %collective-permute-start.7 = (bf16[1040,128]{1,0:T(8,128)(2,1)S(1)}, bf16[1040,128]{1,0:T(8,128)(2,1)S(1)}, u32[]{:S(2)}, u32[]{:S(2)}) collective-permute-start(bf16[1040,128]{1,0:T(8,128)(2,1)S(1)} %collective-permute-done.5.refs_2_), channel_id=1, source_target_pairs={{4,0},{8,12},{5,1},{9,13},{6,2},{10,14},{7,3},{11,15},{20,16},{24,... | collective-permute-start | bytes 798728 | tf_op jit(solution)/shard_map/ppermute | solution.py:577
  29.0 0.7 %collective-permute-start.2 = (bf16[1040,128]{1,0:T(8,128)(2,1)S(1)}, bf16[1040,128]{1,0:T(8,128)(2,1)S(1)}, u32[]{:S(2)}, u32[]{:S(2)}) collective-permute-start(bf16[1040,128]{1,0:T(8,128)(2,1)S(1)} %copy-done.5), channel_id=1, source_target_pairs={{4,8},{8,4},{5,9},{9,5},{6,10},{10,6},{7,11},{11,7},{20,24},{24,20... | collective-permute-start | bytes 798728 | tf_op jit(solution)/shard_map/ppermute | solution.py:577
  29.7 3.7 %collective-permute-done.1.refs_2_ = bf16[1040,128]{1,0:T(8,128)(2,1)S(1)} collective-permute-done((bf16[1040,128]{1,0:T(8,128)(2,1)}, bf16[1040,128]{1,0:T(8,128)(2,1)S(1)}, u32[]{:S(2)}, u32[]{:S(2)}) %collective-permute-start.1) | collective-permute-done | bytes 266272 | tf_op jit(solution)/shard_map/ppermute | solution.py:577
  33.4 1.3 %collective-permute-start.3 = (bf16[1040,128]{1,0:T(8,128)(2,1)S(1)}, bf16[1040,128]{1,0:T(8,128)(2,1)S(1)}, u32[]{:S(2)}, u32[]{:S(2)}) collective-permute-start(bf16[1040,128]{1,0:T(8,128)(2,1)S(1)} %collective-permute-done.1.refs_2_), channel_id=1, source_target_pairs={{4,0},{8,12},{5,1},{9,13},{6,2},{10,14},{7,3},{11,15},{20,16},{24,... | collective-permute-start | bytes 798728 | tf_op jit(solution)/shard_map/ppermute | solution.py:577
  34.7 0.0 collective-permute-done.6.refs_3_
  34.7 0.0 collective-permute-done.4.refs_1_
  34.7 2.4 %collective-permute-done.7.refs_4_ = bf16[1040,128]{1,0:T(8,128)(2,1)S(1)} collective-permute-done((bf16[1040,128]{1,0:T(8,128)(2,1)S(1)}, bf16[1040,128]{1,0:T(8,128)(2,1)S(1)}, u32[]{:S(2)}, u32[]{:S(2)}) %collective-permute-start.7) | collective-permute-done | bytes 266272 | tf_op jit(solution)/shard_map/ppermute | solution.py:577
  37.1 5.1 %attend_line.2 = (bf16[128,512]{1,0:T(8,128)(2,1)}, bf16[128,512]{1,0:T(8,128)(2,1)}, bf16[128,512]{1,0:T(8,128)(2,1)}, bf16[128,512]{1,0:T(8,128)(2,1)}, f32[1024,512]{1,0:T(8,128)}, /*index=5*/f32[1024,512]{1,0:T(8,128)}) custom-call(bf16[1040,128]{1,0:T(8,128)(2,1)S(1)} %copy-done.7, bf16[1040,128]{1,0:T(8,128)(2,1)S(1)} %collective-permute-done.4.refs_1_, ...), custom_call_target="tpu_custom_call" | custom-call | flops 2415919104 | bytes 4194304 | tf_op jit(solution)/shard_map/attend_line/pallas_call | solution.py:532
  42.2 0.0 collective-permute-done.2.refs_3_
  42.2 0.0 collective-permute-done.3.refs_4_
  42.3 5.2 %attend_line.3 = (bf16[128,512]{1,0:T(8,128)(2,1)}, bf16[128,512]{1,0:T(8,128)(2,1)}, bf16[128,512]{1,0:T(8,128)(2,1)}, bf16[128,512]{1,0:T(8,128)(2,1)}, f32[1024,512]{1,0:T(8,128)}, /*index=5*/f32[1024,512]{1,0:T(8,128)}) custom-call(bf16[1040,128]{1,0:T(8,128)(2,1)S(1)} %copy-done.5, ...), custom_call_target="tpu_custom_call", output_to_operand_aliasing={{0}: (11, {}), {1}: (12, {}), {2}: (13, {}), {3}: (14, {}),... | custom-call | flops 2415919104 | bytes 4194304 | tf_op jit(solution)/shard_map/attend_line/pallas_call | solution.py:532
  (12 shorter events, 0.0 us)
Async XLA Ops:
  0.6 36.4 %copy-start.4 = (bf16[128,512]{1,0:T(8,128)(2,1)S(1)}, bf16[128,512]{1,0:T(8,128)(2,1)}, u32[]{:S(2)}) copy-start(bf16[128,512]{1,0:T(8,128)(2,1)} %refs_9_.3) | copy-start | bytes 393220
  0.6 36.4 %copy-start.3 = (bf16[128,512]{1,0:T(8,128)(2,1)S(1)}, bf16[128,512]{1,0:T(8,128)(2,1)}, u32[]{:S(2)}) copy-start(bf16[128,512]{1,0:T(8,128)(2,1)} %refs_8_.3) | copy-start | bytes 393220
  2.8 16.0 %collective-permute-start = (bf16[1040,128]{1,0:T(8,128)(2,1)}, bf16[1040,128]{1,0:T(8,128)(2,1)S(1)}, u32[]{:S(2)}, u32[]{:S(2)}) collective-permute-start(bf16[1040,128]{1,0:T(8,128)(2,1)} %get-tuple-element.18.refs_0_), channel_id=1, source_target_pairs={{0,4},{4,0},{8,12},{12,8},{1,5},{5,1},{9,13},{13,9},{2,6},{6,2},{1... | collective-permute-start | bytes 798728 | tf_op jit(solution)/shard_map/ppermute | solution.py:577
  5.8 21.9 %collective-permute-start.5 = (bf16[1040,128]{1,0:T(8,128)(2,1)}, bf16[1040,128]{1,0:T(8,128)(2,1)S(1)}, u32[]{:S(2)}, u32[]{:S(2)}) collective-permute-start(bf16[1040,128]{1,0:T(8,128)(2,1)} %get-tuple-element.22.refs_0_), channel_id=1, source_target_pairs={{0,8},{8,0},{4,12},{12,4},{1,9},{9,1},{5,13},{13,5},{2,10},{10,2},... | collective-permute-start | bytes 798728 | tf_op jit(solution)/shard_map/ppermute | solution.py:577
  8.4 25.0 %collective-permute-start.1 = (bf16[1040,128]{1,0:T(8,128)(2,1)}, bf16[1040,128]{1,0:T(8,128)(2,1)S(1)}, u32[]{:S(2)}, u32[]{:S(2)}) collective-permute-start(bf16[1040,128]{1,0:T(8,128)(2,1)} %get-tuple-element.18.refs_0_), channel_id=1, source_target_pairs={{0,8},{8,0},{4,12},{12,4},{1,9},{9,1},{5,13},{13,5},{2,10},{10,2},... | collective-permute-start | bytes 798728 | tf_op jit(solution)/shard_map/ppermute | solution.py:577
  8.7 26.0 %collective-permute-start.6 = (bf16[1040,128]{1,0:T(8,128)(2,1)}, bf16[1040,128]{1,0:T(8,128)(2,1)S(1)}, u32[]{:S(2)}, u32[]{:S(2)}) collective-permute-start(bf16[1040,128]{1,0:T(8,128)(2,1)} %get-tuple-element.22.refs_0_), channel_id=1, source_target_pairs={{4,8},{8,4},{5,9},{9,5},{6,10},{10,6},{7,11},{11,7},{20,24},{24,20... | collective-permute-start | bytes 798728 | tf_op jit(solution)/shard_map/ppermute | solution.py:577
  9.4 25.3 %collective-permute-start.4 = (bf16[1040,128]{1,0:T(8,128)(2,1)}, bf16[1040,128]{1,0:T(8,128)(2,1)S(1)}, u32[]{:S(2)}, u32[]{:S(2)}) collective-permute-start(bf16[1040,128]{1,0:T(8,128)(2,1)} %get-tuple-element.22.refs_0_), channel_id=1, source_target_pairs={{0,4},{4,0},{8,12},{12,8},{1,5},{5,1},{9,13},{13,9},{2,6},{6,2},{1... | collective-permute-start | bytes 798728 | tf_op jit(solution)/shard_map/ppermute | solution.py:577
  13.8 1.2 %copy-start = (bf16[1024,512]{1,0:T(8,128)(2,1)S(1)}, bf16[1024,512]{1,0:T(8,128)(2,1)}, u32[]{:S(2)}) copy-start(bf16[1024,512]{1,0:T(8,128)(2,1)} %refs_10_.3) | copy-start | bytes 3145732
  15.1 1.2 %copy-start.2 = (bf16[1024,512]{1,0:T(8,128)(2,1)S(1)}, bf16[1024,512]{1,0:T(8,128)(2,1)}, u32[]{:S(2)}) copy-start(bf16[1024,512]{1,0:T(8,128)(2,1)} %tv_ref.1) | copy-start | bytes 3145732
  16.3 0.7 %copy-start.6 = (s32[4]{0:T(128)S(1)}, s32[4]{0:T(128)}, u32[]{:S(2)}) copy-start(s32[4]{0:T(128)} %len_ref.1) | copy-start | bytes 52
  16.9 12.1 %copy-start.5 = (bf16[1040,128]{1,0:T(8,128)(2,1)S(1)}, bf16[1040,128]{1,0:T(8,128)(2,1)}, u32[]{:S(2)}) copy-start(bf16[1040,128]{1,0:T(8,128)(2,1)} %get-tuple-element.18.refs_0_) | copy-start | bytes 798724
  16.9 20.1 %copy-start.1 = (bf16[1024,512]{1,0:T(8,128)(2,1)S(1)}, bf16[1024,512]{1,0:T(8,128)(2,1)}, u32[]{:S(2)}) copy-start(bf16[1024,512]{1,0:T(8,128)(2,1)} %refs_10_.3) | copy-start | bytes 3145732
  16.9 20.1 %copy-start.7 = (bf16[1040,128]{1,0:T(8,128)(2,1)S(1)}, bf16[1040,128]{1,0:T(8,128)(2,1)}, u32[]{:S(2)}) copy-start(bf16[1040,128]{1,0:T(8,128)(2,1)} %get-tuple-element.22.refs_0_) | copy-start | bytes 798724
  27.7 9.3 %collective-permute-start.7 = (bf16[1040,128]{1,0:T(8,128)(2,1)S(1)}, bf16[1040,128]{1,0:T(8,128)(2,1)S(1)}, u32[]{:S(2)}, u32[]{:S(2)}) collective-permute-start(bf16[1040,128]{1,0:T(8,128)(2,1)S(1)} %collective-permute-done.5.refs_2_), channel_id=1, source_target_pairs={{4,0},{8,12},{5,1},{9,13},{6,2},{10,14},{7,3},{11,15},{20,16},{24,... | collective-permute-start | bytes 798728 | tf_op jit(solution)/shard_map/ppermute | solution.py:577
  29.0 13.2 %collective-permute-start.2 = (bf16[1040,128]{1,0:T(8,128)(2,1)S(1)}, bf16[1040,128]{1,0:T(8,128)(2,1)S(1)}, u32[]{:S(2)}, u32[]{:S(2)}) collective-permute-start(bf16[1040,128]{1,0:T(8,128)(2,1)S(1)} %copy-done.5), channel_id=1, source_target_pairs={{4,8},{8,4},{5,9},{9,5},{6,10},{10,6},{7,11},{11,7},{20,24},{24,20... | collective-permute-start | bytes 798728 | tf_op jit(solution)/shard_map/ppermute | solution.py:577
  33.4 8.9 %collective-permute-start.3 = (bf16[1040,128]{1,0:T(8,128)(2,1)S(1)}, bf16[1040,128]{1,0:T(8,128)(2,1)S(1)}, u32[]{:S(2)}, u32[]{:S(2)}) collective-permute-start(bf16[1040,128]{1,0:T(8,128)(2,1)S(1)} %collective-permute-done.1.refs_2_), channel_id=1, source_target_pairs={{4,0},{8,12},{5,1},{9,13},{6,2},{10,14},{7,3},{11,15},{20,16},{24,... | collective-permute-start | bytes 798728 | tf_op jit(solution)/shard_map/ppermute | solution.py:577

commit v6 on v5

--- a/solution.py
+++ b/solution.py
@@ -587,9 +587,12 @@
             return lax.optimization_barrier((x, *others))[0]
 
         a, b = payloads
-        skip_a, near_a = send(a, across), send(a, outer)
-        skip_b, near_b = send(b, across), send(b, outer)
-        far_a, far_b = send(a, middle), send(b, middle)
+        skip_a = send(a, across)
+        near_a = send(after(a, *text), outer)
+        skip_b = send(after(b, *text), across)
+        near_b = send(b, outer)
+        far_a = send(a, middle)
+        far_b = send(after(b, near_b), middle)
         last_a = send(after(skip_a, near_b, *text), outward)
         last_b = send(skip_b, outward)
         pieces = [(a, near_a, skip_a, far_a, last_a), (b, near_b, skip_b, far_b, last_b)]

time: 47.7 us -> 47.5 us (level)
  no operation moved by 1% of the time
where the time goes in v6:
time: 47.5 us; the launch traced here: 47.3 us
  waiting for transfers between devices  15.2 us (32%)
  starting transfers between devices  14.4 us (30%)
  Pallas kernels  13.8 us (29%)
  local copies, waits for them, and re-layouts  3.12 us (7%)
  between operations  0.74 us (2%)
    ppermute x8, waiting for transfers between devices, send(): return lax.ppermute(x, 'ctx', pairs)  15.2 us
    ppermute x8, starting transfers between devices, send(): return lax.ppermute(x, 'ctx', pairs)  14.4 us
    pallas_call x2, Pallas kernels, attend_line(): pl.pallas_call(functools.partial(line_kernel, first, count, clips), in_sp...  10.3 us
    unnamed x16, local copies, waits for them, and re-layouts  3.12 us
    pallas_call x1, Pallas kernels, pack(): pl.pallas_call(functools.partial(pack_kernel, chunks), out_shape=[jax.Sha...  2.11 us
    pallas_call x1, Pallas kernels, prepare_text(): pl.pallas_call(text_kernel, in_specs=[pl.BlockSpec(memory_space=pltpu.SME...  1.39 us
  transfers between devices with their start and end apart: 8, of which 4 were waited for; matrix products, arithmetic and copies ran while one was open for 0% of the time, Pallas kernels for 14%

profile of v6, /device:TPU:0, one launch (start us, length us, event | category | flops | bytes accessed | tf_op | source)
XLA Modules:
  0.0 47.3 jit_solution(15946884312020047667)
XLA Ops:
  0.6 0.0 copy-start.4
  0.7 2.1 %pack.1 = (bf16[1040,128]{1,0:T(8,128)(2,1)}, bf16[1040,128]{1,0:T(8,128)(2,1)}) custom-call(bf16[128,512]{1,0:T(8,128)(2,1)} %refs_8_.3, bf16[128,512]{1,0:T(8,128)(2,1)} %refs_9_.3, bf16[128,512]{1,0:T(8,128)(2,1)} %v_ref.1, bf16[128,512]{1,0:T(8,128)(2,1)} %g_ref.1, s32[1,128]{1,0:T(1,128)} %bitcast.1), custom_call_target="tpu_custom_call" | custom-call | tf_op jit(solution)/shard_map/pack/pallas_call | solution.py:53
  2.8 3.0 %collective-permute-start = (bf16[1040,128]{1,0:T(8,128)(2,1)}, bf16[1040,128]{1,0:T(8,128)(2,1)S(1)}, u32[]{:S(2)}, u32[]{:S(2)}) collective-permute-start(bf16[1040,128]{1,0:T(8,128)(2,1)} %get-tuple-element.26.refs_0_), channel_id=1, source_target_pairs={{0,4},{4,0},{8,12},{12,8},{1,5},{5,1},{9,13},{13,9},{2,6},{6,2},{1... | collective-permute-start | bytes 798728 | tf_op jit(solution)/shard_map/ppermute | solution.py:577
  5.8 2.6 %collective-permute-start.5 = (bf16[1040,128]{1,0:T(8,128)(2,1)}, bf16[1040,128]{1,0:T(8,128)(2,1)S(1)}, u32[]{:S(2)}, u32[]{:S(2)}) collective-permute-start(bf16[1040,128]{1,0:T(8,128)(2,1)} %get-tuple-element.28.refs_0_), channel_id=1, source_target_pairs={{0,8},{8,0},{4,12},{12,4},{1,9},{9,1},{5,13},{13,5},{2,10},{10,2},... | collective-permute-start | bytes 798728 | tf_op jit(solution)/shard_map/ppermute | solution.py:577
  8.4 1.2 %copy-done = bf16[1024,512]{1,0:T(8,128)(2,1)S(1)} copy-done((bf16[1024,512]{1,0:T(8,128)(2,1)S(1)}, bf16[1024,512]{1,0:T(8,128)(2,1)}, u32[]{:S(2)}) %copy-start) | copy-done | bytes 1048600
  9.6 1.2 %copy-done.2 = bf16[1024,512]{1,0:T(8,128)(2,1)S(1)} copy-done((bf16[1024,512]{1,0:T(8,128)(2,1)S(1)}, bf16[1024,512]{1,0:T(8,128)(2,1)}, u32[]{:S(2)}) %copy-start.2) | copy-done | bytes 1048600
  10.8 0.7 %copy-done.6 = s32[4]{0:T(128)S(1)} copy-done((s32[4]{0:T(128)S(1)}, s32[4]{0:T(128)}, u32[]{:S(2)}) %copy-start.6) | copy-done | bytes 40
  11.5 1.4 %prepare_text.1 = (bf16[4096,256]{1,0:T(8,128)(2,1)S(1)}, bf16[1024,512]{1,0:T(8,128)(2,1)S(1)}, f32[4096,128]{1,0:T(8,128)S(1)}) custom-call(s32[4]{0:T(128)S(1)} %copy-done.6, bf16[1024,512]{1,0:T(8,128)(2,1)S(1)} %copy-done, bf16[1024,512]{1,0:T(8,128)(2,1)S(1)} %copy-done.2), custom_call_target="tpu_custom_call" | custom-call | flops 4194304 | bytes 3145728 | tf_op jit(solution)/shard_map/prepare_text/pallas_call | solution.py:304
  12.9 0.4 collective-permute-start.1
  13.3 0.7 %collective-permute-start.6 = (bf16[1040,128]{1,0:T(8,128)(2,1)S(1)}, bf16[1040,128]{1,0:T(8,128)(2,1)S(1)}, u32[]{:S(2)}, u32[]{:S(2)}) collective-permute-start(bf16[1040,128]{1,0:T(8,128)(2,1)S(1)} %copy-done.7), channel_id=1, source_target_pairs={{4,8},{8,4},{5,9},{9,5},{6,10},{10,6},{7,11},{11,7},{20,24},{24,20... | collective-permute-start | bytes 798728 | tf_op jit(solution)/shard_map/ppermute | solution.py:577
  14.0 4.4 %collective-permute-start.4 = (bf16[1040,128]{1,0:T(8,128)(2,1)S(1)}, bf16[1040,128]{1,0:T(8,128)(2,1)S(1)}, u32[]{:S(2)}, u32[]{:S(2)}) collective-permute-start(bf16[1040,128]{1,0:T(8,128)(2,1)S(1)} %copy-done.7), channel_id=1, source_target_pairs={{0,4},{4,0},{8,12},{12,8},{1,5},{5,1},{9,13},{13,9},{2,6},{6,2},{1... | collective-permute-start | bytes 798728 | tf_op jit(solution)/shard_map/ppermute | solution.py:577
  18.4 0.0 collective-permute-done.refs_1_
  18.4 7.1 %collective-permute-done.5.refs_2_ = bf16[1040,128]{1,0:T(8,128)(2,1)S(1)} collective-permute-done((bf16[1040,128]{1,0:T(8,128)(2,1)}, bf16[1040,128]{1,0:T(8,128)(2,1)S(1)}, u32[]{:S(2)}, u32[]{:S(2)}) %collective-permute-start.5) | collective-permute-done | bytes 266272 | tf_op jit(solution)/shard_map/ppermute | solution.py:577
  25.5 1.3 %collective-permute-start.7 = (bf16[1040,128]{1,0:T(8,128)(2,1)S(1)}, bf16[1040,128]{1,0:T(8,128)(2,1)S(1)}, u32[]{:S(2)}, u32[]{:S(2)}) collective-permute-start(bf16[1040,128]{1,0:T(8,128)(2,1)S(1)} %collective-permute-done.5.refs_2_), channel_id=1, source_target_pairs={{4,0},{8,12},{5,1},{9,13},{6,2},{10,14},{7,3},{11,15},{20,16},{24,... | collective-permute-start | bytes 798728 | tf_op jit(solution)/shard_map/ppermute | solution.py:577
  26.8 0.7 %collective-permute-start.2 = (bf16[1040,128]{1,0:T(8,128)(2,1)S(1)}, bf16[1040,128]{1,0:T(8,128)(2,1)S(1)}, u32[]{:S(2)}, u32[]{:S(2)}) collective-permute-start(bf16[1040,128]{1,0:T(8,128)(2,1)S(1)} %copy-done.5), channel_id=1, source_target_pairs={{4,8},{8,4},{5,9},{9,5},{6,10},{10,6},{7,11},{11,7},{20,24},{24,20... | collective-permute-start | bytes 798728 | tf_op jit(solution)/shard_map/ppermute | solution.py:577
  27.5 4.6 %collective-permute-done.1.refs_2_ = bf16[1040,128]{1,0:T(8,128)(2,1)S(1)} collective-permute-done((bf16[1040,128]{1,0:T(8,128)(2,1)S(1)}, bf16[1040,128]{1,0:T(8,128)(2,1)S(1)}, u32[]{:S(2)}, u32[]{:S(2)}) %collective-permute-start.1) | collective-permute-done | bytes 266272 | tf_op jit(solution)/shard_map/ppermute | solution.py:577
  32.1 1.3 %collective-permute-start.3 = (bf16[1040,128]{1,0:T(8,128)(2,1)S(1)}, bf16[1040,128]{1,0:T(8,128)(2,1)S(1)}, u32[]{:S(2)}, u32[]{:S(2)}) collective-permute-start(bf16[1040,128]{1,0:T(8,128)(2,1)S(1)} %collective-permute-done.1.refs_2_), channel_id=1, source_target_pairs={{4,0},{8,12},{5,1},{9,13},{6,2},{10,14},{7,3},{11,15},{20,16},{24,... | collective-permute-start | bytes 798728 | tf_op jit(solution)/shard_map/ppermute | solution.py:577
  33.4 0.0 collective-permute-done.6.refs_3_
  33.4 0.0 collective-permute-done.4.refs_1_
  33.4 1.8 %collective-permute-done.7.refs_4_ = bf16[1040,128]{1,0:T(8,128)(2,1)S(1)} collective-permute-done((bf16[1040,128]{1,0:T(8,128)(2,1)S(1)}, bf16[1040,128]{1,0:T(8,128)(2,1)S(1)}, u32[]{:S(2)}, u32[]{:S(2)}) %collective-permute-start.7) | collective-permute-done | bytes 266272 | tf_op jit(solution)/shard_map/ppermute | solution.py:577
  35.2 5.1 %attend_line.2 = (bf16[128,512]{1,0:T(8,128)(2,1)}, bf16[128,512]{1,0:T(8,128)(2,1)}, bf16[128,512]{1,0:T(8,128)(2,1)}, bf16[128,512]{1,0:T(8,128)(2,1)}, f32[1024,512]{1,0:T(8,128)}, /*index=5*/f32[1024,512]{1,0:T(8,128)}) custom-call(bf16[1040,128]{1,0:T(8,128)(2,1)S(1)} %copy-done.7, bf16[1040,128]{1,0:T(8,128)(2,1)S(1)} %collective-permute-done.4.refs_1_, ...), custom_call_target="tpu_custom_call" | custom-call | flops 2415919104 | bytes 4194304 | tf_op jit(solution)/shard_map/attend_line/pallas_call | solution.py:532
  40.4 0.0 collective-permute-done.2.refs_3_
  40.4 1.7 %collective-permute-done.3.refs_4_ = bf16[1040,128]{1,0:T(8,128)(2,1)S(1)} collective-permute-done((bf16[1040,128]{1,0:T(8,128)(2,1)S(1)}, bf16[1040,128]{1,0:T(8,128)(2,1)S(1)}, u32[]{:S(2)}, u32[]{:S(2)}) %collective-permute-start.3) | collective-permute-done | bytes 266272 | tf_op jit(solution)/shard_map/ppermute | solution.py:577
  42.1 5.2 %attend_line.3 = (bf16[128,512]{1,0:T(8,128)(2,1)}, bf16[128,512]{1,0:T(8,128)(2,1)}, bf16[128,512]{1,0:T(8,128)(2,1)}, bf16[128,512]{1,0:T(8,128)(2,1)}, f32[1024,512]{1,0:T(8,128)}, /*index=5*/f32[1024,512]{1,0:T(8,128)}) custom-call(bf16[1040,128]{1,0:T(8,128)(2,1)S(1)} %copy-done.5, ...), custom_call_target="tpu_custom_call", output_to_operand_aliasing={{0}: (11, {}), {1}: (12, {}), {2}: (13, {}), {3}: (14, {}),... | custom-call | flops 2415919104 | bytes 4194304 | tf_op jit(solution)/shard_map/attend_line/pallas_call | solution.py:532
  (12 shorter events, 0.0 us)
Async XLA Ops:
  0.6 34.6 %copy-start.4 = (bf16[128,512]{1,0:T(8,128)(2,1)S(1)}, bf16[128,512]{1,0:T(8,128)(2,1)}, u32[]{:S(2)}) copy-start(bf16[128,512]{1,0:T(8,128)(2,1)} %refs_9_.3) | copy-start | bytes 393220
  0.6 34.6 %copy-start.3 = (bf16[128,512]{1,0:T(8,128)(2,1)S(1)}, bf16[128,512]{1,0:T(8,128)(2,1)}, u32[]{:S(2)}) copy-start(bf16[128,512]{1,0:T(8,128)(2,1)} %refs_8_.3) | copy-start | bytes 393220
  2.8 15.7 %collective-permute-start = (bf16[1040,128]{1,0:T(8,128)(2,1)}, bf16[1040,128]{1,0:T(8,128)(2,1)S(1)}, u32[]{:S(2)}, u32[]{:S(2)}) collective-permute-start(bf16[1040,128]{1,0:T(8,128)(2,1)} %get-tuple-element.26.refs_0_), channel_id=1, source_target_pairs={{0,4},{4,0},{8,12},{12,8},{1,5},{5,1},{9,13},{13,9},{2,6},{6,2},{1... | collective-permute-start | bytes 798728 | tf_op jit(solution)/shard_map/ppermute | solution.py:577
  5.8 19.7 %collective-permute-start.5 = (bf16[1040,128]{1,0:T(8,128)(2,1)}, bf16[1040,128]{1,0:T(8,128)(2,1)S(1)}, u32[]{:S(2)}, u32[]{:S(2)}) collective-permute-start(bf16[1040,128]{1,0:T(8,128)(2,1)} %get-tuple-element.28.refs_0_), channel_id=1, source_target_pairs={{0,8},{8,0},{4,12},{12,4},{1,9},{9,1},{5,13},{13,5},{2,10},{10,2},... | collective-permute-start | bytes 798728 | tf_op jit(solution)/shard_map/ppermute | solution.py:577
  8.4 1.2 %copy-start = (bf16[1024,512]{1,0:T(8,128)(2,1)S(1)}, bf16[1024,512]{1,0:T(8,128)(2,1)}, u32[]{:S(2)}) copy-start(bf16[1024,512]{1,0:T(8,128)(2,1)} %refs_10_.3) | copy-start | bytes 3145732
  9.6 1.2 %copy-start.2 = (bf16[1024,512]{1,0:T(8,128)(2,1)S(1)}, bf16[1024,512]{1,0:T(8,128)(2,1)}, u32[]{:S(2)}) copy-start(bf16[1024,512]{1,0:T(8,128)(2,1)} %tv_ref.1) | copy-start | bytes 3145732
  10.8 0.7 %copy-start.6 = (s32[4]{0:T(128)S(1)}, s32[4]{0:T(128)}, u32[]{:S(2)}) copy-start(s32[4]{0:T(128)} %len_ref.1) | copy-start | bytes 52
  11.5 1.4 %copy-start.5 = (bf16[1040,128]{1,0:T(8,128)(2,1)S(1)}, bf16[1040,128]{1,0:T(8,128)(2,1)}, u32[]{:S(2)}) copy-start(bf16[1040,128]{1,0:T(8,128)(2,1)} %get-tuple-element.26.refs_0_) | copy-start | bytes 798724
  11.5 1.8 %copy-start.7 = (bf16[1040,128]{1,0:T(8,128)(2,1)S(1)}, bf16[1040,128]{1,0:T(8,128)(2,1)}, u32[]{:S(2)}) copy-start(bf16[1040,128]{1,0:T(8,128)(2,1)} %get-tuple-element.28.refs_0_) | copy-start | bytes 798724
  11.5 23.7 %copy-start.1 = (bf16[1024,512]{1,0:T(8,128)(2,1)S(1)}, bf16[1024,512]{1,0:T(8,128)(2,1)}, u32[]{:S(2)}) copy-start(bf16[1024,512]{1,0:T(8,128)(2,1)} %refs_10_.3) | copy-start | bytes 3145732
  12.9 19.2 %collective-permute-start.1 = (bf16[1040,128]{1,0:T(8,128)(2,1)S(1)}, bf16[1040,128]{1,0:T(8,128)(2,1)S(1)}, u32[]{:S(2)}, u32[]{:S(2)}) collective-permute-start(bf16[1040,128]{1,0:T(8,128)(2,1)S(1)} %copy-done.5), channel_id=1, source_target_pairs={{0,8},{8,0},{4,12},{12,4},{1,9},{9,1},{5,13},{13,5},{2,10},{10,2},... | collective-permute-start | bytes 798728 | tf_op jit(solution)/shard_map/ppermute | solution.py:577
  13.3 20.1 %collective-permute-start.6 = (bf16[1040,128]{1,0:T(8,128)(2,1)S(1)}, bf16[1040,128]{1,0:T(8,128)(2,1)S(1)}, u32[]{:S(2)}, u32[]{:S(2)}) collective-permute-start(bf16[1040,128]{1,0:T(8,128)(2,1)S(1)} %copy-done.7), channel_id=1, source_target_pairs={{4,8},{8,4},{5,9},{9,5},{6,10},{10,6},{7,11},{11,7},{20,24},{24,20... | collective-permute-start | bytes 798728 | tf_op jit(solution)/shard_map/ppermute | solution.py:577
  14.0 19.4 %collective-permute-start.4 = (bf16[1040,128]{1,0:T(8,128)(2,1)S(1)}, bf16[1040,128]{1,0:T(8,128)(2,1)S(1)}, u32[]{:S(2)}, u32[]{:S(2)}) collective-permute-start(bf16[1040,128]{1,0:T(8,128)(2,1)S(1)} %copy-done.7), channel_id=1, source_target_pairs={{0,4},{4,0},{8,12},{12,8},{1,5},{5,1},{9,13},{13,9},{2,6},{6,2},{1... | collective-permute-start | bytes 798728 | tf_op jit(solution)/shard_map/ppermute | solution.py:577
  25.5 9.7 %collective-permute-start.7 = (bf16[1040,128]{1,0:T(8,128)(2,1)S(1)}, bf16[1040,128]{1,0:T(8,128)(2,1)S(1)}, u32[]{:S(2)}, u32[]{:S(2)}) collective-permute-start(bf16[1040,128]{1,0:T(8,128)(2,1)S(1)} %collective-permute-done.5.refs_2_), channel_id=1, source_target_pairs={{4,0},{8,12},{5,1},{9,13},{6,2},{10,14},{7,3},{11,15},{20,16},{24,... | collective-permute-start | bytes 798728 | tf_op jit(solution)/shard_map/ppermute | solution.py:577
  26.8 13.6 %collective-permute-start.2 = (bf16[1040,128]{1,0:T(8,128)(2,1)S(1)}, bf16[1040,128]{1,0:T(8,128)(2,1)S(1)}, u32[]{:S(2)}, u32[]{:S(2)}) collective-permute-start(bf16[1040,128]{1,0:T(8,128)(2,1)S(1)} %copy-done.5), channel_id=1, source_target_pairs={{4,8},{8,4},{5,9},{9,5},{6,10},{10,6},{7,11},{11,7},{20,24},{24,20... | collective-permute-start | bytes 798728 | tf_op jit(solution)/shard_map/ppermute | solution.py:577
  32.1 10.0 %collective-permute-start.3 = (bf16[1040,128]{1,0:T(8,128)(2,1)S(1)}, bf16[1040,128]{1,0:T(8,128)(2,1)S(1)}, u32[]{:S(2)}, u32[]{:S(2)}) collective-permute-start(bf16[1040,128]{1,0:T(8,128)(2,1)S(1)} %collective-permute-done.1.refs_2_), channel_id=1, source_target_pairs={{4,0},{8,12},{5,1},{9,13},{6,2},{10,14},{7,3},{11,15},{20,16},{24,... | collective-permute-start | bytes 798728 | tf_op jit(solution)/shard_map/ppermute | solution.py:577

commit v7 on v6

--- a/solution.py
+++ b/solution.py
@@ -588,10 +588,10 @@
 
         a, b = payloads
         skip_a = send(a, across)
+        near_b = send(b, outer)
         near_a = send(after(a, *text), outer)
         skip_b = send(after(b, *text), across)
-        near_b = send(b, outer)
-        far_a = send(a, middle)
+        far_a = send(after(a, near_b), middle)
         far_b = send(after(b, near_b), middle)
         last_a = send(after(skip_a, near_b, *text), outward)
         last_b = send(skip_b, outward)

time: 47.5 us -> 47.5 us (level)
  starting transfers between devices: 14.4 us -> 10.1 us
  waiting for transfers between devices: 15.2 us -> 19.5 us
    ppermute x8, starting transfers between devices: 14.4 us -> 10.1 us  [send(): return lax.ppermute(x, 'ctx', pairs)]
    ppermute x8, waiting for transfers between devices: 15.2 us -> 19.5 us  [send(): return lax.ppermute(x, 'ctx', pairs)]
  transfers between devices with their start and end apart: 8 -> 8, of which waited for: 4 -> 5; matrix products, arithmetic and copies ran while one was open for 0% -> 0% of each run, Pallas kernels for 14% -> 14%
where the time goes in v7:
time: 47.5 us; the launch traced here: 47.3 us
  waiting for transfers between devices  19.5 us (41%)
  Pallas kernels  13.8 us (29%)
  starting transfers between devices  10.1 us (21%)
  local copies, waits for them, and re-layouts  3.12 us (7%)
  between operations  0.74 us (2%)
    ppermute x8, waiting for transfers between devices, send(): return lax.ppermute(x, 'ctx', pairs)  19.5 us
    pallas_call x2, Pallas kernels, attend_line(): pl.pallas_call(functools.partial(line_kernel, first, count, clips), in_sp...  10.3 us
    ppermute x8, starting transfers between devices, send(): return lax.ppermute(x, 'ctx', pairs)  10.1 us
    unnamed x16, local copies, waits for them, and re-layouts  3.12 us
    pallas_call x1, Pallas kernels, pack(): pl.pallas_call(functools.partial(pack_kernel, chunks), out_shape=[jax.Sha...  2.11 us
    pallas_call x1, Pallas kernels, prepare_text(): pl.pallas_call(text_kernel, in_specs=[pl.BlockSpec(memory_space=pltpu.SME...  1.39 us
  transfers between devices with their start and end apart: 8, of which 5 were waited for; matrix products, arithmetic and copies ran while one was open for 0% of the time, Pallas kernels for 14%

profile of v7, /device:TPU:0, one launch (start us, length us, event | category | flops | bytes accessed | tf_op | source)
XLA Modules:
  0.0 47.3 jit_solution(15167699319391648362)
XLA Ops:
  0.6 0.0 copy-start.4
  0.7 2.1 %pack.1 = (bf16[1040,128]{1,0:T(8,128)(2,1)}, bf16[1040,128]{1,0:T(8,128)(2,1)}) custom-call(bf16[128,512]{1,0:T(8,128)(2,1)} %refs_8_.3, bf16[128,512]{1,0:T(8,128)(2,1)} %refs_9_.3, bf16[128,512]{1,0:T(8,128)(2,1)} %v_ref.1, bf16[128,512]{1,0:T(8,128)(2,1)} %g_ref.1, s32[1,128]{1,0:T(1,128)} %bitcast.1), custom_call_target="tpu_custom_call" | custom-call | tf_op jit(solution)/shard_map/pack/pallas_call | solution.py:53
  2.8 3.0 %collective-permute-start = (bf16[1040,128]{1,0:T(8,128)(2,1)}, bf16[1040,128]{1,0:T(8,128)(2,1)S(1)}, u32[]{:S(2)}, u32[]{:S(2)}) collective-permute-start(bf16[1040,128]{1,0:T(8,128)(2,1)} %get-tuple-element.27.refs_0_), channel_id=1, source_target_pairs={{0,4},{4,0},{8,12},{12,8},{1,5},{5,1},{9,13},{13,9},{2,6},{6,2},{1... | collective-permute-start | bytes 798728 | tf_op jit(solution)/shard_map/ppermute | solution.py:577
  5.8 2.6 %collective-permute-start.5 = (bf16[1040,128]{1,0:T(8,128)(2,1)}, bf16[1040,128]{1,0:T(8,128)(2,1)S(1)}, u32[]{:S(2)}, u32[]{:S(2)}) collective-permute-start(bf16[1040,128]{1,0:T(8,128)(2,1)} %get-tuple-element.30.refs_0_), channel_id=1, source_target_pairs={{0,8},{8,0},{4,12},{12,4},{1,9},{9,1},{5,13},{13,5},{2,10},{10,2},... | collective-permute-start | bytes 798728 | tf_op jit(solution)/shard_map/ppermute | solution.py:577
  8.4 1.2 %copy-done = bf16[1024,512]{1,0:T(8,128)(2,1)S(1)} copy-done((bf16[1024,512]{1,0:T(8,128)(2,1)S(1)}, bf16[1024,512]{1,0:T(8,128)(2,1)}, u32[]{:S(2)}) %copy-start) | copy-done | bytes 1048600
  9.6 1.2 %copy-done.2 = bf16[1024,512]{1,0:T(8,128)(2,1)S(1)} copy-done((bf16[1024,512]{1,0:T(8,128)(2,1)S(1)}, bf16[1024,512]{1,0:T(8,128)(2,1)}, u32[]{:S(2)}) %copy-start.2) | copy-done | bytes 1048600
  10.8 0.7 %copy-done.6 = s32[4]{0:T(128)S(1)} copy-done((s32[4]{0:T(128)S(1)}, s32[4]{0:T(128)}, u32[]{:S(2)}) %copy-start.6) | copy-done | bytes 40
  11.5 1.4 %prepare_text.1 = (bf16[4096,256]{1,0:T(8,128)(2,1)S(1)}, bf16[1024,512]{1,0:T(8,128)(2,1)S(1)}, f32[4096,128]{1,0:T(8,128)S(1)}) custom-call(s32[4]{0:T(128)S(1)} %copy-done.6, bf16[1024,512]{1,0:T(8,128)(2,1)S(1)} %copy-done, bf16[1024,512]{1,0:T(8,128)(2,1)S(1)} %copy-done.2), custom_call_target="tpu_custom_call" | custom-call | flops 4194304 | bytes 3145728 | tf_op jit(solution)/shard_map/prepare_text/pallas_call | solution.py:304
  12.9 0.4 collective-permute-start.1
  13.3 0.2 collective-permute-start.4
  13.5 5.3 %collective-permute-done.refs_1_ = bf16[1040,128]{1,0:T(8,128)(2,1)S(1)} collective-permute-done((bf16[1040,128]{1,0:T(8,128)(2,1)}, bf16[1040,128]{1,0:T(8,128)(2,1)S(1)}, u32[]{:S(2)}, u32[]{:S(2)}) %collective-permute-start) | collective-permute-done | bytes 266272 | tf_op jit(solution)/shard_map/ppermute | solution.py:577
  18.8 0.7 %collective-permute-start.6 = (bf16[1040,128]{1,0:T(8,128)(2,1)S(1)}, bf16[1040,128]{1,0:T(8,128)(2,1)S(1)}, u32[]{:S(2)}, u32[]{:S(2)}) collective-permute-start(bf16[1040,128]{1,0:T(8,128)(2,1)S(1)} %copy-done.7), channel_id=1, source_target_pairs={{4,8},{8,4},{5,9},{9,5},{6,10},{10,6},{7,11},{11,7},{20,24},{24,20... | collective-permute-start | bytes 798728 | tf_op jit(solution)/shard_map/ppermute | solution.py:577
  19.5 6.0 %collective-permute-done.5.refs_2_ = bf16[1040,128]{1,0:T(8,128)(2,1)S(1)} collective-permute-done((bf16[1040,128]{1,0:T(8,128)(2,1)}, bf16[1040,128]{1,0:T(8,128)(2,1)S(1)}, u32[]{:S(2)}, u32[]{:S(2)}) %collective-permute-start.5) | collective-permute-done | bytes 266272 | tf_op jit(solution)/shard_map/ppermute | solution.py:577
  25.5 1.3 %collective-permute-start.7 = (bf16[1040,128]{1,0:T(8,128)(2,1)S(1)}, bf16[1040,128]{1,0:T(8,128)(2,1)S(1)}, u32[]{:S(2)}, u32[]{:S(2)}) collective-permute-start(bf16[1040,128]{1,0:T(8,128)(2,1)S(1)} %collective-permute-done.5.refs_2_), channel_id=1, source_target_pairs={{4,0},{8,12},{5,1},{9,13},{6,2},{10,14},{7,3},{11,15},{20,16},{24,... | collective-permute-start | bytes 798728 | tf_op jit(solution)/shard_map/ppermute | solution.py:577
  26.8 0.7 %collective-permute-start.2 = (bf16[1040,128]{1,0:T(8,128)(2,1)S(1)}, bf16[1040,128]{1,0:T(8,128)(2,1)S(1)}, u32[]{:S(2)}, u32[]{:S(2)}) collective-permute-start(bf16[1040,128]{1,0:T(8,128)(2,1)S(1)} %copy-done.5), channel_id=1, source_target_pairs={{4,8},{8,4},{5,9},{9,5},{6,10},{10,6},{7,11},{11,7},{20,24},{24,20... | collective-permute-start | bytes 798728 | tf_op jit(solution)/shard_map/ppermute | solution.py:577
  27.5 4.6 %collective-permute-done.1.refs_2_ = bf16[1040,128]{1,0:T(8,128)(2,1)S(1)} collective-permute-done((bf16[1040,128]{1,0:T(8,128)(2,1)S(1)}, bf16[1040,128]{1,0:T(8,128)(2,1)S(1)}, u32[]{:S(2)}, u32[]{:S(2)}) %collective-permute-start.1) | collective-permute-done | bytes 266272 | tf_op jit(solution)/shard_map/ppermute | solution.py:577
  32.1 1.3 %collective-permute-start.3 = (bf16[1040,128]{1,0:T(8,128)(2,1)S(1)}, bf16[1040,128]{1,0:T(8,128)(2,1)S(1)}, u32[]{:S(2)}, u32[]{:S(2)}) collective-permute-start(bf16[1040,128]{1,0:T(8,128)(2,1)S(1)} %collective-permute-done.1.refs_2_), channel_id=1, source_target_pairs={{4,0},{8,12},{5,1},{9,13},{6,2},{10,14},{7,3},{11,15},{20,16},{24,... | collective-permute-start | bytes 798728 | tf_op jit(solution)/shard_map/ppermute | solution.py:577
  33.4 0.0 collective-permute-done.4.refs_1_
  33.4 0.0 collective-permute-done.6.refs_3_
  33.4 1.8 %collective-permute-done.7.refs_4_ = bf16[1040,128]{1,0:T(8,128)(2,1)S(1)} collective-permute-done((bf16[1040,128]{1,0:T(8,128)(2,1)S(1)}, bf16[1040,128]{1,0:T(8,128)(2,1)S(1)}, u32[]{:S(2)}, u32[]{:S(2)}) %collective-permute-start.7) | collective-permute-done | bytes 266272 | tf_op jit(solution)/shard_map/ppermute | solution.py:577
  35.2 5.1 %attend_line.2 = (bf16[128,512]{1,0:T(8,128)(2,1)}, bf16[128,512]{1,0:T(8,128)(2,1)}, bf16[128,512]{1,0:T(8,128)(2,1)}, bf16[128,512]{1,0:T(8,128)(2,1)}, f32[1024,512]{1,0:T(8,128)}, /*index=5*/f32[1024,512]{1,0:T(8,128)}) custom-call(bf16[1040,128]{1,0:T(8,128)(2,1)S(1)} %copy-done.7, bf16[1040,128]{1,0:T(8,128)(2,1)S(1)} %collective-permute-done.4.refs_1_, ...), custom_call_target="tpu_custom_call" | custom-call | flops 2415919104 | bytes 4194304 | tf_op jit(solution)/shard_map/attend_line/pallas_call | solution.py:532
  40.4 0.0 collective-permute-done.2.refs_3_
  40.4 1.7 %collective-permute-done.3.refs_4_ = bf16[1040,128]{1,0:T(8,128)(2,1)S(1)} collective-permute-done((bf16[1040,128]{1,0:T(8,128)(2,1)S(1)}, bf16[1040,128]{1,0:T(8,128)(2,1)S(1)}, u32[]{:S(2)}, u32[]{:S(2)}) %collective-permute-start.3) | collective-permute-done | bytes 266272 | tf_op jit(solution)/shard_map/ppermute | solution.py:577
  42.1 5.2 %attend_line.3 = (bf16[128,512]{1,0:T(8,128)(2,1)}, bf16[128,512]{1,0:T(8,128)(2,1)}, bf16[128,512]{1,0:T(8,128)(2,1)}, bf16[128,512]{1,0:T(8,128)(2,1)}, f32[1024,512]{1,0:T(8,128)}, /*index=5*/f32[1024,512]{1,0:T(8,128)}) custom-call(bf16[1040,128]{1,0:T(8,128)(2,1)S(1)} %copy-done.5, ...), custom_call_target="tpu_custom_call", output_to_operand_aliasing={{0}: (11, {}), {1}: (12, {}), {2}: (13, {}), {3}: (14, {}),... | custom-call | flops 2415919104 | bytes 4194304 | tf_op jit(solution)/shard_map/attend_line/pallas_call | solution.py:532
  (12 shorter events, 0.0 us)
Async XLA Ops:
  0.6 34.6 %copy-start.4 = (bf16[128,512]{1,0:T(8,128)(2,1)S(1)}, bf16[128,512]{1,0:T(8,128)(2,1)}, u32[]{:S(2)}) copy-start(bf16[128,512]{1,0:T(8,128)(2,1)} %refs_9_.3) | copy-start | bytes 393220
  0.6 34.6 %copy-start.3 = (bf16[128,512]{1,0:T(8,128)(2,1)S(1)}, bf16[128,512]{1,0:T(8,128)(2,1)}, u32[]{:S(2)}) copy-start(bf16[128,512]{1,0:T(8,128)(2,1)} %refs_8_.3) | copy-start | bytes 393220
  2.8 16.0 %collective-permute-start = (bf16[1040,128]{1,0:T(8,128)(2,1)}, bf16[1040,128]{1,0:T(8,128)(2,1)S(1)}, u32[]{:S(2)}, u32[]{:S(2)}) collective-permute-start(bf16[1040,128]{1,0:T(8,128)(2,1)} %get-tuple-element.27.refs_0_), channel_id=1, source_target_pairs={{0,4},{4,0},{8,12},{12,8},{1,5},{5,1},{9,13},{13,9},{2,6},{6,2},{1... | collective-permute-start | bytes 798728 | tf_op jit(solution)/shard_map/ppermute | solution.py:577
  5.8 19.7 %collective-permute-start.5 = (bf16[1040,128]{1,0:T(8,128)(2,1)}, bf16[1040,128]{1,0:T(8,128)(2,1)S(1)}, u32[]{:S(2)}, u32[]{:S(2)}) collective-permute-start(bf16[1040,128]{1,0:T(8,128)(2,1)} %get-tuple-element.30.refs_0_), channel_id=1, source_target_pairs={{0,8},{8,0},{4,12},{12,4},{1,9},{9,1},{5,13},{13,5},{2,10},{10,2},... | collective-permute-start | bytes 798728 | tf_op jit(solution)/shard_map/ppermute | solution.py:577
  8.4 1.2 %copy-start = (bf16[1024,512]{1,0:T(8,128)(2,1)S(1)}, bf16[1024,512]{1,0:T(8,128)(2,1)}, u32[]{:S(2)}) copy-start(bf16[1024,512]{1,0:T(8,128)(2,1)} %refs_10_.3) | copy-start | bytes 3145732
  9.6 1.2 %copy-start.2 = (bf16[1024,512]{1,0:T(8,128)(2,1)S(1)}, bf16[1024,512]{1,0:T(8,128)(2,1)}, u32[]{:S(2)}) copy-start(bf16[1024,512]{1,0:T(8,128)(2,1)} %tv_ref.1) | copy-start | bytes 3145732
  10.8 0.7 %copy-start.6 = (s32[4]{0:T(128)S(1)}, s32[4]{0:T(128)}, u32[]{:S(2)}) copy-start(s32[4]{0:T(128)} %len_ref.1) | copy-start | bytes 52
  11.5 1.4 %copy-start.5 = (bf16[1040,128]{1,0:T(8,128)(2,1)S(1)}, bf16[1040,128]{1,0:T(8,128)(2,1)}, u32[]{:S(2)}) copy-start(bf16[1040,128]{1,0:T(8,128)(2,1)} %get-tuple-element.27.refs_0_) | copy-start | bytes 798724
  11.5 1.8 %copy-start.7 = (bf16[1040,128]{1,0:T(8,128)(2,1)S(1)}, bf16[1040,128]{1,0:T(8,128)(2,1)}, u32[]{:S(2)}) copy-start(bf16[1040,128]{1,0:T(8,128)(2,1)} %get-tuple-element.30.refs_0_) | copy-start | bytes 798724
  11.5 23.7 %copy-start.1 = (bf16[1024,512]{1,0:T(8,128)(2,1)S(1)}, bf16[1024,512]{1,0:T(8,128)(2,1)}, u32[]{:S(2)}) copy-start(bf16[1024,512]{1,0:T(8,128)(2,1)} %refs_10_.3) | copy-start | bytes 3145732
  12.9 19.2 %collective-permute-start.1 = (bf16[1040,128]{1,0:T(8,128)(2,1)S(1)}, bf16[1040,128]{1,0:T(8,128)(2,1)S(1)}, u32[]{:S(2)}, u32[]{:S(2)}) collective-permute-start(bf16[1040,128]{1,0:T(8,128)(2,1)S(1)} %copy-done.5), channel_id=1, source_target_pairs={{0,8},{8,0},{4,12},{12,4},{1,9},{9,1},{5,13},{13,5},{2,10},{10,2},... | collective-permute-start | bytes 798728 | tf_op jit(solution)/shard_map/ppermute | solution.py:577
  13.3 20.1 %collective-permute-start.4 = (bf16[1040,128]{1,0:T(8,128)(2,1)S(1)}, bf16[1040,128]{1,0:T(8,128)(2,1)S(1)}, u32[]{:S(2)}, u32[]{:S(2)}) collective-permute-start(bf16[1040,128]{1,0:T(8,128)(2,1)S(1)} %copy-done.7), channel_id=1, source_target_pairs={{0,4},{4,0},{8,12},{12,8},{1,5},{5,1},{9,13},{13,9},{2,6},{6,2},{1... | collective-permute-start | bytes 798728 | tf_op jit(solution)/shard_map/ppermute | solution.py:577
  18.8 14.6 %collective-permute-start.6 = (bf16[1040,128]{1,0:T(8,128)(2,1)S(1)}, bf16[1040,128]{1,0:T(8,128)(2,1)S(1)}, u32[]{:S(2)}, u32[]{:S(2)}) collective-permute-start(bf16[1040,128]{1,0:T(8,128)(2,1)S(1)} %copy-done.7), channel_id=1, source_target_pairs={{4,8},{8,4},{5,9},{9,5},{6,10},{10,6},{7,11},{11,7},{20,24},{24,20... | collective-permute-start | bytes 798728 | tf_op jit(solution)/shard_map/ppermute | solution.py:577
  25.5 9.7 %collective-permute-start.7 = (bf16[1040,128]{1,0:T(8,128)(2,1)S(1)}, bf16[1040,128]{1,0:T(8,128)(2,1)S(1)}, u32[]{:S(2)}, u32[]{:S(2)}) collective-permute-start(bf16[1040,128]{1,0:T(8,128)(2,1)S(1)} %collective-permute-done.5.refs_2_), channel_id=1, source_target_pairs={{4,0},{8,12},{5,1},{9,13},{6,2},{10,14},{7,3},{11,15},{20,16},{24,... | collective-permute-start | bytes 798728 | tf_op jit(solution)/shard_map/ppermute | solution.py:577
  26.8 13.6 %collective-permute-start.2 = (bf16[1040,128]{1,0:T(8,128)(2,1)S(1)}, bf16[1040,128]{1,0:T(8,128)(2,1)S(1)}, u32[]{:S(2)}, u32[]{:S(2)}) collective-permute-start(bf16[1040,128]{1,0:T(8,128)(2,1)S(1)} %copy-done.5), channel_id=1, source_target_pairs={{4,8},{8,4},{5,9},{9,5},{6,10},{10,6},{7,11},{11,7},{20,24},{24,20... | collective-permute-start | bytes 798728 | tf_op jit(solution)/shard_map/ppermute | solution.py:577
  32.1 10.0 %collective-permute-start.3 = (bf16[1040,128]{1,0:T(8,128)(2,1)S(1)}, bf16[1040,128]{1,0:T(8,128)(2,1)S(1)}, u32[]{:S(2)}, u32[]{:S(2)}) collective-permute-start(bf16[1040,128]{1,0:T(8,128)(2,1)S(1)} %collective-permute-done.1.refs_2_), channel_id=1, source_target_pairs={{4,0},{8,12},{5,1},{9,13},{6,2},{10,14},{7,3},{11,15},{20,16},{24,... | collective-permute-start | bytes 798728 | tf_op jit(solution)/shard_map/ppermute | solution.py:577
